TPU v7x, 32 devices: a whole 2x2x4 slice. The times are simulated.
32 devices in a mesh: wide: 16 (over z, y, x), narrow: 2 (over core).
Axes of the slice: x: 2, y: 2, z: 4, core: 2. Of those that a mesh axis runs over, the one named last changes fastest.
Arguments:
- inputs: bfloat16 [1536, 6528], P(('wide', 'narrow')), may hold values from -6 to 6
- cotangent: bfloat16 [1536, 6528], P(('wide', 'narrow')), may hold values from -6 to 6
- master: float32 [296960], P('wide'), may hold values from -1.5 to 1.5, as said below
- first: float32 [296960], P('wide'), may hold values from -0.02734375 to 0.02734375
- second: float32 [296960], P('wide'), may hold values from 1.6837284e-06 to 2.6939655e-05
Outputs:
- block_out: bfloat16 [1536, 6528], P(('wide', 'narrow'))
- input_grad: float32 [1536, 6528], P(('wide', 'narrow'))
- clipped_grad: float32 [296960], P('wide')
- grad_norm: float32 [], replicated
- new_master: float32 [296960], P('wide')
- new_copy: bfloat16 [296960], P('wide')
- new_first: float32 [296960], P('wide')
- new_second: float32 [296960], P('wide')
Inputs may be any that keep to these rules, and one draw needn't show every extreme that they name: master holds weights, gains near one and biases of a few tenths.
All inputs are finite; a program needn't handle non-finite values.
Results may differ from a plain program's by a relative error of at most 0.012.
The roundings to bfloat16 on the way count: a program that leaves them out, or rounds other values in their place, can miss the bound.
Values sent between devices are 32-bit elements; how exact they have to be, the bound alone decides.
A program may use at most 128 MiB of HBM per device.

v0:
```python
import functools
import math

import jax
import jax.numpy as jnp
from jax import lax
from jax.experimental import pallas as pl
from jax.experimental.pallas import tpu as pltpu
from jax.sharding import PartitionSpec as P

D = 192
HEADS = 8
HEAD_DIM = 24
FF = 256
SEQ = 34
STEP = 5
ROWS = 40
GROUP = 3
GROWS = GROUP * ROWS
HJ = HEADS * ROWS
LANES = 128
F32 = jnp.float32
BF16 = jnp.bfloat16
MATS = ((0, D), (288, D), (576, D), (864, D), (1920, FF))
W1_AT = 1152
VEC_AT = 2304
GELU_C = math.sqrt(2.0 / math.pi)


def nn(a, b):
    return lax.dot_general(a, b, (((1,), (0,)), ((), ())), preferred_element_type=F32)


def nt(a, b):
    return lax.dot_general(a, b, (((1,), (1,)), ((), ())), preferred_element_type=F32)


def tn(a, b):
    return lax.dot_general(a, b, (((0,), (0,)), ((), ())), preferred_element_type=F32)


def low_half(v):
    lane = lax.broadcasted_iota(jnp.int32, v.shape, 1)
    return lane < 64


def load_square(flat, base, rows, tmp, out):
    half = rows // 2
    f0 = flat[pl.ds(base, half, stride=3), :]
    f1 = flat[pl.ds(base + 1, half, stride=3), :]
    f2 = flat[pl.ds(base + 2, half, stride=3), :]
    r1 = pltpu.roll(f1, 64, 1)
    r2 = pltpu.roll(f2, 64, 1)
    left = low_half(f0)
    lo, hi = tmp.at[0], tmp.at[1]
    lo[pl.ds(0, half, stride=2), :] = f0
    hi[pl.ds(0, half, stride=2), :] = jnp.where(left, f1, 0.0)
    lo[pl.ds(1, half, stride=2), :] = jnp.where(left, r1, r2)
    hi[pl.ds(1, half, stride=2), :] = jnp.where(left, r2, 0.0)
    out[0:rows, 0:128] = lo[0:rows, :].astype(BF16)
    out[0:rows, 128:256] = hi[0:rows, :].astype(BF16)
    if rows < 256:
        out[rows:256, :] = jnp.zeros((256 - rows, 256), BF16)


def store_square(val, flat, base, rows, tmp):
    half = rows // 2
    lo, hi = tmp.at[0], tmp.at[1]
    lo[0:rows, :] = val[0:rows, 0:128]
    hi[0:rows, :] = val[0:rows, 128:256]
    e0 = lo[pl.ds(0, half, stride=2), :]
    e1 = hi[pl.ds(0, half, stride=2), :]
    o0 = pltpu.roll(lo[pl.ds(1, half, stride=2), :], 64, 1)
    o1 = pltpu.roll(hi[pl.ds(1, half, stride=2), :], 64, 1)
    left = low_half(e0)
    flat[pl.ds(base, half, stride=3), :] = e0
    flat[pl.ds(base + 1, half, stride=3), :] = jnp.where(left, e1, o0)
    flat[pl.ds(base + 2, half, stride=3), :] = jnp.where(left, o0, o1)


def norm_fwd(x):
    mean = jnp.sum(x, -1, keepdims=True) * (1.0 / D)
    right = x[:, 128:256] - mean
    c = jnp.concatenate([x[:, 0:128] - mean, jnp.where(low_half(right), right, 0.0)], 1)
    var = jnp.sum(c * c, -1, keepdims=True) * (1.0 / D)
    r = lax.rsqrt(var + 1e-05)
    return c * r, r


def norm_back(d, xh, r, g):
    e = d * g
    m1 = jnp.sum(e, -1, keepdims=True) * (1.0 / D)
    m2 = jnp.sum(e * xh, -1, keepdims=True) * (1.0 / D)
    return r * (e - m1 - xh * m2)


def rows8(v):
    return jnp.sum(v.reshape(v.shape[0] // 8, 8, v.shape[1]), 0)


def split_pair(v):
    zero = jnp.zeros((v.shape[0], 64), v.dtype)
    even = jnp.concatenate([v[:, 0:D], zero], 1)
    odd = jnp.concatenate([v[:, D : 2 * D], zero], 1)
    return jnp.concatenate([even, odd], 0)


def join_pair(v, n):
    return jnp.concatenate([v[0:n, 0:D], v[n : 2 * n, 0:D]], 1)


def block_kernel(
    x_ref, dy_ref, flat, out_ref, ig_ref, gflat,
    qs, ks, vs, os_, kbd, vbd, psc, xh1, r1, dx2s, h, h2, z, dul, o_t, dal, dyt, dqt, dkt, dvt,
    wq, wk, wv, wo, w1, w2, tmp, hm2, hm, acc, acc2,
):
    n = x_ref.shape[0]
    toks = n * SEQ
    pairs = SEQ // 2
    chunk = 2 * n
    groups = n // GROUP

    for (base, rows), ref in zip(MATS, (wq, wk, wv, wo, w2)):
        load_square(flat, base, rows, tmp, ref)
    for c in range(4):
        w1[0:D, 128 * c : 128 * (c + 1)] = flat[pl.ds(W1_AT + c, D, stride=4), :].astype(BF16)

    w1[D:256, :] = jnp.zeros((256 - D, 2 * FF), BF16)

    def vec(k):
        a = VEC_AT + 3 * (k // 2)
        zero = jnp.zeros((1, 64), F32)
        if k % 2 == 0:
            return jnp.concatenate([flat[a : a + 1, :], flat[a + 1 : a + 2, 0:64], zero], 1)
        return jnp.concatenate([flat[a + 1 : a + 2, 64:128], flat[a + 2 : a + 3, :], zero], 1)

    g1, n1, bq, bv, bo, g2, n2, b2 = [vec(k) for k in range(8)]
    b1 = jnp.concatenate([flat[VEC_AT + 12 + c : VEC_AT + 13 + c, :] for c in range(4)], 1)

    lane = lax.broadcasted_iota(jnp.int32, (80, 256), 1)
    row = lax.broadcasted_iota(jnp.int32, (80, 256), 0)
    for p in range(4):
        lo = jnp.where(row < ROWS, HEAD_DIM * 2 * p, HEAD_DIM * (2 * p + 1))
        hm2[80 * p : 80 * (p + 1), :] = jnp.where(
            (lane >= lo) & (lane < lo + HEAD_DIM), 1.0, 0.0
        ).astype(BF16)
    lane16 = lax.broadcasted_iota(jnp.int32, (16, 256), 1)
    for k in range(HEADS):
        hm[16 * k : 16 * (k + 1), :] = jnp.where(
            (lane16 >= HEAD_DIM * k) & (lane16 < HEAD_DIM * (k + 1)), 1.0, 0.0
        ).astype(BF16)
    ones_lane = (lax.broadcasted_iota(jnp.int32, (toks, 64), 1) == 0).astype(F32).astype(BF16)
    for ref in (h, h2, o_t):
        ref[:, D:256] = ones_lane
    for ref in (qs, ks, vs, os_):
        ref[...] = jnp.zeros(ref.shape, F32)

    def pair_of(ref, i):
        return split_pair(
            ref[:, pl.ds(pl.multiple_of(i * (2 * D), 128), 2 * D)].astype(F32)
        )

    def put_tokens(ref, i, val):
        for half in range(2):
            for par in range(2):
                ref.at[half][pl.ds(2 * i + par, n, stride=ROWS), :] = val[
                    n * par : n * (par + 1), 128 * half : 128 * (half + 1)
                ]

    def get_tokens(ref, i):
        return jnp.concatenate(
            [
                jnp.concatenate(
                    [ref.at[half][pl.ds(2 * i + par, n, stride=ROWS), :] for half in range(2)], 1
                )
                for par in range(2)
            ],
            0,
        )

    def get_rows(ref, start, count):
        return jnp.concatenate([ref[0, pl.ds(start, count), :], ref[1, pl.ds(start, count), :]], 1)

    def put_rows(ref, start, val):
        for half in range(2):
            ref[half, pl.ds(start, val.shape[0]), :] = val[:, 128 * half : 128 * (half + 1)]

    def at(i):
        return pl.ds(pl.multiple_of(i * chunk, 32), chunk)

    def dense1(i, _):
        x = pair_of(x_ref, i)
        xh, r = norm_fwd(x)
        hb = (xh * g1 + n1).astype(BF16)
        xh1[at(i), :] = xh
        r1[at(i), :] = r
        h[at(i), 0:D] = hb[:, 0:D]
        put_tokens(qs, i, (nn(hb, wq[...]) + bq).astype(BF16).astype(F32))
        put_tokens(ks, i, nn(hb, wk[...]).astype(BF16).astype(F32))
        put_tokens(vs, i, (nn(hb, wv[...]) + bv).astype(BF16).astype(F32))
        return 0

    lax.fori_loop(0, pairs, dense1, 0)

    lane3 = lax.broadcasted_iota(jnp.int32, (1, LANES), 1)

    def squeeze(v):
        return jnp.where(
            lane3 < ROWS, v[0:HJ], jnp.where(lane3 < 2 * ROWS, v[HJ : 2 * HJ], v[2 * HJ : 3 * HJ])
        ).reshape(HEADS, ROWS, LANES)

    jrow = lax.broadcasted_iota(jnp.int32, (1, ROWS, LANES), 1)
    cexp = math.log2(math.e) / math.sqrt(HEAD_DIM)
    scale = 1.0 / math.sqrt(HEAD_DIM)

    def attn(g, _):
        r = pl.multiple_of(g * GROWS, 8)
        qg = get_rows(qs, r, LANES).astype(BF16)
        base = pl.multiple_of(g * (3 * HJ), 64)
        for src, dst in ((ks, kbd), (vs, vbd)):
            for b in range(GROUP):
                one = get_rows(src, r + ROWS * b, ROWS)
                two = jnp.concatenate([one, one], 0).astype(BF16)
                for p in range(4):
                    dst[pl.ds(base + HJ * b + 80 * p, 80), :] = two * hm2[80 * p : 80 * (p + 1), :]
        st = squeeze(nt(kbd[pl.ds(base, 3 * HJ), :], qg))
        st = jnp.where(jrow < SEQ, st, -1e30)
        m = jnp.max(st, 1, keepdims=True)
        e = jnp.exp2((st - m) * cexp)
        p = e * (1.0 / jnp.sum(e, 1, keepdims=True))
        p = p.reshape(HJ, LANES)
        psc[pl.ds(pl.multiple_of(g * HJ, 64), HJ), :] = p
        pt = p.T
        for b in range(GROUP):
            ob = nn(
                pt[ROWS * b : ROWS * (b + 1), :].astype(BF16), vbd[pl.ds(base + HJ * b, HJ), :]
            )
            put_rows(os_, r + ROWS * b, ob.astype(BF16).astype(F32)[0:SEQ])
        return 0

    lax.fori_loop(0, groups, attn, 0)

    def dense2(i, carry):
        dg2, dn2, db2 = carry
        o = get_tokens(os_, i).astype(BF16)
        o_t[at(i), 0:D] = o[:, 0:D]
        x2 = pair_of(x_ref, i) + (nn(o, wo[...]) + bo)
        xh, r = norm_fwd(x2)
        hb = (xh * g2 + n2).astype(BF16)
        h2[at(i), 0:D] = hb[:, 0:D]
        u = nn(hb, w1[...]) + b1
        gate, up = u[:, :FF], u[:, FF:]
        sq = gate * gate
        t = jnp.tanh(gate * (GELU_C + (GELU_C * 0.044715) * sq))
        half = 0.5 + 0.5 * t
        act = gate * half
        zb = (act * up).astype(BF16)
        z[at(i), :] = zb
        y = x2 + nn(zb, w2[...]) + b2
        out_ref[:, pl.ds(pl.multiple_of(i * (2 * D), 128), 2 * D)] = join_pair(y, n).astype(BF16)
        dyf = pair_of(dy_ref, i)
        dyb = dyf.astype(BF16)
        dyt[at(i), :] = dyb
        dz = nt(dyb, w2[...])
        slope = half + gate * (0.5 - 0.5 * t * t) * (GELU_C + (3 * GELU_C * 0.044715) * sq)
        du = jnp.concatenate([(dz * up * slope).astype(BF16), (dz * act).astype(BF16)], 1)
        dul[at(i), :] = du
        dh = nt(du, w1[...])
        dx2 = dyf + norm_back(dh, xh, r, g2)
        dx2s[at(i), :] = dx2
        da = dx2.astype(BF16)
        dal[at(i), :] = da
        put_tokens(os_, i, nt(da, wo[...]).astype(BF16).astype(F32))
        return dg2 + rows8(dh * xh), dn2 + rows8(dh), db2 + rows8(dyf)

    zero = jnp.zeros((8, 256), F32)
    dg2, dn2, db2 = lax.fori_loop(0, pairs, dense2, (zero, zero, zero))

    def total(v):
        return jnp.sum(v, 0, keepdims=True)

    def over_tokens(acc, a, b):
        acc[...] = jnp.zeros(acc.shape, F32)

        @pl.loop(0, SEQ // 2)
        def _(i):
            acc[...] += tn(a[at(i), :], b[at(i), :])

        return acc[...]

    store_square(over_tokens(acc, z, dyt), gflat, 1920, FF, tmp)
    dw1 = over_tokens(acc2, h2, dul)
    for c in range(4):
        gflat[pl.ds(W1_AT + c, D, stride=4), :] = dw1[0:D, 128 * c : 128 * (c + 1)]
        gflat[VEC_AT + 12 + c : VEC_AT + 13 + c, :] = dw1[D : D + 1, 128 * c : 128 * (c + 1)]
    dwo = over_tokens(acc, o_t, dal)
    store_square(dwo, gflat, 864, D, tmp)
    dbo = dwo[D : D + 1]

    def attn_back(g, _):
        r = pl.multiple_of(g * GROWS, 8)
        base = pl.multiple_of(g * (3 * HJ), 64)
        qg = get_rows(qs, r, LANES).astype(BF16)
        dg = get_rows(os_, r, LANES).astype(BF16)
        dp = squeeze(nt(vbd[pl.ds(base, 3 * HJ), :], dg))
        p = psc[pl.ds(pl.multiple_of(g * HJ, 64), HJ), :].reshape(HEADS, ROWS, LANES)
        pd = p * dp
        ds = p * dp - p * jnp.sum(pd, 1, keepdims=True)
        dst = ds.reshape(HJ, LANES).T

        def wide(v):
            blocks = []
            for k in range(HEADS):
                one = v[k]
                parts = [
                    jnp.where((lane3 >= ROWS * b) & (lane3 < ROWS * (b + 1)), one, 0.0)
                    for b in range(GROUP)
                ]
                parts.append(jnp.zeros((8, LANES), F32))
                blocks.append(jnp.concatenate(parts, 0).astype(BF16))
            return jnp.concatenate(blocks, 1)

        def masked(v):
            v3 = v.reshape(8, 16, 256)
            return jnp.concatenate(
                [(v3 * hm[16 * k : 16 * (k + 1), :][None]).reshape(128, 256) for k in range(HEADS)], 0
            )

        dv = nn(wide(p), masked(dg))
        dk = nn(wide(ds), masked(qg)) * scale
        for b in range(GROUP):
            dq = nn(
                dst[ROWS * b : ROWS * (b + 1), :].astype(BF16), kbd[pl.ds(base + HJ * b, HJ), :]
            )
            put_rows(qs, r + ROWS * b, (dq * scale).astype(BF16).astype(F32))
        put_rows(vs, r, dv.astype(BF16).astype(F32)[0:GROWS])
        put_rows(ks, r, dk.astype(BF16).astype(F32)[0:GROWS])
        return 0

    lax.fori_loop(0, groups, attn_back, 0)

    def dense3(i, carry):
        dg1, dn1 = carry
        dq = get_tokens(qs, i).astype(BF16)
        dk = get_tokens(ks, i).astype(BF16)
        dv = get_tokens(vs, i).astype(BF16)
        dqt[at(i), :] = dq
        dkt[at(i), :] = dk
        dvt[at(i), :] = dv
        dh = nt(dq, wq[...]) + nt(dk, wk[...]) + nt(dv, wv[...])
        xh = xh1[at(i), :]
        ig = dx2s[at(i), :] + norm_back(dh, xh, r1[at(i), :], g1)
        ig_ref[:, pl.ds(pl.multiple_of(i * (2 * D), 128), 2 * D)] = join_pair(ig, n)
        return dg1 + rows8(dh * xh), dn1 + rows8(dh)

    dg1, dn1 = lax.fori_loop(0, pairs, dense3, (zero, zero))
    dwq = over_tokens(acc, h, dqt)
    store_square(dwq, gflat, 0, D, tmp)
    store_square(over_tokens(acc, h, dkt), gflat, 288, D, tmp)
    dwv = over_tokens(acc, h, dvt)
    store_square(dwv, gflat, 576, D, tmp)

    vecs = [total(dg1), total(dn1), dwq[D : D + 1], dwv[D : D + 1], dbo, total(dg2), total(dn2), total(db2)]
    for k in range(4):
        a, b = vecs[2 * k], vecs[2 * k + 1]
        gflat[VEC_AT + 3 * k : VEC_AT + 3 * k + 1, :] = a[:, 0:128]
        gflat[VEC_AT + 3 * k + 1 : VEC_AT + 3 * k + 2, :] = jnp.concatenate(
            [a[:, 128:192], b[:, 0:64]], 1
        )
        gflat[VEC_AT + 3 * k + 2 : VEC_AT + 3 * k + 3, :] = b[:, 64:192]
    used = VEC_AT + 16
    if gflat.shape[0] > used:
        gflat[used:, :] = jnp.zeros((gflat.shape[0] - used, LANES), F32)


def block(x, dy, flat):
    n = x.shape[0]
    toks = n * SEQ
    sm = (2, n * ROWS + 8, LANES)
    groups = n // GROUP
    vm = pltpu.VMEM
    tok = vm((toks, 256), BF16)
    scratch = (
        [vm(sm, F32)] * 4
        + [vm((groups * 3 * HJ, 256), BF16)] * 2
        + [vm((groups * HJ, LANES), F32)]
        + [vm((toks, 256), F32), vm((toks, 1), F32), vm((toks, 256), F32)]
        + [tok, tok, tok, vm((toks, 2 * FF), BF16), tok]
        + [tok] * 5
        + [vm((256, 256), BF16)] * 4
        + [vm((256, 2 * FF), BF16), vm((FF, 256), BF16), vm((2, FF, 128), F32)]
        + [vm((320, 256), BF16), vm((128, 256), BF16), vm((256, 256), F32), vm((256, 512), F32)]
    )
    return pl.pallas_call(
        block_kernel,
        out_shape=(
            jax.ShapeDtypeStruct(x.shape, BF16),
            jax.ShapeDtypeStruct(x.shape, F32),
            jax.ShapeDtypeStruct(flat.shape, F32),
        ),
        in_specs=[pl.BlockSpec(memory_space=pltpu.VMEM)] * 3,
        out_specs=(pl.BlockSpec(memory_space=pltpu.VMEM),) * 3,
        scratch_shapes=scratch,
        compiler_params=pltpu.CompilerParams(vmem_limit_bytes=60 * 2**20),
        name="block",
    )(x, dy, flat)


def on_device(inputs, cotangent, master, first, second):
    shard = master.shape[0]
    wide = lax.axis_size("wide")
    full = lax.all_gather(master, "wide", axis=0, tiled=True)
    block_out, input_grad, gflat = block(inputs, cotangent, full.reshape(-1, LANES))
    grad = gflat.reshape(-1)
    owned = lax.psum_scatter(grad, "wide", scatter_dimension=0, tiled=True)
    owned = lax.psum(owned, "narrow")
    squares = lax.psum(jnp.sum(owned * owned), "wide")
    grad_norm = jnp.sqrt(squares)
    factor = jnp.minimum(1.0, 1.0 / (grad_norm + 1e-06))
    clipped = owned * factor
    new_first = 0.5 * first + 0.5 * clipped
    new_second = 0.5 * second + 0.5 * clipped * clipped
    fixed = 1.0 - 0.5**STEP
    new_master = master - 0.05 * (
        new_first / fixed / (jnp.sqrt(new_second / fixed) + 1e-08) + 0.1 * master
    )
    return (
        block_out,
        input_grad,
        clipped,
        grad_norm,
        new_master,
        new_master.astype(jnp.bfloat16),
        new_first,
        new_second,
    )


def solution(mesh):
    both, part = P(("wide", "narrow"), None), P("wide")
    return jax.shard_map(
        on_device,
        mesh=mesh,
        in_specs=(both, both, part, part, part),
        out_specs=(both, both, part, P(), part, part, part, part),
        check_vma=False,
    )
```

profile of v0, /device:TPU:0, one launch (start us, length us, event | category | flops | bytes accessed | tf_op | source)
XLA Modules:
  0.0 338.2 jit_solution(1135292165496207154)
XLA Ops:
  7.2 0.0 all-gather.3.cloned.1.call-start
  7.2 1.6 reshape.24
  8.8 0.0 all-gather.3.cloned.1.call-update
  8.8 0.0 all-reduce.6.cloned.1.call-start
  8.9 61.4 %all-gather.3.cloned.1.call-done = f32[16,1,18560]{2,1,0:T(1,128)} async-done(((f32[1,1,18560]{2,1,0:T(1,128)}), f32[16,1,18560]{2,1,0:T(1,128)}) %all-gather.3.cloned.1.call-update) | async-done | bytes 1187856 | tf_op jit(solution)/shard_map/all_gather | solution.py:412
  70.2 81.2 %block.1 = (bf16[48,6528]{1,0:T(8,128)(2,1)}, f32[48,6528]{1,0:T(8,128)}, f32[2320,128]{1,0:T(8,128)}) custom-call(bf16[48,6528]{1,0:T(8,128)(2,1)} %x_ref.1, bf16[48,6528]{1,0:T(8,128)(2,1)} %dy_ref.1, f32[2320,128]{1,0:T(8,128)} %bitcast.4), custom_call_target="tpu_custom_call" | custom-call | tf_op jit(solution)/shard_map/block/pallas_call | solution.py:394
  151.4 0.0 copy-start.3
  151.4 0.0 copy-start
  151.4 0.0 copy-start.1
  151.4 0.0 copy-start.2
  151.4 0.0 all-reduce.6.cloned.1.call-update
  151.5 0.0 all-reduce.4.cloned.1.call-start
  151.5 0.6 copy-done.3
  152.1 0.6 dynamic-slice
  153.3 110.9 %all-reduce.6.cloned.1.call-done = f32[296960]{0:T(1024)} async-done(((f32[296960]{0:T(1024)}), f32[296960]{0:T(1024)}) %all-reduce.6.cloned.1.call-update) | async-done | bytes 1187856
  264.2 1.6 dynamic-slice.1
  265.8 0.0 all-reduce.4.cloned.1.call-update
  265.8 18.2 %all-reduce.4.cloned.1.call-done = f32[18560]{0:T(1024)} async-done(((f32[18560]{0:T(1024)}), f32[18560]{0:T(1024)}) %all-reduce.4.cloned.1.call-update) | async-done | bytes 74256 | tf_op jit(solution)/shard_map/psum | solution.py:416
  284.0 1.5 multiply_reduce_fusion
  285.5 42.6 %psum.15 = f32[]{:T(128)} all-reduce(f32[]{:T(128)} %multiply_reduce_fusion), channel_id=1, replica_groups=mesh['wide'=16,'narrow'=2] {'wide'}, use_global_device_ids=true, to_apply=%region_3.0 | all-reduce | flops 1 | bytes 8 | tf_op jit(solution)/shard_map/psum | solution.py:417
  328.9 0.0 copy-done
  328.9 0.0 copy-done.1
  328.9 0.0 copy-done.2
  328.9 1.6 fusion.1
Async XLA Ops:
  7.2 63.1 %all-gather.3.cloned.1.call-start = ((), (), s32[]{:S(2)}) async-start(), calls=%async_computation.1 | async-start | bytes 1262080 | tf_op jit(solution)/shard_map/all_gather | solution.py:412
  8.8 255.4 %all-reduce.6.cloned.1.call-start = ((), (), s32[]{:S(2)}) async-start(), calls=%async_computation.2 | async-start | bytes 2375680
  151.4 0.7 copy-start.3
  151.4 177.4 %copy-start = (f32[18560]{0:T(1024)S(1)}, f32[18560]{0:T(1024)}, u32[]{:S(2)}) copy-start(f32[18560]{0:T(1024)} %param.7) | copy-start | bytes 222724
  151.4 177.4 %copy-start.1 = (f32[18560]{0:T(1024)S(1)}, f32[18560]{0:T(1024)}, u32[]{:S(2)}) copy-start(f32[18560]{0:T(1024)} %param.8) | copy-start | bytes 222724
  151.4 177.5 %copy-start.2 = (f32[18560]{0:T(1024)S(1)}, f32[18560]{0:T(1024)}, u32[]{:S(2)}) copy-start(f32[18560]{0:T(1024)} %param.9) | copy-start | bytes 222724
  151.5 132.5 %all-reduce.4.cloned.1.call-start = ((), (), s32[]{:S(2)}) async-start(), calls=%async_computation | async-start | bytes 155648 | tf_op jit(solution)/shard_map/psum | solution.py:416
Sparse Core Ops, SparseCore 0:
  11.4 58.8 all-gather.2
  151.6 112.5 all-reduce.5
  267.1 16.8 all-reduce.3
where the time goes:
time: 339 us; the launch traced here: 338 us
  waiting for transfers between devices  190 us (56%)
  Pallas kernels  81.2 us (24%)
  blocking collectives  42.6 us (13%)
  between operations  16.3 us (5%)
  local copies, waits for them, and re-layouts  4.34 us (1%)
    unnamed x4, waiting for transfers between devices  111 us
    pallas_call x1, Pallas kernels, block(): pl.pallas_call(block_kernel, out_shape=(jax.ShapeDtypeStruct(x.shape, BF1...  81.2 us
    all_gather x1, waiting for transfers between devices, on_device(): full = lax.all_gather(master, 'wide', axis=0, tiled=True)  61.4 us
    psum x1, blocking collectives, on_device(): squares = lax.psum(jnp.sum(owned * owned), 'wide')  42.6 us
    psum x1, waiting for transfers between devices, on_device(): owned = lax.psum(owned, 'narrow')  18.2 us
  transfers between devices with their start and end apart: 3, of which 3 were waited for; matrix products, arithmetic and copies ran while one was open for 0% of the time, Pallas kernels for 0%

commit v1 on v0

--- a/solution.py
+++ b/solution.py
@@ -110,7 +110,7 @@
 
 
 def block_kernel(
-    x_ref, dy_ref, flat, out_ref, ig_ref, gflat,
+    x_ref, dy_ref, gathered, out_ref, ig_ref, gshards, flat, gflat,
     qs, ks, vs, os_, kbd, vbd, psc, xh1, r1, dx2s, h, h2, z, dul, o_t, dal, dyt, dqt, dkt, dvt,
     wq, wk, wv, wo, w1, w2, tmp, hm2, hm, acc, acc2,
 ):
@@ -120,6 +120,9 @@
     chunk = 2 * n
     groups = n // GROUP
 
+    wide, rows_sh = gathered.shape[0], flat.shape[0] // gathered.shape[0]
+    for w in range(wide):
+        flat[rows_sh * w : rows_sh * (w + 1), :] = gathered[w, 0:rows_sh, :]
     for (base, rows), ref in zip(MATS, (wq, wk, wv, wo, w2)):
         load_square(flat, base, rows, tmp, ref)
     for c in range(4):
@@ -371,17 +374,22 @@
     used = VEC_AT + 16
     if gflat.shape[0] > used:
         gflat[used:, :] = jnp.zeros((gflat.shape[0] - used, LANES), F32)
-
-
-def block(x, dy, flat):
+    for w in range(wide):
+        gshards[w, 0:rows_sh, :] = gflat[rows_sh * w : rows_sh * (w + 1), :]
+        gshards[w, rows_sh:, :] = jnp.zeros((gshards.shape[1] - rows_sh, LANES), F32)
+
+
+def block(x, dy, gathered, rows_sh):
     n = x.shape[0]
     toks = n * SEQ
     sm = (2, n * ROWS + 8, LANES)
     groups = n // GROUP
     vm = pltpu.VMEM
     tok = vm((toks, 256), BF16)
+    flat = vm((gathered.shape[0] * rows_sh, LANES), F32)
     scratch = (
-        [vm(sm, F32)] * 4
+        [flat, flat]
+        + [vm(sm, F32)] * 4
         + [vm((groups * 3 * HJ, 256), BF16)] * 2
         + [vm((groups * HJ, LANES), F32)]
         + [vm((toks, 256), F32), vm((toks, 1), F32), vm((toks, 256), F32)]
@@ -396,25 +404,233 @@
         out_shape=(
             jax.ShapeDtypeStruct(x.shape, BF16),
             jax.ShapeDtypeStruct(x.shape, F32),
-            jax.ShapeDtypeStruct(flat.shape, F32),
+            jax.ShapeDtypeStruct(gathered.shape, F32),
         ),
         in_specs=[pl.BlockSpec(memory_space=pltpu.VMEM)] * 3,
         out_specs=(pl.BlockSpec(memory_space=pltpu.VMEM),) * 3,
         scratch_shapes=scratch,
         compiler_params=pltpu.CompilerParams(vmem_limit_bytes=60 * 2**20),
         name="block",
-    )(x, dy, flat)
+    )(x, dy, gathered)
+
+
+def factors(wide):
+    inner = max(k for k in range(1, int(math.isqrt(wide)) + 1) if wide % k == 0)
+    return wide // inner, inner
+
+
+def remote(src, dst, send, recv, where):
+    return pltpu.make_async_remote_copy(
+        src_ref=src,
+        dst_ref=dst,
+        send_sem=send,
+        recv_sem=recv,
+        device_id=where,
+        device_id_type=pl.DeviceIdType.MESH,
+    )
+
+
+def greet(devices):
+    barrier = pltpu.get_barrier_semaphore()
+    for dev in devices:
+        pl.semaphore_signal(barrier, inc=1, device_id=dev, device_id_type=pl.DeviceIdType.MESH)
+    pl.semaphore_wait(barrier, len(devices))
+
+
+def gather_kernel(wide, shard, buf, send, send_sib, recv, recv_sib):
+    outer, inner = factors(wide)
+    me, core = lax.axis_index("wide"), lax.axis_index("narrow")
+    zo, pi = me // inner, lax.rem(me, inner)
+    rows, half = shard.shape[0], buf.shape[1] // 2
+    mine = pl.ds(pl.multiple_of(core * half, 8), half)
+    plane = [(zo * inner + lax.rem(pi + k, inner), core) for k in range(1, inner)]
+    column = [(lax.rem(zo + k, outer) * inner + pi, core) for k in range(1, outer)]
+    sibling = (me, 1 - core)
+    greet(plane + column + [sibling])
+
+    buf[me, 0:rows, :] = shard[...]
+    buf[me, rows:, :] = jnp.zeros((buf.shape[1] - rows, LANES), F32)
+    started = []
+
+    def push(s, where, sems, k, recvs):
+        copy = remote(buf.at[s, mine], buf.at[s, mine], sems.at[k], recvs.at[s], where)
+        copy.start()
+        started.append(copy)
+
+    def arrived(s, recvs, part):
+        remote(buf.at[s, part], buf.at[s, part], send.at[0], recvs.at[s], sibling).wait_recv()
+
+    count = 0
+    for where in column + plane:
+        push(me, where, send, count, recv)
+        count += 1
+    sib = 0
+    for k in range(outer - 1, 0, -1):
+        s = lax.rem(zo + k, outer) * inner + pi
+        arrived(s, recv, mine)
+        for where in plane:
+            push(s, where, send, count, recv)
+            count += 1
+        push(s, sibling, send_sib, sib, recv_sib)
+        sib += 1
+    for j in range(outer):
+        for k in range(1, inner):
+            s = lax.rem(zo + j, outer) * inner + lax.rem(pi + k, inner)
+            arrived(s, recv, mine)
+            push(s, sibling, send_sib, sib, recv_sib)
+            sib += 1
+    theirs = pl.ds(pl.multiple_of((1 - core) * half, 8), half)
+    for k in range(1, wide):
+        arrived(lax.rem(me + k, wide), recv_sib, theirs)
+    for copy in started:
+        copy.wait_send()
+
+
+def gather(master, wide, padded):
+    outer, inner = factors(wide)
+    sends = outer - 1 + inner - 1 + (outer - 1) * (inner - 1)
+    return pl.pallas_call(
+        functools.partial(gather_kernel, wide),
+        out_shape=jax.ShapeDtypeStruct((wide, padded, LANES), F32),
+        in_specs=[pl.BlockSpec(memory_space=pltpu.VMEM)],
+        out_specs=pl.BlockSpec(memory_space=pltpu.VMEM),
+        scratch_shapes=[
+            pltpu.SemaphoreType.DMA((sends,)),
+            pltpu.SemaphoreType.DMA((wide - 1,)),
+            pltpu.SemaphoreType.DMA((wide,)),
+            pltpu.SemaphoreType.DMA((wide,)),
+        ],
+        compiler_params=pltpu.CompilerParams(
+            collective_id=0, has_side_effects=True, vmem_limit_bytes=16 * 2**20
+        ),
+        name="gather",
+    )(master)
+
+
+def scatter_kernel(
+    wide, parts, own, squares, sib_in, plane_in, col_in, res, sq, out_p, out_c,
+    sib_send, sib_recv, plane_send, plane_recv, col_send, col_recv, fin, sq_send, sq_recv,
+):
+    outer, inner = factors(wide)
+    me, core = lax.axis_index("wide"), lax.axis_index("narrow")
+    zo, pi = me // inner, lax.rem(me, inner)
+    rows, half = own.shape[0], res.shape[0] // 2
+    mine = pl.ds(pl.multiple_of(core * half, 8), half)
+    theirs = pl.ds(pl.multiple_of((1 - core) * half, 8), half)
+    sibling = (me, 1 - core)
+    others = [(lax.rem(me + k, wide), core) for k in range(1, wide)]
+    greet(others + [sibling])
+    started = []
+
+    def go(copy):
+        copy.start()
+        started.append(copy)
+
+    order = [lax.rem(pi + k, inner) for k in range(1, inner)] + [pi]
+    for k, q in enumerate(order):
+        go(remote(parts.at[:, q, theirs], sib_in.at[q], sib_send.at[k], sib_recv.at[q], sibling))
+    for k, q in enumerate(order):
+        remote(sib_in.at[q], sib_in.at[q], sib_send.at[k], sib_recv.at[q], sibling).wait_recv()
+        both = parts[:, q, mine, :] + sib_in[q]
+        if k < inner - 1:
+            out_p[k] = both
+            go(
+                remote(
+                    out_p.at[k], plane_in.at[pi], plane_send.at[k], plane_recv.at[pi],
+                    (zo * inner + q, core),
+                )
+            )
+        else:
+            plane_in[pi] = both
+    for q in order[:-1]:
+        remote(
+            plane_in.at[q], plane_in.at[q], plane_send.at[0], plane_recv.at[q], sibling
+        ).wait_recv()
+    levels = [lax.rem(zo + k, outer) for k in range(1, outer)] + [zo]
+    for k, t in enumerate(levels):
+        line = plane_in[0, t]
+        for q in range(1, inner):
+            line = line + plane_in[q, t]
+        if k < outer - 1:
+            out_c[k] = line
+            go(
+                remote(
+                    out_c.at[k], col_in.at[zo], col_send.at[k], col_recv.at[zo],
+                    (t * inner + pi, core),
+                )
+            )
+        else:
+            col_in[zo] = line
+    for t in levels[:-1]:
+        remote(col_in.at[t], col_in.at[t], col_send.at[0], col_recv.at[t], sibling).wait_recv()
+    line = col_in[0]
+    for t in range(1, outer):
+        line = line + col_in[t]
+    res[mine, :] = line
+    last = remote(res.at[mine], res.at[mine], fin.at[0], fin.at[1], sibling)
+    last.start()
+    started.append(last)
+    remote(res.at[theirs], res.at[theirs], fin.at[0], fin.at[1], sibling).wait_recv()
+    full = res[...]
+    own[...] = full[0:rows]
+    sq[me] = rows8(full * full)
+    for k, where in enumerate(others):
+        go(remote(sq.at[me], sq.at[me], sq_send.at[k], sq_recv.at[me], where))
+    for k in range(1, wide):
+        s = lax.rem(me + k, wide)
+        remote(sq.at[s], sq.at[s], sq_send.at[0], sq_recv.at[s], sibling).wait_recv()
+    squares[...] = jnp.broadcast_to(jnp.sum(jnp.sum(sq[...], 0), keepdims=True), squares.shape)
+    for copy in started:
+        copy.wait_send()
+
+
+def scatter(parts, rows, wide):
+    outer, inner = factors(wide)
+    padded = parts.shape[1]
+    half = padded // 2
+    vm, dma = pltpu.VMEM, pltpu.SemaphoreType.DMA
+    return pl.pallas_call(
+        functools.partial(scatter_kernel, wide),
+        out_shape=(
+            jax.ShapeDtypeStruct((rows, LANES), F32),
+            jax.ShapeDtypeStruct((8, LANES), F32),
+        ),
+        in_specs=[pl.BlockSpec(memory_space=pltpu.VMEM)],
+        out_specs=(pl.BlockSpec(memory_space=pltpu.VMEM),) * 2,
+        scratch_shapes=[
+            vm((inner, outer, half, LANES), F32),
+            vm((inner, outer, half, LANES), F32),
+            vm((outer, half, LANES), F32),
+            vm((padded, LANES), F32),
+            vm((wide, 8, LANES), F32),
+            vm((inner - 1, outer, half, LANES), F32),
+            vm((outer - 1, half, LANES), F32),
+            dma((inner,)),
+            dma((inner,)),
+            dma((inner - 1,)),
+            dma((inner,)),
+            dma((outer - 1,)),
+            dma((outer,)),
+            dma((2,)),
+            dma((wide - 1,)),
+            dma((wide,)),
+        ],
+        compiler_params=pltpu.CompilerParams(
+            collective_id=1, has_side_effects=True, vmem_limit_bytes=32 * 2**20
+        ),
+        name="scatter",
+    )(parts.reshape(outer, inner, padded, LANES))
 
 
 def on_device(inputs, cotangent, master, first, second):
-    shard = master.shape[0]
     wide = lax.axis_size("wide")
-    full = lax.all_gather(master, "wide", axis=0, tiled=True)
-    block_out, input_grad, gflat = block(inputs, cotangent, full.reshape(-1, LANES))
-    grad = gflat.reshape(-1)
-    owned = lax.psum_scatter(grad, "wide", scatter_dimension=0, tiled=True)
-    owned = lax.psum(owned, "narrow")
-    squares = lax.psum(jnp.sum(owned * owned), "wide")
+    rows = master.shape[0] // LANES
+    padded = (rows + 15) // 16 * 16
+    gathered = gather(master.reshape(rows, LANES), wide, padded)
+    block_out, input_grad, parts = block(inputs, cotangent, gathered, rows)
+    owned, squares = scatter(parts, rows, wide)
+    owned = owned.reshape(-1)
+    squares = squares[0, 0]
     grad_norm = jnp.sqrt(squares)
     factor = jnp.minimum(1.0, 1.0 / (grad_norm + 1e-06))
     clipped = owned * factor

time: 339 us -> 130 us (0.38)
  waiting for transfers between devices: 190 us -> 0 us
  blocking collectives: 42.6 us -> 0 us
  Pallas kernels: 81.2 us -> 122 us
  between operations: 16.3 us -> 2.56 us
    unnamed x4 -> x0, waiting for transfers between devices: 111 us -> none
    all_gather x1 -> x0, waiting for transfers between devices: 61.4 us -> none  [on_device(): full = lax.all_gather(master, 'wide', axis=0, tiled=True)]
    psum x1 -> x0, blocking collectives: 42.6 us -> none  [on_device(): squares = lax.psum(jnp.sum(owned * owned), 'wide')]
    pallas_call x0 -> x2, Pallas kernels: none -> 41 us  [the longest x1 24.3 us: scatter(): pl.pallas_call(functools.partial(scatter_kernel, wide), out_shape=(jax.Sh...]
    psum x1 -> x0, waiting for transfers between devices: 18.2 us -> none  [on_device(): owned = lax.psum(owned, 'narrow')]
  transfers between devices with their start and end apart: 3 -> 0, of which waited for: 3 -> 0; matrix products, arithmetic and copies ran while one was open for 0% -> 0% of each run, Pallas kernels for 0% -> 0%
where the time goes in v1:
time: 130 us; the launch traced here: 129 us
  Pallas kernels  122 us (94%)
  local copies, waits for them, and re-layouts  3.78 us (3%)
  between operations  2.56 us (2%)
    pallas_call x1, Pallas kernels, block(): pl.pallas_call(block_kernel, out_shape=(jax.ShapeDtypeStruct(x.shape, BF1...  81.3 us
    pallas_call x1, Pallas kernels, scatter(): pl.pallas_call(functools.partial(scatter_kernel, wide), out_shape=(jax.Sh...  24.3 us
    pallas_call x1, Pallas kernels, gather(): pl.pallas_call(functools.partial(gather_kernel, wide), out_shape=jax.Shap...  16.8 us
    unnamed x12, local copies, waits for them, and re-layouts  3.27 us

profile of v1, /device:TPU:0, one launch (start us, length us, event | category | flops | bytes accessed | tf_op | source)
XLA Modules:
  0.0 129.4 jit_solution(7390807133794249692)
XLA Ops:
  0.6 0.0 copy-start.2
  0.6 0.9 copy-done.2
  1.5 16.8 %gather.1.gathered = f32[16,160,128]{2,1,0:T(8,128)S(1)} custom-call(f32[145,128]{1,0:T(8,128)S(1)} %bitcast.7), custom_call_target="tpu_custom_call" | custom-call | tf_op jit(solution)/shard_map/gather/pallas_call | solution.py:492
  18.3 0.0 copy-start
  18.3 1.1 copy-done
  19.4 0.0 copy-start.3
  19.4 0.0 copy-start.4
  19.4 0.0 copy-start.5
  19.4 81.3 %block.1 = (bf16[48,6528]{1,0:T(8,128)(2,1)}, f32[48,6528]{1,0:T(8,128)}, f32[16,160,128]{2,1,0:T(8,128)}) custom-call(bf16[48,6528]{1,0:T(8,128)(2,1)} %x_ref.1, bf16[48,6528]{1,0:T(8,128)(2,1)} %dy_ref.1, f32[16,160,128]{2,1,0:T(8,128)} %copy-done), custom_call_target="tpu_custom_call" | custom-call | tf_op jit(solution)/shard_map/block/pallas_call | solution.py:402
  100.7 0.0 copy-start.1
  100.7 1.3 %copy-done.1 = f32[16,160,128]{2,1,0:T(8,128)S(1)} copy-done((f32[16,160,128]{2,1,0:T(8,128)S(1)}, f32[16,160,128]{2,1,0:T(8,128)}, u32[]{:S(2)}) %copy-start.1) | copy-done | bytes 1310744
  102.0 24.3 %scatter.1 = (f32[145,128]{1,0:T(8,128)S(1)}, f32[8,128]{1,0:T(8,128)S(1)}) custom-call(f32[4,4,160,128]{3,2,1,0:T(8,128)S(1)} %bitcast.6), custom_call_target="tpu_custom_call" | custom-call | tf_op jit(solution)/shard_map/scatter/pallas_call | solution.py:592
  126.3 0.5 slice.3
  127.5 0.0 copy-done.3
  127.5 0.0 copy-done.4
  127.5 0.0 copy-done.5
  127.5 0.7 fusion.1
Async XLA Ops:
  0.6 0.9 copy-start.2
  18.3 1.1 copy-start
  19.4 108.2 %copy-start.3 = (f32[18560]{0:T(1024)S(1)}, f32[18560]{0:T(1024)}, u32[]{:S(2)}) copy-start(f32[18560]{0:T(1024)} %param.7) | copy-start | bytes 222724
  19.4 108.2 %copy-start.4 = (f32[18560]{0:T(1024)S(1)}, f32[18560]{0:T(1024)}, u32[]{:S(2)}) copy-start(f32[18560]{0:T(1024)} %param.8) | copy-start | bytes 222724
  19.4 108.2 %copy-start.5 = (f32[18560]{0:T(1024)S(1)}, f32[18560]{0:T(1024)}, u32[]{:S(2)}) copy-start(f32[18560]{0:T(1024)} %param.9) | copy-start | bytes 222724
  100.7 1.3 %copy-start.1 = (f32[16,160,128]{2,1,0:T(8,128)S(1)}, f32[16,160,128]{2,1,0:T(8,128)}, u32[]{:S(2)}) copy-start(f32[16,160,128]{2,1,0:T(8,128)} %get-tuple-element.15) | copy-start | bytes 3932164

commit v2 on v1

--- a/solution.py
+++ b/solution.py
@@ -23,6 +23,8 @@
 BF16 = jnp.bfloat16
 MATS = ((0, D), (288, D), (576, D), (864, D), (1920, FF))
 W1_AT = 1152
+WIDTH1, WIDTH2, WIDTH3, DW_STEPS = 4, 4, 4, 2
+LOCK1, LOCK2 = 4, 4
 VEC_AT = 2304
 GELU_C = math.sqrt(2.0 / math.pi)
 
@@ -98,26 +100,25 @@
     return jnp.sum(v.reshape(v.shape[0] // 8, 8, v.shape[1]), 0)
 
 
-def split_pair(v):
-    zero = jnp.zeros((v.shape[0], 64), v.dtype)
-    even = jnp.concatenate([v[:, 0:D], zero], 1)
-    odd = jnp.concatenate([v[:, D : 2 * D], zero], 1)
-    return jnp.concatenate([even, odd], 0)
-
-
-def join_pair(v, n):
-    return jnp.concatenate([v[0:n, 0:D], v[n : 2 * n, 0:D]], 1)
+def split_tokens(v, count):
+    zero = jnp.zeros((v.shape[0], 256 - D), v.dtype)
+    return jnp.concatenate(
+        [jnp.concatenate([v[:, D * t : D * (t + 1)], zero], 1) for t in range(count)], 0
+    )
+
+
+def join_tokens(v, n):
+    return jnp.concatenate([v[n * t : n * (t + 1), 0:D] for t in range(v.shape[0] // n)], 1)
 
 
 def block_kernel(
     x_ref, dy_ref, gathered, out_ref, ig_ref, gshards, flat, gflat,
-    qs, ks, vs, os_, kbd, vbd, psc, xh1, r1, dx2s, h, h2, z, dul, o_t, dal, dyt, dqt, dkt, dvt,
-    wq, wk, wv, wo, w1, w2, tmp, hm2, hm, acc, acc2,
+    qs, ks, vs, os_, kbd, vbd, psc, xh1, r1, dx2s, h, h2, z, dul, o_t, dal, dyt, dqkv,
+    wq, wk, wv, wo, w1, w2, tmp, hm2, hm, acc, acc2, acc3,
 ):
     n = x_ref.shape[0]
     toks = n * SEQ
     pairs = SEQ // 2
-    chunk = 2 * n
     groups = n // GROUP
 
     wide, rows_sh = gathered.shape[0], flat.shape[0] // gathered.shape[0]
@@ -158,29 +159,36 @@
     for ref in (qs, ks, vs, os_):
         ref[...] = jnp.zeros(ref.shape, F32)
 
-    def pair_of(ref, i):
-        return split_pair(
-            ref[:, pl.ds(pl.multiple_of(i * (2 * D), 128), 2 * D)].astype(F32)
+    def tokens_of(ref, t, count):
+        return split_tokens(
+            ref[:, pl.ds(pl.multiple_of(t * D, 128), count * D)].astype(F32), count
         )
 
-    def put_tokens(ref, i, val):
+    def put_tokens(ref, t, val):
         for half in range(2):
-            for par in range(2):
-                ref.at[half][pl.ds(2 * i + par, n, stride=ROWS), :] = val[
-                    n * par : n * (par + 1), 128 * half : 128 * (half + 1)
+            for k in range(val.shape[0] // n):
+                ref.at[half][pl.ds(t + k, n, stride=ROWS), :] = val[
+                    n * k : n * (k + 1), 128 * half : 128 * (half + 1)
                 ]
 
-    def get_tokens(ref, i):
+    def get_tokens(ref, t, count):
         return jnp.concatenate(
             [
                 jnp.concatenate(
-                    [ref.at[half][pl.ds(2 * i + par, n, stride=ROWS), :] for half in range(2)], 1
+                    [ref.at[half][pl.ds(t + k, n, stride=ROWS), :] for half in range(2)], 1
                 )
-                for par in range(2)
+                for k in range(count)
             ],
             0,
         )
 
+    def over_token_chunks(body, width, carry):
+        whole = pairs // width
+        carry = lax.fori_loop(0, whole, lambda i, c: body(i * (2 * width), 2 * width, c), carry)
+        if pairs % width:
+            carry = body(whole * 2 * width, 2 * (pairs % width), carry)
+        return carry
+
     def get_rows(ref, start, count):
         return jnp.concatenate([ref[0, pl.ds(start, count), :], ref[1, pl.ds(start, count), :]], 1)
 
@@ -188,22 +196,22 @@
         for half in range(2):
             ref[half, pl.ds(start, val.shape[0]), :] = val[:, 128 * half : 128 * (half + 1)]
 
-    def at(i):
-        return pl.ds(pl.multiple_of(i * chunk, 32), chunk)
-
-    def dense1(i, _):
-        x = pair_of(x_ref, i)
-        xh, r = norm_fwd(x)
+    def rows_at(t, count):
+        return pl.ds(pl.multiple_of(t * n, 32), count * n)
+
+    def dense1(t, count, carry):
+        at = rows_at(t, count)
+        xh, r = norm_fwd(tokens_of(x_ref, t, count))
         hb = (xh * g1 + n1).astype(BF16)
-        xh1[at(i), :] = xh
-        r1[at(i), :] = r
-        h[at(i), 0:D] = hb[:, 0:D]
-        put_tokens(qs, i, (nn(hb, wq[...]) + bq).astype(BF16).astype(F32))
-        put_tokens(ks, i, nn(hb, wk[...]).astype(BF16).astype(F32))
-        put_tokens(vs, i, (nn(hb, wv[...]) + bv).astype(BF16).astype(F32))
-        return 0
-
-    lax.fori_loop(0, pairs, dense1, 0)
+        xh1[at, :] = xh
+        r1[at, :] = r
+        h[at, 0:D] = hb[:, 0:D]
+        put_tokens(qs, t, (nn(hb, wq[...]) + bq).astype(BF16).astype(F32))
+        put_tokens(ks, t, nn(hb, wk[...]).astype(BF16).astype(F32))
+        put_tokens(vs, t, (nn(hb, wv[...]) + bv).astype(BF16).astype(F32))
+        return carry
+
+    over_token_chunks(dense1, WIDTH1, 0)
 
     lane3 = lax.broadcasted_iota(jnp.int32, (1, LANES), 1)
 
@@ -216,41 +224,50 @@
     cexp = math.log2(math.e) / math.sqrt(HEAD_DIM)
     scale = 1.0 / math.sqrt(HEAD_DIM)
 
-    def attn(g, _):
-        r = pl.multiple_of(g * GROWS, 8)
-        qg = get_rows(qs, r, LANES).astype(BF16)
-        base = pl.multiple_of(g * (3 * HJ), 64)
-        for src, dst in ((ks, kbd), (vs, vbd)):
-            for b in range(GROUP):
-                one = get_rows(src, r + ROWS * b, ROWS)
-                two = jnp.concatenate([one, one], 0).astype(BF16)
-                for p in range(4):
-                    dst[pl.ds(base + HJ * b + 80 * p, 80), :] = two * hm2[80 * p : 80 * (p + 1), :]
-        st = squeeze(nt(kbd[pl.ds(base, 3 * HJ), :], qg))
-        st = jnp.where(jrow < SEQ, st, -1e30)
-        m = jnp.max(st, 1, keepdims=True)
-        e = jnp.exp2((st - m) * cexp)
-        p = e * (1.0 / jnp.sum(e, 1, keepdims=True))
-        p = p.reshape(HJ, LANES)
-        psc[pl.ds(pl.multiple_of(g * HJ, 64), HJ), :] = p
-        pt = p.T
+    def attn(i, carry):
+        r0 = pl.multiple_of(i * (LOCK1 * GROWS), 8)
+        base0 = pl.multiple_of(i * (LOCK1 * 3 * HJ), 64)
+        p0 = pl.multiple_of(i * (LOCK1 * HJ), 64)
+        sets = range(LOCK1)
+        qg = [get_rows(qs, r0 + GROWS * k, LANES).astype(BF16) for k in sets]
+        for k in sets:
+            for src, dst in ((ks, kbd), (vs, vbd)):
+                for b in range(GROUP):
+                    one = get_rows(src, r0 + GROWS * k + ROWS * b, ROWS)
+                    two = jnp.concatenate([one, one], 0).astype(BF16)
+                    for p in range(4):
+                        dst[pl.ds(base0 + HJ * (3 * k + b) + 80 * p, 80), :] = (
+                            two * hm2[80 * p : 80 * (p + 1), :]
+                        )
+        st = [squeeze(nt(kbd[pl.ds(base0 + 3 * HJ * k, 3 * HJ), :], qg[k])) for k in sets]
+        st = [jnp.where(jrow < SEQ, v, -1e30) for v in st]
+        m = [jnp.max(v, 1, keepdims=True) for v in st]
+        e = [jnp.exp2((st[k] - m[k]) * cexp) for k in sets]
+        l = [1.0 / jnp.sum(v, 1, keepdims=True) for v in e]
+        p = [(e[k] * l[k]).reshape(HJ, LANES) for k in sets]
+        for k in sets:
+            psc[pl.ds(p0 + HJ * k, HJ), :] = p[k]
+        pt = [v.T for v in p]
         for b in range(GROUP):
-            ob = nn(
-                pt[ROWS * b : ROWS * (b + 1), :].astype(BF16), vbd[pl.ds(base + HJ * b, HJ), :]
-            )
-            put_rows(os_, r + ROWS * b, ob.astype(BF16).astype(F32)[0:SEQ])
-        return 0
-
-    lax.fori_loop(0, groups, attn, 0)
-
-    def dense2(i, carry):
+            for k in sets:
+                ob = nn(
+                    pt[k][ROWS * b : ROWS * (b + 1), :].astype(BF16),
+                    vbd[pl.ds(base0 + HJ * (3 * k + b), HJ), :],
+                )
+                put_rows(os_, r0 + GROWS * k + ROWS * b, ob.astype(BF16).astype(F32)[0:SEQ])
+        return carry
+
+    lax.fori_loop(0, groups // LOCK1, attn, 0)
+
+    def dense2(t0, count, carry):
         dg2, dn2, db2 = carry
-        o = get_tokens(os_, i).astype(BF16)
-        o_t[at(i), 0:D] = o[:, 0:D]
-        x2 = pair_of(x_ref, i) + (nn(o, wo[...]) + bo)
+        at = rows_at(t0, count)
+        o = get_tokens(os_, t0, count).astype(BF16)
+        o_t[at, 0:D] = o[:, 0:D]
+        x2 = tokens_of(x_ref, t0, count) + (nn(o, wo[...]) + bo)
         xh, r = norm_fwd(x2)
         hb = (xh * g2 + n2).astype(BF16)
-        h2[at(i), 0:D] = hb[:, 0:D]
+        h2[at, 0:D] = hb[:, 0:D]
         u = nn(hb, w1[...]) + b1
         gate, up = u[:, :FF], u[:, FF:]
         sq = gate * gate
@@ -258,36 +275,39 @@
         half = 0.5 + 0.5 * t
         act = gate * half
         zb = (act * up).astype(BF16)
-        z[at(i), :] = zb
+        z[at, :] = zb
         y = x2 + nn(zb, w2[...]) + b2
-        out_ref[:, pl.ds(pl.multiple_of(i * (2 * D), 128), 2 * D)] = join_pair(y, n).astype(BF16)
-        dyf = pair_of(dy_ref, i)
+        out_ref[:, pl.ds(pl.multiple_of(t0 * D, 128), count * D)] = join_tokens(y, n).astype(BF16)
+        dyf = tokens_of(dy_ref, t0, count)
         dyb = dyf.astype(BF16)
-        dyt[at(i), :] = dyb
+        dyt[at, :] = dyb
         dz = nt(dyb, w2[...])
         slope = half + gate * (0.5 - 0.5 * t * t) * (GELU_C + (3 * GELU_C * 0.044715) * sq)
         du = jnp.concatenate([(dz * up * slope).astype(BF16), (dz * act).astype(BF16)], 1)
-        dul[at(i), :] = du
+        dul[at, :] = du
         dh = nt(du, w1[...])
         dx2 = dyf + norm_back(dh, xh, r, g2)
-        dx2s[at(i), :] = dx2
+        dx2s[at, :] = dx2
         da = dx2.astype(BF16)
-        dal[at(i), :] = da
-        put_tokens(os_, i, nt(da, wo[...]).astype(BF16).astype(F32))
+        dal[at, :] = da
+        put_tokens(os_, t0, nt(da, wo[...]).astype(BF16).astype(F32))
         return dg2 + rows8(dh * xh), dn2 + rows8(dh), db2 + rows8(dyf)
 
     zero = jnp.zeros((8, 256), F32)
-    dg2, dn2, db2 = lax.fori_loop(0, pairs, dense2, (zero, zero, zero))
+    dg2, dn2, db2 = over_token_chunks(dense2, WIDTH2, (zero, zero, zero))
 
     def total(v):
         return jnp.sum(v, 0, keepdims=True)
 
     def over_tokens(acc, a, b):
         acc[...] = jnp.zeros(acc.shape, F32)
-
-        @pl.loop(0, SEQ // 2)
+        steps = DW_STEPS
+        size = toks // steps
+
+        @pl.loop(0, steps)
         def _(i):
-            acc[...] += tn(a[at(i), :], b[at(i), :])
+            at = pl.ds(pl.multiple_of(i * size, 16), size)
+            acc[...] += tn(a[at, :], b[at, :])
 
         return acc[...]
 
@@ -300,70 +320,71 @@
     store_square(dwo, gflat, 864, D, tmp)
     dbo = dwo[D : D + 1]
 
-    def attn_back(g, _):
-        r = pl.multiple_of(g * GROWS, 8)
-        base = pl.multiple_of(g * (3 * HJ), 64)
-        qg = get_rows(qs, r, LANES).astype(BF16)
-        dg = get_rows(os_, r, LANES).astype(BF16)
-        dp = squeeze(nt(vbd[pl.ds(base, 3 * HJ), :], dg))
-        p = psc[pl.ds(pl.multiple_of(g * HJ, 64), HJ), :].reshape(HEADS, ROWS, LANES)
-        pd = p * dp
-        ds = p * dp - p * jnp.sum(pd, 1, keepdims=True)
-        dst = ds.reshape(HJ, LANES).T
-
-        def wide(v):
-            blocks = []
-            for k in range(HEADS):
-                one = v[k]
-                parts = [
-                    jnp.where((lane3 >= ROWS * b) & (lane3 < ROWS * (b + 1)), one, 0.0)
-                    for b in range(GROUP)
-                ]
-                parts.append(jnp.zeros((8, LANES), F32))
-                blocks.append(jnp.concatenate(parts, 0).astype(BF16))
-            return jnp.concatenate(blocks, 1)
-
-        def masked(v):
-            v3 = v.reshape(8, 16, 256)
-            return jnp.concatenate(
-                [(v3 * hm[16 * k : 16 * (k + 1), :][None]).reshape(128, 256) for k in range(HEADS)], 0
-            )
-
-        dv = nn(wide(p), masked(dg))
-        dk = nn(wide(ds), masked(qg)) * scale
+    def wide_rows(v):
+        blocks = []
+        for k in range(HEADS):
+            one = v[k]
+            parts = [
+                jnp.where((lane3 >= ROWS * b) & (lane3 < ROWS * (b + 1)), one, 0.0)
+                for b in range(GROUP)
+            ]
+            parts.append(jnp.zeros((8, LANES), F32))
+            blocks.append(jnp.concatenate(parts, 0).astype(BF16))
+        return jnp.concatenate(blocks, 1)
+
+    def masked(v):
+        v3 = v.reshape(8, 16, 256)
+        return jnp.concatenate(
+            [(v3 * hm[16 * k : 16 * (k + 1), :][None]).reshape(128, 256) for k in range(HEADS)], 0
+        )
+
+    def attn_back(i, carry):
+        r0 = pl.multiple_of(i * (LOCK2 * GROWS), 8)
+        base0 = pl.multiple_of(i * (LOCK2 * 3 * HJ), 64)
+        p0 = pl.multiple_of(i * (LOCK2 * HJ), 64)
+        sets = range(LOCK2)
+        qg = [get_rows(qs, r0 + GROWS * k, LANES).astype(BF16) for k in sets]
+        dg = [get_rows(os_, r0 + GROWS * k, LANES).astype(BF16) for k in sets]
+        dp = [squeeze(nt(vbd[pl.ds(base0 + 3 * HJ * k, 3 * HJ), :], dg[k])) for k in sets]
+        p = [psc[pl.ds(p0 + HJ * k, HJ), :].reshape(HEADS, ROWS, LANES) for k in sets]
+        t = [jnp.sum(p[k] * dp[k], 1, keepdims=True) for k in sets]
+        ds = [p[k] * (dp[k] - t[k]) for k in sets]
+        dst = [v.reshape(HJ, LANES).T for v in ds]
+        dv = [nn(wide_rows(p[k]), masked(dg[k])) for k in sets]
+        dk = [nn(wide_rows(ds[k]), masked(qg[k])) * scale for k in sets]
         for b in range(GROUP):
-            dq = nn(
-                dst[ROWS * b : ROWS * (b + 1), :].astype(BF16), kbd[pl.ds(base + HJ * b, HJ), :]
-            )
-            put_rows(qs, r + ROWS * b, (dq * scale).astype(BF16).astype(F32))
-        put_rows(vs, r, dv.astype(BF16).astype(F32)[0:GROWS])
-        put_rows(ks, r, dk.astype(BF16).astype(F32)[0:GROWS])
-        return 0
-
-    lax.fori_loop(0, groups, attn_back, 0)
-
-    def dense3(i, carry):
+            for k in sets:
+                dq = nn(
+                    dst[k][ROWS * b : ROWS * (b + 1), :].astype(BF16),
+                    kbd[pl.ds(base0 + HJ * (3 * k + b), HJ), :],
+                )
+                put_rows(qs, r0 + GROWS * k + ROWS * b, (dq * scale).astype(BF16).astype(F32))
+        for k in sets:
+            put_rows(vs, r0 + GROWS * k, dv[k].astype(BF16).astype(F32)[0:GROWS])
+            put_rows(ks, r0 + GROWS * k, dk[k].astype(BF16).astype(F32)[0:GROWS])
+        return carry
+
+    lax.fori_loop(0, groups // LOCK2, attn_back, 0)
+
+    def dense3(t0, count, carry):
         dg1, dn1 = carry
-        dq = get_tokens(qs, i).astype(BF16)
-        dk = get_tokens(ks, i).astype(BF16)
-        dv = get_tokens(vs, i).astype(BF16)
-        dqt[at(i), :] = dq
-        dkt[at(i), :] = dk
-        dvt[at(i), :] = dv
+        at = rows_at(t0, count)
+        dq = get_tokens(qs, t0, count).astype(BF16)
+        dk = get_tokens(ks, t0, count).astype(BF16)
+        dv = get_tokens(vs, t0, count).astype(BF16)
+        dqkv[at, :] = jnp.concatenate([dq, dk, dv], 1)
         dh = nt(dq, wq[...]) + nt(dk, wk[...]) + nt(dv, wv[...])
-        xh = xh1[at(i), :]
-        ig = dx2s[at(i), :] + norm_back(dh, xh, r1[at(i), :], g1)
-        ig_ref[:, pl.ds(pl.multiple_of(i * (2 * D), 128), 2 * D)] = join_pair(ig, n)
+        xh = xh1[at, :]
+        ig = dx2s[at, :] + norm_back(dh, xh, r1[at, :], g1)
+        ig_ref[:, pl.ds(pl.multiple_of(t0 * D, 128), count * D)] = join_tokens(ig, n)
         return dg1 + rows8(dh * xh), dn1 + rows8(dh)
 
-    dg1, dn1 = lax.fori_loop(0, pairs, dense3, (zero, zero))
-    dwq = over_tokens(acc, h, dqt)
-    store_square(dwq, gflat, 0, D, tmp)
-    store_square(over_tokens(acc, h, dkt), gflat, 288, D, tmp)
-    dwv = over_tokens(acc, h, dvt)
-    store_square(dwv, gflat, 576, D, tmp)
-
-    vecs = [total(dg1), total(dn1), dwq[D : D + 1], dwv[D : D + 1], dbo, total(dg2), total(dn2), total(db2)]
+    dg1, dn1 = over_token_chunks(dense3, WIDTH3, (zero, zero))
+    dw = over_tokens(acc3, h, dqkv)
+    for k in range(3):
+        store_square(dw[:, 256 * k : 256 * (k + 1)], gflat, 288 * k, D, tmp)
+
+    vecs = [total(dg1), total(dn1), dw[D : D + 1, 0:256], dw[D : D + 1, 512:768], dbo, total(dg2), total(dn2), total(db2)]
     for k in range(4):
         a, b = vecs[2 * k], vecs[2 * k + 1]
         gflat[VEC_AT + 3 * k : VEC_AT + 3 * k + 1, :] = a[:, 0:128]
@@ -394,10 +415,10 @@
         + [vm((groups * HJ, LANES), F32)]
         + [vm((toks, 256), F32), vm((toks, 1), F32), vm((toks, 256), F32)]
         + [tok, tok, tok, vm((toks, 2 * FF), BF16), tok]
-        + [tok] * 5
+        + [tok, tok, vm((toks, 3 * 256), BF16)]
         + [vm((256, 256), BF16)] * 4
         + [vm((256, 2 * FF), BF16), vm((FF, 256), BF16), vm((2, FF, 128), F32)]
-        + [vm((320, 256), BF16), vm((128, 256), BF16), vm((256, 256), F32), vm((256, 512), F32)]
+        + [vm((320, 256), BF16), vm((128, 256), BF16), vm((256, 256), F32), vm((256, 512), F32), vm((256, 768), F32)]
     )
     return pl.pallas_call(
         block_kernel,

time: 130 us -> 82 us (0.63)
  Pallas kernels: 122 us -> 74.6 us
    pallas_call x1, Pallas kernels: 81.3 us -> 33.6 us  [block(): pl.pallas_call(block_kernel, out_shape=(jax.ShapeDtypeStruct(x.shape, BF1...]
where the time goes in v2:
time: 82 us; the launch traced here: 81.7 us
  Pallas kernels  74.6 us (91%)
  local copies, waits for them, and re-layouts  3.78 us (5%)
  between operations  2.56 us (3%)
    pallas_call x1, Pallas kernels, block(): pl.pallas_call(block_kernel, out_shape=(jax.ShapeDtypeStruct(x.shape, BF1...  33.6 us
    pallas_call x1, Pallas kernels, scatter(): pl.pallas_call(functools.partial(scatter_kernel, wide), out_shape=(jax.Sh...  24.3 us
    pallas_call x1, Pallas kernels, gather(): pl.pallas_call(functools.partial(gather_kernel, wide), out_shape=jax.Shap...  16.8 us
    unnamed x12, local copies, waits for them, and re-layouts  3.27 us

profile of v2, /device:TPU:0, one launch (start us, length us, event | category | flops | bytes accessed | tf_op | source)
XLA Modules:
  0.0 81.7 jit_solution(14031264964261710367)
XLA Ops:
  0.6 0.0 copy-start.2
  0.6 0.9 %copy-done.2 = f32[18560]{0:T(1024)S(1)} copy-done((f32[18560]{0:T(1024)S(1)}, f32[18560]{0:T(1024)}, u32[]{:S(2)}) %copy-start.2) | copy-done | bytes 74264
  1.5 16.8 %gather.1.gathered = f32[16,160,128]{2,1,0:T(8,128)S(1)} custom-call(f32[145,128]{1,0:T(8,128)S(1)} %bitcast.7), custom_call_target="tpu_custom_call" | custom-call | tf_op jit(solution)/shard_map/gather/pallas_call | solution.py:513
  18.3 0.0 copy-start
  18.3 1.1 %copy-done = f32[16,160,128]{2,1,0:T(8,128)} copy-done((f32[16,160,128]{2,1,0:T(8,128)}, f32[16,160,128]{2,1,0:T(8,128)S(1)}, u32[]{:S(2)}) %copy-start) | copy-done | bytes 1310744
  19.4 0.0 copy-start.3
  19.4 0.0 copy-start.4
  19.4 0.0 copy-start.5
  19.4 33.6 %block.1 = (bf16[48,6528]{1,0:T(8,128)(2,1)}, f32[48,6528]{1,0:T(8,128)}, f32[16,160,128]{2,1,0:T(8,128)}) custom-call(bf16[48,6528]{1,0:T(8,128)(2,1)} %x_ref.1, bf16[48,6528]{1,0:T(8,128)(2,1)} %dy_ref.1, f32[16,160,128]{2,1,0:T(8,128)} %copy-done), custom_call_target="tpu_custom_call" | custom-call | tf_op jit(solution)/shard_map/block/pallas_call | solution.py:423
  52.9 0.0 copy-start.1
  52.9 1.3 %copy-done.1 = f32[16,160,128]{2,1,0:T(8,128)S(1)} copy-done((f32[16,160,128]{2,1,0:T(8,128)S(1)}, f32[16,160,128]{2,1,0:T(8,128)}, u32[]{:S(2)}) %copy-start.1) | copy-done | bytes 1310744
  54.2 24.3 %scatter.1 = (f32[145,128]{1,0:T(8,128)S(1)}, f32[8,128]{1,0:T(8,128)S(1)}) custom-call(f32[4,4,160,128]{3,2,1,0:T(8,128)S(1)} %bitcast.6), custom_call_target="tpu_custom_call" | custom-call | tf_op jit(solution)/shard_map/scatter/pallas_call | solution.py:613
  78.6 0.5 slice.3
  79.8 0.0 copy-done.3
  79.8 0.0 copy-done.4
  79.8 0.0 copy-done.5
  79.8 0.7 fusion.1
Async XLA Ops:
  0.6 0.9 %copy-start.2 = (f32[18560]{0:T(1024)S(1)}, f32[18560]{0:T(1024)}, u32[]{:S(2)}) copy-start(f32[18560]{0:T(1024)} %param.7) | copy-start | bytes 222724
  18.3 1.1 %copy-start = (f32[16,160,128]{2,1,0:T(8,128)}, f32[16,160,128]{2,1,0:T(8,128)S(1)}, u32[]{:S(2)}) copy-start(f32[16,160,128]{2,1,0:T(8,128)S(1)} %gather.1.gathered) | copy-start | bytes 3932164
  19.4 60.4 %copy-start.3 = (f32[18560]{0:T(1024)S(1)}, f32[18560]{0:T(1024)}, u32[]{:S(2)}) copy-start(f32[18560]{0:T(1024)} %param.7) | copy-start | bytes 222724
  19.4 60.5 %copy-start.4 = (f32[18560]{0:T(1024)S(1)}, f32[18560]{0:T(1024)}, u32[]{:S(2)}) copy-start(f32[18560]{0:T(1024)} %param.8) | copy-start | bytes 222724
  19.4 60.5 %copy-start.5 = (f32[18560]{0:T(1024)S(1)}, f32[18560]{0:T(1024)}, u32[]{:S(2)}) copy-start(f32[18560]{0:T(1024)} %param.9) | copy-start | bytes 222724
  52.9 1.3 %copy-start.1 = (f32[16,160,128]{2,1,0:T(8,128)S(1)}, f32[16,160,128]{2,1,0:T(8,128)}, u32[]{:S(2)}) copy-start(f32[16,160,128]{2,1,0:T(8,128)} %get-tuple-element.15) | copy-start | bytes 3932164

commit v3 on v2

v3 whole, which is shorter than its diff:
```python
import functools
import math

import jax
import jax.numpy as jnp
from jax import lax
from jax.experimental import pallas as pl
from jax.experimental.pallas import tpu as pltpu
from jax.sharding import PartitionSpec as P

D = 192
HEADS = 8
HEAD_DIM = 24
FF = 256
SEQ = 34
STEP = 5
ROWS = 40
GROUP = 3
GROWS = GROUP * ROWS
HJ = HEADS * ROWS
LANES = 128
F32 = jnp.float32
BF16 = jnp.bfloat16
MATS = ((0, D), (288, D), (576, D), (864, D), (1920, FF))
W1_AT = 1152
WIDTH1, WIDTH2, WIDTH3, DW_STEPS = 4, 4, 4, 2
LOCK1, LOCK2 = 4, 4
VEC_AT = 2304
USED_ROWS = VEC_AT + 16
QKV_ROWS = 864
GELU_C = math.sqrt(2.0 / math.pi)


def nn(a, b):
    return lax.dot_general(a, b, (((1,), (0,)), ((), ())), preferred_element_type=F32)


def nt(a, b):
    return lax.dot_general(a, b, (((1,), (1,)), ((), ())), preferred_element_type=F32)


def tn(a, b):
    return lax.dot_general(a, b, (((0,), (0,)), ((), ())), preferred_element_type=F32)


def low_half(v):
    lane = lax.broadcasted_iota(jnp.int32, v.shape, 1)
    return lane < 64


def load_square(flat, base, rows, tmp, out):
    half = rows // 2
    f0 = flat[pl.ds(base, half, stride=3), :]
    f1 = flat[pl.ds(base + 1, half, stride=3), :]
    f2 = flat[pl.ds(base + 2, half, stride=3), :]
    r1 = pltpu.roll(f1, 64, 1)
    r2 = pltpu.roll(f2, 64, 1)
    left = low_half(f0)
    lo, hi = tmp.at[0], tmp.at[1]
    lo[pl.ds(0, half, stride=2), :] = f0
    hi[pl.ds(0, half, stride=2), :] = jnp.where(left, f1, 0.0)
    lo[pl.ds(1, half, stride=2), :] = jnp.where(left, r1, r2)
    hi[pl.ds(1, half, stride=2), :] = jnp.where(left, r2, 0.0)
    out[0:rows, 0:128] = lo[0:rows, :].astype(BF16)
    out[0:rows, 128:256] = hi[0:rows, :].astype(BF16)
    if rows < 256:
        out[rows:256, :] = jnp.zeros((256 - rows, 256), BF16)


def store_square(val, flat, base, rows, tmp):
    half = rows // 2
    lo, hi = tmp.at[0], tmp.at[1]
    lo[0:rows, :] = val[0:rows, 0:128]
    hi[0:rows, :] = val[0:rows, 128:256]
    e0 = lo[pl.ds(0, half, stride=2), :]
    e1 = hi[pl.ds(0, half, stride=2), :]
    o0 = pltpu.roll(lo[pl.ds(1, half, stride=2), :], 64, 1)
    o1 = pltpu.roll(hi[pl.ds(1, half, stride=2), :], 64, 1)
    left = low_half(e0)
    flat[pl.ds(base, half, stride=3), :] = e0
    flat[pl.ds(base + 1, half, stride=3), :] = jnp.where(left, e1, o0)
    flat[pl.ds(base + 2, half, stride=3), :] = jnp.where(left, o0, o1)


def norm_fwd(x):
    mean = jnp.sum(x, -1, keepdims=True) * (1.0 / D)
    right = x[:, 128:256] - mean
    c = jnp.concatenate([x[:, 0:128] - mean, jnp.where(low_half(right), right, 0.0)], 1)
    var = jnp.sum(c * c, -1, keepdims=True) * (1.0 / D)
    r = lax.rsqrt(var + 1e-05)
    return c * r, r


def norm_back(d, xh, r, g):
    e = d * g
    m1 = jnp.sum(e, -1, keepdims=True) * (1.0 / D)
    m2 = jnp.sum(e * xh, -1, keepdims=True) * (1.0 / D)
    return r * (e - m1 - xh * m2)


def rows8(v):
    return jnp.sum(v.reshape(v.shape[0] // 8, 8, v.shape[1]), 0)


def split_tokens(v, count):
    zero = jnp.zeros((v.shape[0], 256 - D), v.dtype)
    return jnp.concatenate(
        [jnp.concatenate([v[:, D * t : D * (t + 1)], zero], 1) for t in range(count)], 0
    )


def join_tokens(v, n):
    return jnp.concatenate([v[n * t : n * (t + 1), 0:D] for t in range(v.shape[0] // n)], 1)


def factors(wide):
    inner = max(k for k in range(1, int(math.isqrt(wide)) + 1) if wide % k == 0)
    return wide // inner, inner


def remote(src, dst, send, recv, where):
    return pltpu.make_async_remote_copy(
        src_ref=src,
        dst_ref=dst,
        send_sem=send,
        recv_sem=recv,
        device_id=where,
        device_id_type=pl.DeviceIdType.MESH,
    )


def greet(devices):
    barrier = pltpu.get_barrier_semaphore()
    for dev in devices:
        pl.semaphore_signal(barrier, inc=1, device_id=dev, device_id_type=pl.DeviceIdType.MESH)
    pl.semaphore_wait(barrier, len(devices))


def step_kernel(
    wide,
    x_hbm, dy_hbm, shard, out_hbm, ig_hbm, own, squares,
    x_ref, dy_ref, out_ref, ig_ref, flat, gflat,
    qs, ks, vs, os_, kbd, vbd, psc, xh1, r1, dx2s, h, h2, z, dul, o_t, dal, dyt, dqkv,
    wq, wk, wv, wo, w1, w2, tmp, hm2, hm, acc, acc2, acc3,
    buf, parts, sib_in, plane_in, out_p, col_in, out_c, res, vec_own, vec_sib, vec_plane, vec_col,
    vec_at, sq_plane, sq_col,
    io_sem, g_col, g_fw, g_sib, g_recv, g_recv_sib, s_send, s_recv, p_send, p_recv, c_send, c_recv,
    f_sem, v_send, v_recv, n_send, n_recv,
):
    n = x_ref.shape[0]
    toks = n * SEQ
    pairs = SEQ // 2
    groups = n // GROUP
    rows = shard.shape[0]
    half = buf.shape[1] // 2
    outer, inner = factors(wide)
    me, core = lax.axis_index("wide"), lax.axis_index("narrow")
    zo, pi = me // inner, lax.rem(me, inner)
    mine = pl.ds(pl.multiple_of(core * half, 8), half)
    theirs = pl.ds(pl.multiple_of((1 - core) * half, 8), half)
    sibling = (me, 1 - core)
    around = [lax.rem(pi + k, inner) for k in range(1, inner)]
    along = [lax.rem(zo + k, outer) for k in range(1, outer)]
    plane = [(zo * inner + q, core) for q in around]
    column = [(t * inner + pi, core) for t in along]
    first = -(-QKV_ROWS // (rows * inner))

    copies_in = [
        pltpu.make_async_copy(x_hbm, x_ref, io_sem.at[0]),
        pltpu.make_async_copy(dy_hbm, dy_ref, io_sem.at[1]),
    ]
    for copy in copies_in:
        copy.start()

    greet(plane + column + [sibling])
    buf[me, 0:rows, :] = shard[...]
    buf[me, rows:, :] = jnp.zeros((buf.shape[1] - rows, LANES), F32)

    def push(s, send, recvs, where):
        return remote(buf.at[s, mine], buf.at[s, mine], send, recvs.at[s], where)

    def arrived(s, recvs, part):
        remote(buf.at[s, part], buf.at[s, part], g_sib.at[s], recvs.at[s], sibling).wait_recv()

    def forwards(t, s):
        return [push(s, g_fw.at[t, k], g_recv, where) for k, where in enumerate(plane)]

    own_pushes = [push(me, g_col.at[k], g_recv, where) for k, where in enumerate(column)]
    own_pushes += forwards(zo, me)
    for copy in own_pushes:
        copy.start()

    def to_sibling(s):
        return push(s, g_sib.at[s], g_recv_sib, sibling)

    def forward_level(t):
        s = t * inner + pi

        @pl.when(t != zo)
        def _():
            arrived(s, g_recv, mine)
            for copy in forwards(t, s):
                copy.start()
            to_sibling(s).start()

    def pass_level(t):
        for q in around:
            s = t * inner + q
            arrived(s, g_recv, mine)
            to_sibling(s).start()

    def whole_shard(s):
        @pl.when(s != me)
        def _():
            arrived(s, g_recv_sib, theirs)

    def unpack(s):
        flat[rows * s : rows * (s + 1), :] = buf[s, 0:rows, :]

    vec_shards = range(VEC_AT // rows, (USED_ROWS - 1) // rows + 1)
    early_shards = [s for s in range(wide) if s < first * inner or s in vec_shards]
    late_shards = [s for s in range(wide) if s not in early_shards]

    lane = lax.broadcasted_iota(jnp.int32, (80, 256), 1)
    row = lax.broadcasted_iota(jnp.int32, (80, 256), 0)
    for p in range(4):
        lo = jnp.where(row < ROWS, HEAD_DIM * 2 * p, HEAD_DIM * (2 * p + 1))
        hm2[80 * p : 80 * (p + 1), :] = jnp.where(
            (lane >= lo) & (lane < lo + HEAD_DIM), 1.0, 0.0
        ).astype(BF16)
    lane16 = lax.broadcasted_iota(jnp.int32, (16, 256), 1)
    for k in range(HEADS):
        hm[16 * k : 16 * (k + 1), :] = jnp.where(
            (lane16 >= HEAD_DIM * k) & (lane16 < HEAD_DIM * (k + 1)), 1.0, 0.0
        ).astype(BF16)
    ones_lane = (lax.broadcasted_iota(jnp.int32, (toks, 64), 1) == 0).astype(F32).astype(BF16)
    for ref in (h, h2, o_t):
        ref[:, D:256] = ones_lane
    for ref in (qs, ks, vs, os_):
        ref[...] = jnp.zeros(ref.shape, F32)

    parts[...] = jnp.zeros(parts.shape, F32)
    vec_at[...] = jnp.zeros(vec_at.shape, F32)
    for t in range(outer):
        forward_level(t)

    def tokens_of(ref, t, count):
        return split_tokens(
            ref[:, pl.ds(pl.multiple_of(t * D, 128), count * D)].astype(F32), count
        )

    def put_tokens(ref, t, val):
        for half in range(2):
            for k in range(val.shape[0] // n):
                ref.at[half][pl.ds(t + k, n, stride=ROWS), :] = val[
                    n * k : n * (k + 1), 128 * half : 128 * (half + 1)
                ]

    def get_tokens(ref, t, count):
        return jnp.concatenate(
            [
                jnp.concatenate(
                    [ref.at[half][pl.ds(t + k, n, stride=ROWS), :] for half in range(2)], 1
                )
                for k in range(count)
            ],
            0,
        )

    def over_token_chunks(body, width, carry, hook=lambda i: None):
        whole = pairs // width

        def step(i, c):
            hook(i)
            return body(i * (2 * width), 2 * width, c)

        carry = lax.fori_loop(0, whole, step, carry)
        if pairs % width:
            carry = body(whole * 2 * width, 2 * (pairs % width), carry)
        return carry

    def get_rows(ref, start, count):
        return jnp.concatenate([ref[0, pl.ds(start, count), :], ref[1, pl.ds(start, count), :]], 1)

    def put_rows(ref, start, val):
        for half in range(2):
            ref[half, pl.ds(start, val.shape[0]), :] = val[:, 128 * half : 128 * (half + 1)]

    def rows_at(t, count):
        return pl.ds(pl.multiple_of(t * n, 32), count * n)

    def norm1(t, count, carry):
        at = rows_at(t, count)
        xh, r = norm_fwd(tokens_of(x_ref, t, count))
        xh1[at, :] = xh
        r1[at, :] = r
        return carry

    copies_in[0].wait()
    over_token_chunks(norm1, WIDTH1, 0)

    for t in range(first):
        pass_level(t)
    for t in range(first, outer):
        if any(s // inner == t for s in vec_shards):
            pass_level(t)
    for s in early_shards:
        whole_shard(s)
        unpack(s)
    for (base, count), ref in zip(MATS[0:3], (wq, wk, wv)):
        load_square(flat, base, count, tmp, ref)

    def vec(k):
        a = VEC_AT + 3 * (k // 2)
        zero = jnp.zeros((1, 64), F32)
        if k % 2 == 0:
            return jnp.concatenate([flat[a : a + 1, :], flat[a + 1 : a + 2, 0:64], zero], 1)
        return jnp.concatenate([flat[a + 1 : a + 2, 64:128], flat[a + 2 : a + 3, :], zero], 1)

    g1, n1, bq, bv, bo, g2, n2, b2 = [vec(k) for k in range(8)]
    b1 = jnp.concatenate([flat[VEC_AT + 12 + c : VEC_AT + 13 + c, :] for c in range(4)], 1)

    def dense1(t, count, carry):
        at = rows_at(t, count)
        hb = (xh1[at, :] * g1 + n1).astype(BF16)
        h[at, 0:D] = hb[:, 0:D]
        put_tokens(qs, t, (nn(hb, wq[...]) + bq).astype(BF16).astype(F32))
        put_tokens(ks, t, nn(hb, wk[...]).astype(BF16).astype(F32))
        put_tokens(vs, t, (nn(hb, wv[...]) + bv).astype(BF16).astype(F32))
        return carry

    over_token_chunks(dense1, WIDTH1, 0)

    lane3 = lax.broadcasted_iota(jnp.int32, (1, LANES), 1)

    def squeeze(v):
        return jnp.where(
            lane3 < ROWS, v[0:HJ], jnp.where(lane3 < 2 * ROWS, v[HJ : 2 * HJ], v[2 * HJ : 3 * HJ])
        ).reshape(HEADS, ROWS, LANES)

    jrow = lax.broadcasted_iota(jnp.int32, (1, ROWS, LANES), 1)
    cexp = math.log2(math.e) / math.sqrt(HEAD_DIM)
    scale = 1.0 / math.sqrt(HEAD_DIM)

    def attn(i, carry):
        @pl.when(i == 1)
        def _():
            for t in range(first, outer):
                if not any(s // inner == t for s in vec_shards):
                    pass_level(t)

        r0 = pl.multiple_of(i * (LOCK1 * GROWS), 8)
        base0 = pl.multiple_of(i * (LOCK1 * 3 * HJ), 64)
        p0 = pl.multiple_of(i * (LOCK1 * HJ), 64)
        sets = range(LOCK1)
        qg = [get_rows(qs, r0 + GROWS * k, LANES).astype(BF16) for k in sets]
        for k in sets:
            for src, dst in ((ks, kbd), (vs, vbd)):
                for b in range(GROUP):
                    one = get_rows(src, r0 + GROWS * k + ROWS * b, ROWS)
                    two = jnp.concatenate([one, one], 0).astype(BF16)
                    for p in range(4):
                        dst[pl.ds(base0 + HJ * (3 * k + b) + 80 * p, 80), :] = (
                            two * hm2[80 * p : 80 * (p + 1), :]
                        )
        st = [squeeze(nt(kbd[pl.ds(base0 + 3 * HJ * k, 3 * HJ), :], qg[k])) for k in sets]
        st = [jnp.where(jrow < SEQ, v, -1e30) for v in st]
        m = [jnp.max(v, 1, keepdims=True) for v in st]
        e = [jnp.exp2((st[k] - m[k]) * cexp) for k in sets]
        l = [1.0 / jnp.sum(v, 1, keepdims=True) for v in e]
        p = [(e[k] * l[k]).reshape(HJ, LANES) for k in sets]
        for k in sets:
            psc[pl.ds(p0 + HJ * k, HJ), :] = p[k]
        pt = [v.T for v in p]
        for b in range(GROUP):
            for k in sets:
                ob = nn(
                    pt[k][ROWS * b : ROWS * (b + 1), :].astype(BF16),
                    vbd[pl.ds(base0 + HJ * (3 * k + b), HJ), :],
                )
                put_rows(os_, r0 + GROWS * k + ROWS * b, ob.astype(BF16).astype(F32)[0:SEQ])
        return carry

    lax.fori_loop(0, groups // LOCK1, attn, 0)

    for s in late_shards:
        whole_shard(s)
        unpack(s)
    for (base, count), ref in zip(MATS[3:5], (wo, w2)):
        load_square(flat, base, count, tmp, ref)
    for c in range(4):
        w1[0:D, 128 * c : 128 * (c + 1)] = flat[pl.ds(W1_AT + c, D, stride=4), :].astype(BF16)
    w1[D:256, :] = jnp.zeros((256 - D, 2 * FF), BF16)
    copies_in[1].wait()

    def dense2(t0, count, carry):
        dg2, dn2, db2 = carry
        at = rows_at(t0, count)
        o = get_tokens(os_, t0, count).astype(BF16)
        o_t[at, 0:D] = o[:, 0:D]
        x2 = tokens_of(x_ref, t0, count) + (nn(o, wo[...]) + bo)
        xh, r = norm_fwd(x2)
        hb = (xh * g2 + n2).astype(BF16)
        h2[at, 0:D] = hb[:, 0:D]
        u = nn(hb, w1[...]) + b1
        gate, up = u[:, :FF], u[:, FF:]
        sq = gate * gate
        t = jnp.tanh(gate * (GELU_C + (GELU_C * 0.044715) * sq))
        half = 0.5 + 0.5 * t
        act = gate * half
        zb = (act * up).astype(BF16)
        z[at, :] = zb
        y = x2 + nn(zb, w2[...]) + b2
        out_ref[:, pl.ds(pl.multiple_of(t0 * D, 128), count * D)] = join_tokens(y, n).astype(BF16)
        dyf = tokens_of(dy_ref, t0, count)
        dyb = dyf.astype(BF16)
        dyt[at, :] = dyb
        dz = nt(dyb, w2[...])
        slope = half + gate * (0.5 - 0.5 * t * t) * (GELU_C + (3 * GELU_C * 0.044715) * sq)
        du = jnp.concatenate([(dz * up * slope).astype(BF16), (dz * act).astype(BF16)], 1)
        dul[at, :] = du
        dh = nt(du, w1[...])
        dx2 = dyf + norm_back(dh, xh, r, g2)
        dx2s[at, :] = dx2
        da = dx2.astype(BF16)
        dal[at, :] = da
        put_tokens(os_, t0, nt(da, wo[...]).astype(BF16).astype(F32))
        return dg2 + rows8(dh * xh), dn2 + rows8(dh), db2 + rows8(dyf)

    zero = jnp.zeros((8, 256), F32)
    dg2, dn2, db2 = over_token_chunks(dense2, WIDTH2, (zero, zero, zero))

    copy_out = pltpu.make_async_copy(out_ref, out_hbm, io_sem.at[2])
    copy_out.start()

    def total(v):
        return jnp.sum(v, 0, keepdims=True)

    def over_tokens(acc, a, b):
        acc[...] = jnp.zeros(acc.shape, F32)
        steps = DW_STEPS
        size = toks // steps

        @pl.loop(0, steps)
        def _(i):
            at = pl.ds(pl.multiple_of(i * size, 16), size)
            acc[...] += tn(a[at, :], b[at, :])

        return acc[...]

    store_square(over_tokens(acc, z, dyt), gflat, 1920, FF, tmp)
    dw1 = over_tokens(acc2, h2, dul)
    for c in range(4):
        gflat[pl.ds(W1_AT + c, D, stride=4), :] = dw1[0:D, 128 * c : 128 * (c + 1)]
        vec_own[12 + c : 13 + c, :] = dw1[D : D + 1, 128 * c : 128 * (c + 1)]
    dwo = over_tokens(acc, o_t, dal)
    store_square(dwo, gflat, 864, D, tmp)
    dbo = dwo[D : D + 1]

    def pack(lo, hi):
        for s in range(lo * inner, hi * inner):
            stop = min(rows * (s + 1), VEC_AT)
            if stop > rows * s:
                parts[s // inner, s % inner, 0 : stop - rows * s, :] = gflat[rows * s : stop, :]

    places = around + [pi]

    def sib_copies(part, lo, hi):
        return [
            remote(
                parts.at[lo:hi, q, theirs], sib_in.at[lo:hi, q],
                s_send.at[part, k], s_recv.at[part, q], sibling,
            )
            for k, q in enumerate(places)
        ]

    def plane_copies(part, lo, hi):
        return [
            remote(
                out_p.at[k, lo:hi], plane_in.at[pi, lo:hi],
                p_send.at[part, k], p_recv.at[part, pi], plane[k],
            )
            for k in range(inner - 1)
        ]

    def col_copy(t):
        return remote(
            out_c.at[t], col_in.at[zo], c_send.at[t], c_recv.at[zo], (t * inner + pi, core)
        )

    def sum_cores(part, lo, hi):
        sends = plane_copies(part, lo, hi)
        for k, q in enumerate(places):
            remote(
                sib_in.at[lo:hi, q], sib_in.at[lo:hi, q],
                s_send.at[part, k], s_recv.at[part, q], sibling,
            ).wait_recv()
            both = parts[lo:hi, q, mine, :] + sib_in[lo:hi, q]
            if k < inner - 1:
                out_p[k, lo:hi] = both
                sends[k].start()
            else:
                plane_in[pi, lo:hi] = both

    def sum_plane(part, lo, hi):
        for k, q in enumerate(around):
            remote(
                plane_in.at[q, lo:hi], plane_in.at[q, lo:hi],
                p_send.at[part, k], p_recv.at[part, q], sibling,
            ).wait_recv()
        for t in range(lo, hi):
            line = plane_in[0, t]
            for q in range(1, inner):
                line = line + plane_in[q, t]
            out_c[t] = line

            @pl.when(t != zo)
            def _():
                col_copy(t).start()

    pack(first, outer)
    for copy in sib_copies(0, first, outer):
        copy.start()

    def wide_rows(v):
        blocks = []
        for k in range(HEADS):
            one = v[k]
            parts = [
                jnp.where((lane3 >= ROWS * b) & (lane3 < ROWS * (b + 1)), one, 0.0)
                for b in range(GROUP)
            ]
            parts.append(jnp.zeros((8, LANES), F32))
            blocks.append(jnp.concatenate(parts, 0).astype(BF16))
        return jnp.concatenate(blocks, 1)

    def masked(v):
        v3 = v.reshape(8, 16, 256)
        return jnp.concatenate(
            [(v3 * hm[16 * k : 16 * (k + 1), :][None]).reshape(128, 256) for k in range(HEADS)], 0
        )

    def attn_back(i, carry):
        @pl.when(i == 1)
        def _():
            sum_cores(0, first, outer)

        @pl.when(i == 3)
        def _():
            sum_plane(0, first, outer)

        r0 = pl.multiple_of(i * (LOCK2 * GROWS), 8)
        base0 = pl.multiple_of(i * (LOCK2 * 3 * HJ), 64)
        p0 = pl.multiple_of(i * (LOCK2 * HJ), 64)
        sets = range(LOCK2)
        qg = [get_rows(qs, r0 + GROWS * k, LANES).astype(BF16) for k in sets]
        dg = [get_rows(os_, r0 + GROWS * k, LANES).astype(BF16) for k in sets]
        dp = [squeeze(nt(vbd[pl.ds(base0 + 3 * HJ * k, 3 * HJ), :], dg[k])) for k in sets]
        p = [psc[pl.ds(p0 + HJ * k, HJ), :].reshape(HEADS, ROWS, LANES) for k in sets]
        t = [jnp.sum(p[k] * dp[k], 1, keepdims=True) for k in sets]
        ds = [p[k] * (dp[k] - t[k]) for k in sets]
        dst = [v.reshape(HJ, LANES).T for v in ds]
        dv = [nn(wide_rows(p[k]), masked(dg[k])) for k in sets]
        dk = [nn(wide_rows(ds[k]), masked(qg[k])) * scale for k in sets]
        for b in range(GROUP):
            for k in sets:
                dq = nn(
                    dst[k][ROWS * b : ROWS * (b + 1), :].astype(BF16),
                    kbd[pl.ds(base0 + HJ * (3 * k + b), HJ), :],
                )
                put_rows(qs, r0 + GROWS * k + ROWS * b, (dq * scale).astype(BF16).astype(F32))
        for k in sets:
            put_rows(vs, r0 + GROWS * k, dv[k].astype(BF16).astype(F32)[0:GROWS])
            put_rows(ks, r0 + GROWS * k, dk[k].astype(BF16).astype(F32)[0:GROWS])
        return carry

    lax.fori_loop(0, groups // LOCK2, attn_back, 0)

    def collect(t0, count, carry):
        at = rows_at(t0, count)
        dqkv[at, :] = jnp.concatenate(
            [get_tokens(ref, t0, count).astype(BF16) for ref in (qs, ks, vs)], 1
        )
        return carry

    over_token_chunks(collect, WIDTH3, 0)
    dw = over_tokens(acc3, h, dqkv)
    for k in range(3):
        store_square(dw[:, 256 * k : 256 * (k + 1)], gflat, 288 * k, D, tmp)
    pack(0, first)
    for copy in sib_copies(1, 0, first):
        copy.start()

    def dense3(t0, count, carry):
        dg1, dn1 = carry
        at = rows_at(t0, count)
        dh = (
            nt(dqkv[at, 0:256], wq[...])
            + nt(dqkv[at, 256:512], wk[...])
            + nt(dqkv[at, 512:768], wv[...])
        )
        xh = xh1[at, :]
        ig = dx2s[at, :] + norm_back(dh, xh, r1[at, :], g1)
        ig_ref[:, pl.ds(pl.multiple_of(t0 * D, 128), count * D)] = join_tokens(ig, n)
        return dg1 + rows8(dh * xh), dn1 + rows8(dh)

    def hook3(i):
        @pl.when(i == 1)
        def _():
            sum_cores(1, 0, first)

    dg1, dn1 = over_token_chunks(dense3, WIDTH3, (zero, zero), hook3)

    vecs = [
        total(dg1), total(dn1), dw[D : D + 1, 0:256], dw[D : D + 1, 512:768],
        dbo, total(dg2), total(dn2), total(db2),
    ]
    for k in range(4):
        a, b = vecs[2 * k], vecs[2 * k + 1]
        vec_own[3 * k : 3 * k + 1, :] = a[:, 0:128]
        vec_own[3 * k + 1 : 3 * k + 2, :] = jnp.concatenate([a[:, 128:192], b[:, 0:64]], 1)
        vec_own[3 * k + 2 : 3 * k + 3, :] = b[:, 64:192]
    vec_sends = [remote(vec_own, vec_sib, v_send.at[0], v_recv.at[0], sibling)]
    vec_sends[0].start()
    copy_ig = pltpu.make_async_copy(ig_ref, ig_hbm, io_sem.at[3])
    copy_ig.start()

    def spread(slots, at, sends, recvs, base, where):
        out = [
            remote(slots.at[at], slots.at[at], sends.at[base + k], recvs.at[base + at], dev)
            for k, dev in enumerate(where)
        ]
        for copy in out:
            copy.start()
        return out

    def collected(slots, others, sends, recvs, base):
        for k, q in enumerate(others):
            remote(
                slots.at[q], slots.at[q], sends.at[base + k], recvs.at[base + q], sibling
            ).wait_recv()
        return jnp.sum(slots[...], 0)

    remote(vec_sib, vec_sib, v_send.at[0], v_recv.at[0], sibling).wait_recv()
    vec_plane[pi] = vec_own[...] + vec_sib[...]
    vec_sends += spread(vec_plane, pi, v_send, v_recv, 1, plane)
    sum_plane(1, 0, first)
    vec_col[zo] = collected(vec_plane, around, v_send, v_recv, 1)
    vec_sends += spread(vec_col, zo, v_send, v_recv, 1 + inner, column)

    col_in[zo] = out_c[zo]
    for t in along:
        remote(col_in.at[t], col_in.at[t], c_send.at[t], c_recv.at[t], sibling).wait_recv()
    line = col_in[0]
    for t in range(1, outer):
        line = line + col_in[t]
    res[mine, :] = line
    last = remote(res.at[mine], res.at[mine], f_sem.at[0], f_sem.at[1], sibling)
    last.start()
    vec = collected(vec_col, along, v_send, v_recv, 1 + inner)
    vec_at[VEC_AT:USED_ROWS, :] = vec
    remote(res.at[theirs], res.at[theirs], f_sem.at[0], f_sem.at[1], sibling).wait_recv()
    full = res[...]
    sq_plane[pi] = rows8(full * full)
    sq_sends = spread(sq_plane, pi, n_send, n_recv, 0, plane)
    own[...] = full[0:rows] + vec_at[pl.ds(me * rows, rows), :]
    sq_col[zo] = collected(sq_plane, around, n_send, n_recv, 0)
    sq_sends += spread(sq_col, zo, n_send, n_recv, inner, column)
    both = collected(sq_col, along, n_send, n_recv, inner) + rows8(vec * vec)
    squares[...] = jnp.broadcast_to(jnp.sum(both, keepdims=True), squares.shape)

    for copy in own_pushes + vec_sends + sq_sends + [last]:
        copy.wait_send()
    for t in range(outer):
        @pl.when(t != zo)
        def _(t=t):
            for copy in forwards(t, t * inner + pi):
                copy.wait_send()
            to_sibling(t * inner + pi).wait_send()
            col_copy(t).wait_send()

        for q in around:
            to_sibling(t * inner + q).wait_send()
    for part, lo, hi in ((0, first, outer), (1, 0, first)):
        for copy in sib_copies(part, lo, hi) + plane_copies(part, lo, hi):
            copy.wait_send()
    copy_out.wait()
    copy_ig.wait()


def step(x, dy, shard, wide):
    outer, inner = factors(wide)
    n, rows = x.shape[0], shard.shape[0]
    toks = n * SEQ
    groups = n // GROUP
    padded = (rows + 15) // 16 * 16
    half = padded // 2
    vm, dma = pltpu.VMEM, pltpu.SemaphoreType.DMA
    sm = vm((2, n * ROWS + 8, LANES), F32)
    tok = vm((toks, 256), BF16)
    tile = (8, LANES)
    scratch = (
        [vm(x.shape, BF16), vm(x.shape, BF16), vm(x.shape, BF16), vm(x.shape, F32)]
        + [vm((wide * rows, LANES), F32)] * 2
        + [sm] * 4
        + [vm((groups * 3 * HJ, 256), BF16)] * 2
        + [vm((groups * HJ, LANES), F32)]
        + [vm((toks, 256), F32), vm((toks, 1), F32), vm((toks, 256), F32)]
        + [tok, tok, tok, vm((toks, 2 * FF), BF16), tok]
        + [tok, tok, vm((toks, 3 * 256), BF16)]
        + [vm((256, 256), BF16)] * 4
        + [vm((256, 2 * FF), BF16), vm((FF, 256), BF16), vm((2, FF, 128), F32)]
        + [vm((320, 256), BF16), vm((128, 256), BF16)]
        + [vm((256, 256), F32), vm((256, 512), F32), vm((256, 768), F32)]
        + [vm((wide, padded, LANES), F32), vm((outer, inner, padded, LANES), F32)]
        + [vm((outer, inner, half, LANES), F32), vm((inner, outer, half, LANES), F32)]
        + [vm((inner - 1, outer, half, LANES), F32)]
        + [vm((outer, half, LANES), F32)] * 2
        + [vm((padded, LANES), F32)]
        + [vm((16, LANES), F32)] * 2
        + [vm((inner, 16, LANES), F32), vm((outer, 16, LANES), F32)]
        + [vm((wide * rows, LANES), F32)]
        + [vm((inner, *tile), F32), vm((outer, *tile), F32)]
        + [dma((4,)), dma((outer - 1,)), dma((outer, inner - 1)), dma((wide,)), dma((wide,)), dma((wide,))]
        + [dma((2, inner)), dma((2, inner)), dma((2, inner)), dma((2, inner))]
        + [dma((outer,)), dma((outer,)), dma((2,))]
        + [dma((1 + inner + outer,))] * 2
        + [dma((inner + outer,))] * 2
    )
    anywhere, vmem = pl.BlockSpec(memory_space=pl.ANY), pl.BlockSpec(memory_space=pltpu.VMEM)
    return pl.pallas_call(
        functools.partial(step_kernel, wide),
        out_shape=(
            jax.ShapeDtypeStruct(x.shape, BF16),
            jax.ShapeDtypeStruct(x.shape, F32),
            jax.ShapeDtypeStruct((rows, LANES), F32),
            jax.ShapeDtypeStruct(tile, F32),
        ),
        in_specs=[anywhere, anywhere, vmem],
        out_specs=(anywhere, anywhere, vmem, vmem),
        scratch_shapes=scratch,
        compiler_params=pltpu.CompilerParams(
            collective_id=0, has_side_effects=True, vmem_limit_bytes=60 * 2**20
        ),
        name="step",
    )(x, dy, shard)


def on_device(inputs, cotangent, master, first, second):
    rows = master.shape[0] // LANES
    block_out, input_grad, owned, squares = step(
        inputs, cotangent, master.reshape(rows, LANES), lax.axis_size("wide")
    )
    owned = owned.reshape(-1)
    squares = squares[0, 0]
    grad_norm = jnp.sqrt(squares)
    factor = jnp.minimum(1.0, 1.0 / (grad_norm + 1e-06))
    clipped = owned * factor
    new_first = 0.5 * first + 0.5 * clipped
    new_second = 0.5 * second + 0.5 * clipped * clipped
    fixed = 1.0 - 0.5**STEP
    new_master = master - 0.05 * (
        new_first / fixed / (jnp.sqrt(new_second / fixed) + 1e-08) + 0.1 * master
    )
    return (
        block_out,
        input_grad,
        clipped,
        grad_norm,
        new_master,
        new_master.astype(jnp.bfloat16),
        new_first,
        new_second,
    )


def solution(mesh):
    both, part = P(("wide", "narrow"), None), P("wide")
    return jax.shard_map(
        on_device,
        mesh=mesh,
        in_specs=(both, both, part, part, part),
        out_specs=(both, both, part, P(), part, part, part, part),
        check_vma=False,
    )
```

time: 82 us -> 76.6 us (0.934)
  Pallas kernels: 74.6 us -> 67.9 us
  other arithmetic: 0.74 us -> 1.62 us
    pallas_call x3 -> x1, Pallas kernels: 74.6 us -> 67.9 us  [step(): pl.pallas_call(functools.partial(step_kernel, wide), out_shape=(jax.Shape...]
    convert_element_type x1, other arithmetic: 0.74 us -> 1.62 us  [on_device(): new_master.astype(jnp.bfloat16)]
    unnamed x12 -> x10, local copies, waits for them, and re-layouts: 3.27 us -> 3 us
where the time goes in v3:
time: 76.6 us; the launch traced here: 76.3 us
  Pallas kernels  67.9 us (89%)
  local copies, waits for them, and re-layouts  4.28 us (6%)
  between operations  2.56 us (3%)
  other arithmetic  1.62 us (2%)
    pallas_call x1, Pallas kernels, step(): pl.pallas_call(functools.partial(step_kernel, wide), out_shape=(jax.Shape...  67.9 us
    unnamed x10, local copies, waits for them, and re-layouts  3 us
    convert_element_type x1, other arithmetic, on_device(): new_master.astype(jnp.bfloat16)  1.62 us

profile of v3, /device:TPU:0, one launch (start us, length us, event | category | flops | bytes accessed | tf_op | source)
XLA Modules:
  0.0 76.3 jit_solution(15188240904090809078)
XLA Ops:
  0.6 0.0 copy-start.1
  0.6 0.0 copy-start.2
  0.7 0.0 copy-start.3
  0.7 67.9 %step.1 = (bf16[48,6528]{1,0:T(8,128)(2,1)}, f32[48,6528]{1,0:T(8,128)}, f32[145,128]{1,0:T(8,128)}, f32[8,128]{1,0:T(8,128)}) custom-call(bf16[48,6528]{1,0:T(8,128)(2,1)} %x_hbm.1, bf16[48,6528]{1,0:T(8,128)(2,1)} %dy_hbm.1, f32[145,128]{1,0:T(8,128)} %bitcast.5), custom_call_target="tpu_custom_call" | custom-call | tf_op jit(solution)/shard_map/step/pallas_call | solution.py:731
  68.5 0.0 copy-start
  68.5 1.3 %slice.3 = f32[1,1]{1,0:T(1,128)} slice(f32[8,128]{1,0:T(8,128)} %get-tuple-element.15), slice={[0:1], [0:1]} | slice | bytes 8 | tf_op jit(solution)/shard_map/slice | solution.py:755
  70.6 0.0 copy-done.1
  70.6 0.0 copy-done.2
  70.6 0.0 copy-done.3
  70.6 1.6 %fusion.1 = (bf16[18560]{0:T(1024)(128)(2,1)}, f32[18560]{0:T(1024)}, f32[18560]{0:T(1024)}, f32[18560]{0:T(1024)}, f32[18560]{0:T(1024)}) fusion(f32[18560]{0:T(1024)S(1)} %copy-done.1, f32[18560]{0:T(1024)S(1)} %copy-done.2, f32[18560]{0:T(1024)S(1)} %copy-done.3, f32[145,128]{1,0:T(8,128)} %get-tuple-element.14, f32[]{:T(128)S(6)} %min.3), kind=kLoop, calls=%fused_computation.5 | loop fusion | flops 296960 | bytes 631044 | tf_op jit(solution)/shard_map/convert_element_type | solution.py:771
  72.2 1.9 %copy.15 = bf16[48,6528]{1,0:T(8,128)(2,1)} copy(bf16[48,6528]{1,0:T(8,128)(2,1)} %get-tuple-element.29) | data formatting | bytes 1253376
  74.2 0.0 copy-done
  74.2 1.0 %copy.16 = f32[48,6528]{1,0:T(8,128)} copy(f32[48,6528]{1,0:T(8,128)S(1)} %copy-done) | data formatting | bytes 2506752
Async XLA Ops:
  0.6 69.9 %copy-start.1 = (f32[18560]{0:T(1024)S(1)}, f32[18560]{0:T(1024)}, u32[]{:S(2)}) copy-start(f32[18560]{0:T(1024)} %param.7) | copy-start | bytes 222724
  0.6 69.9 %copy-start.2 = (f32[18560]{0:T(1024)S(1)}, f32[18560]{0:T(1024)}, u32[]{:S(2)}) copy-start(f32[18560]{0:T(1024)} %param.8) | copy-start | bytes 222724
  0.7 69.9 %copy-start.3 = (f32[18560]{0:T(1024)S(1)}, f32[18560]{0:T(1024)}, u32[]{:S(2)}) copy-start(f32[18560]{0:T(1024)} %param.9) | copy-start | bytes 222724
  68.5 5.6 %copy-start = (f32[48,6528]{1,0:T(8,128)S(1)}, f32[48,6528]{1,0:T(8,128)}, u32[]{:S(2)}) copy-start(f32[48,6528]{1,0:T(8,128)} %get-tuple-element.30) | copy-start | bytes 3760132

commit v4 on v3

--- a/solution.py
+++ b/solution.py
@@ -25,6 +25,7 @@
 W1_AT = 1152
 WIDTH1, WIDTH2, WIDTH3, DW_STEPS = 4, 4, 4, 2
 LOCK1, LOCK2 = 4, 4
+PIECES = 1
 VEC_AT = 2304
 USED_ROWS = VEC_AT + 16
 QKV_ROWS = 864
@@ -130,10 +131,11 @@
 
 
 def greet(devices):
-    barrier = pltpu.get_barrier_semaphore()
     for dev in devices:
-        pl.semaphore_signal(barrier, inc=1, device_id=dev, device_id_type=pl.DeviceIdType.MESH)
-    pl.semaphore_wait(barrier, len(devices))
+        pl.semaphore_signal(
+            pltpu.get_barrier_semaphore(), inc=1, device_id=dev,
+            device_id_type=pl.DeviceIdType.MESH,
+        )
 
 
 def step_kernel(
@@ -172,55 +174,9 @@
     for copy in copies_in:
         copy.start()
 
-    greet(plane + column + [sibling])
-    buf[me, 0:rows, :] = shard[...]
-    buf[me, rows:, :] = jnp.zeros((buf.shape[1] - rows, LANES), F32)
-
-    def push(s, send, recvs, where):
-        return remote(buf.at[s, mine], buf.at[s, mine], send, recvs.at[s], where)
-
-    def arrived(s, recvs, part):
-        remote(buf.at[s, part], buf.at[s, part], g_sib.at[s], recvs.at[s], sibling).wait_recv()
-
-    def forwards(t, s):
-        return [push(s, g_fw.at[t, k], g_recv, where) for k, where in enumerate(plane)]
-
-    own_pushes = [push(me, g_col.at[k], g_recv, where) for k, where in enumerate(column)]
-    own_pushes += forwards(zo, me)
-    for copy in own_pushes:
-        copy.start()
-
-    def to_sibling(s):
-        return push(s, g_sib.at[s], g_recv_sib, sibling)
-
-    def forward_level(t):
-        s = t * inner + pi
-
-        @pl.when(t != zo)
-        def _():
-            arrived(s, g_recv, mine)
-            for copy in forwards(t, s):
-                copy.start()
-            to_sibling(s).start()
-
-    def pass_level(t):
-        for q in around:
-            s = t * inner + q
-            arrived(s, g_recv, mine)
-            to_sibling(s).start()
-
-    def whole_shard(s):
-        @pl.when(s != me)
-        def _():
-            arrived(s, g_recv_sib, theirs)
-
-    def unpack(s):
-        flat[rows * s : rows * (s + 1), :] = buf[s, 0:rows, :]
-
-    vec_shards = range(VEC_AT // rows, (USED_ROWS - 1) // rows + 1)
-    early_shards = [s for s in range(wide) if s < first * inner or s in vec_shards]
-    late_shards = [s for s in range(wide) if s not in early_shards]
-
+    cross = [(zo * inner + q, 1 - core) for q in around]
+    known = plane + cross + column + [sibling]
+    greet(known)
     lane = lax.broadcasted_iota(jnp.int32, (80, 256), 1)
     row = lax.broadcasted_iota(jnp.int32, (80, 256), 0)
     for p in range(4):
@@ -241,6 +197,55 @@
 
     parts[...] = jnp.zeros(parts.shape, F32)
     vec_at[...] = jnp.zeros(vec_at.shape, F32)
+    pl.semaphore_wait(pltpu.get_barrier_semaphore(), len(known))
+    buf[me, 0:rows, :] = shard[...]
+    buf[me, rows:, :] = jnp.zeros((buf.shape[1] - rows, LANES), F32)
+
+    def push(s, send, recvs, where):
+        return remote(buf.at[s, mine], buf.at[s, mine], send, recvs.at[s], where)
+
+    def arrived(s, recvs, part):
+        remote(buf.at[s, part], buf.at[s, part], g_sib.at[s], recvs.at[s], sibling).wait_recv()
+
+    def forwards(t, s):
+        return [push(s, g_fw.at[t, k], g_recv, where) for k, where in enumerate(plane)]
+
+    own_pushes = [push(me, g_col.at[k], g_recv, where) for k, where in enumerate(column)]
+    own_pushes += forwards(zo, me)
+    for copy in own_pushes:
+        copy.start()
+
+    def to_sibling(s):
+        return push(s, g_sib.at[s], g_recv_sib, sibling)
+
+    def forward_level(t):
+        s = t * inner + pi
+
+        @pl.when(t != zo)
+        def _():
+            arrived(s, g_recv, mine)
+            for copy in forwards(t, s):
+                copy.start()
+            to_sibling(s).start()
+
+    def pass_level(t):
+        for q in around:
+            s = t * inner + q
+            arrived(s, g_recv, mine)
+            to_sibling(s).start()
+
+    def whole_shard(s):
+        @pl.when(s != me)
+        def _():
+            arrived(s, g_recv_sib, theirs)
+
+    def unpack(s):
+        flat[rows * s : rows * (s + 1), :] = buf[s, 0:rows, :]
+
+    vec_shards = range(VEC_AT // rows, (USED_ROWS - 1) // rows + 1)
+    early_shards = [s for s in range(wide) if s < first * inner or s in vec_shards]
+    late_shards = [s for s in range(wide) if s not in early_shards]
+
     for t in range(outer):
         forward_level(t)
 
@@ -657,16 +662,17 @@
     res[mine, :] = line
     last = remote(res.at[mine], res.at[mine], f_sem.at[0], f_sem.at[1], sibling)
     last.start()
+    slot = 2 * pi + core
+    near = [2 * q + core for q in around] + [2 * q + 1 - core for q in around] + [2 * pi + 1 - core]
+    sq_plane[slot] = rows8(line * line)
+    sq_sends = spread(sq_plane, slot, n_send, n_recv, 0, plane + cross + [sibling])
     vec = collected(vec_col, along, v_send, v_recv, 1 + inner)
     vec_at[VEC_AT:USED_ROWS, :] = vec
     remote(res.at[theirs], res.at[theirs], f_sem.at[0], f_sem.at[1], sibling).wait_recv()
-    full = res[...]
-    sq_plane[pi] = rows8(full * full)
-    sq_sends = spread(sq_plane, pi, n_send, n_recv, 0, plane)
-    own[...] = full[0:rows] + vec_at[pl.ds(me * rows, rows), :]
-    sq_col[zo] = collected(sq_plane, around, n_send, n_recv, 0)
-    sq_sends += spread(sq_col, zo, n_send, n_recv, inner, column)
-    both = collected(sq_col, along, n_send, n_recv, inner) + rows8(vec * vec)
+    own[...] = res[0:rows, :] + vec_at[pl.ds(me * rows, rows), :]
+    sq_col[zo] = collected(sq_plane, near, n_send, n_recv, 0)
+    sq_sends += spread(sq_col, zo, n_send, n_recv, 2 * inner, column)
+    both = collected(sq_col, along, n_send, n_recv, 2 * inner) + rows8(vec * vec)
     squares[...] = jnp.broadcast_to(jnp.sum(both, keepdims=True), squares.shape)
 
     for copy in own_pushes + vec_sends + sq_sends + [last]:
@@ -720,12 +726,12 @@
         + [vm((16, LANES), F32)] * 2
         + [vm((inner, 16, LANES), F32), vm((outer, 16, LANES), F32)]
         + [vm((wide * rows, LANES), F32)]
-        + [vm((inner, *tile), F32), vm((outer, *tile), F32)]
+        + [vm((2 * inner, *tile), F32), vm((outer, *tile), F32)]
         + [dma((4,)), dma((outer - 1,)), dma((outer, inner - 1)), dma((wide,)), dma((wide,)), dma((wide,))]
         + [dma((2, inner)), dma((2, inner)), dma((2, inner)), dma((2, inner))]
         + [dma((outer,)), dma((outer,)), dma((2,))]
         + [dma((1 + inner + outer,))] * 2
-        + [dma((inner + outer,))] * 2
+        + [dma((2 * inner + outer,))] * 2
     )
     anywhere, vmem = pl.BlockSpec(memory_space=pl.ANY), pl.BlockSpec(memory_space=pltpu.VMEM)
     return pl.pallas_call(
@@ -746,31 +752,112 @@
     )(x, dy, shard)
 
 
+def finish_kernel(*refs):
+    big_in, small_in = refs[0:2], refs[2:7]
+    big_out, norm_out, small_out = refs[7:9], refs[9], refs[10:15]
+    stages, ins, norm, outs = refs[15:17], refs[17:22], refs[22], refs[23:28]
+    sem_in, sem_out, sem_small = refs[28:31]
+    pieces = []
+    for k in range(2):
+        size = big_in[k].shape[0] // PIECES
+        for p in range(PIECES):
+            at = pl.ds(size * p, size)
+            pieces.append(
+                (
+                    pltpu.make_async_copy(big_in[k].at[at], stages[k].at[at], sem_in.at[k, p]),
+                    pltpu.make_async_copy(stages[k].at[at], big_out[k].at[at], sem_out.at[k, p]),
+                )
+            )
+    loads = [pltpu.make_async_copy(small_in[k], ins[k], sem_small.at[k]) for k in range(5)]
+    for copy in loads:
+        copy.start()
+    for come, _ in pieces:
+        come.start()
+    for copy in loads:
+        copy.wait()
+    own, squares, master, first, second = ins
+    clipped, new_master, new_copy, new_first, new_second = outs
+    grad_norm = jnp.sqrt(squares[...])
+    norm[...] = grad_norm[0:1, 0:1]
+    factor = jnp.minimum(1.0, 1.0 / (grad_norm[0:1, :] + 1e-06))
+    grad = own[...] * factor
+    clipped[...] = grad
+    one = 0.5 * first[...] + 0.5 * grad
+    two = 0.5 * second[...] + 0.5 * grad * grad
+    new_first[...] = one
+    new_second[...] = two
+    fixed = 1.0 - 0.5**STEP
+    old = master[...]
+    new = old - 0.05 * ((one / fixed) / (jnp.sqrt(two / fixed) + 1e-08) + 0.1 * old)
+    new_master[...] = new
+    new_copy[...] = new.astype(BF16)
+    stores = [
+        pltpu.make_async_copy(src, dst, sem_small.at[5 + k])
+        for k, (src, dst) in enumerate(zip((norm, *outs), (norm_out, *small_out)))
+    ]
+    for copy in stores:
+        copy.start()
+    for come, go in pieces:
+        come.wait()
+        go.start()
+    for copy in stores:
+        copy.wait()
+    for _, go in pieces:
+        go.wait()
+
+
+def finish(block_out, input_grad, owned, squares, master, first, second):
+    anywhere, vm = pl.BlockSpec(memory_space=pl.ANY), pltpu.VMEM
+    one, flat = (1, 1), owned.shape
+    kinds = [(flat, F32), (flat, F32), (flat, BF16), (flat, F32), (flat, F32)]
+    like = jax.ShapeDtypeStruct
+    return pl.pallas_call(
+        finish_kernel,
+        out_shape=(
+            like(block_out.shape, BF16),
+            like(input_grad.shape, F32),
+            like(one, F32),
+            *[like(*kind) for kind in kinds],
+        ),
+        in_specs=[anywhere] * 7,
+        out_specs=(anywhere,) * 8,
+        scratch_shapes=[
+            vm(block_out.shape, BF16),
+            vm(input_grad.shape, F32),
+            vm(flat, F32),
+            vm(squares.shape, F32),
+            vm(flat, F32),
+            vm(flat, F32),
+            vm(flat, F32),
+            vm(one, F32),
+            *[vm(*kind) for kind in kinds],
+            pltpu.SemaphoreType.DMA((2, PIECES)),
+            pltpu.SemaphoreType.DMA((2, PIECES)),
+            pltpu.SemaphoreType.DMA((11,)),
+        ],
+        compiler_params=pltpu.CompilerParams(vmem_limit_bytes=60 * 2**20),
+        name="finish",
+    )(block_out, input_grad, owned, squares, master, first, second)
+
+
 def on_device(inputs, cotangent, master, first, second):
-    rows = master.shape[0] // LANES
+    flat = lambda a: a.reshape(-1)
+    tall = lambda a: a.reshape(-1, LANES)
     block_out, input_grad, owned, squares = step(
-        inputs, cotangent, master.reshape(rows, LANES), lax.axis_size("wide")
+        inputs, cotangent, tall(master), lax.axis_size("wide")
     )
-    owned = owned.reshape(-1)
-    squares = squares[0, 0]
-    grad_norm = jnp.sqrt(squares)
-    factor = jnp.minimum(1.0, 1.0 / (grad_norm + 1e-06))
-    clipped = owned * factor
-    new_first = 0.5 * first + 0.5 * clipped
-    new_second = 0.5 * second + 0.5 * clipped * clipped
-    fixed = 1.0 - 0.5**STEP
-    new_master = master - 0.05 * (
-        new_first / fixed / (jnp.sqrt(new_second / fixed) + 1e-08) + 0.1 * master
+    block_out, input_grad, norm, clipped, new_master, new_copy, new_first, new_second = finish(
+        block_out, input_grad, owned, squares, tall(master), tall(first), tall(second)
     )
     return (
         block_out,
         input_grad,
-        clipped,
-        grad_norm,
-        new_master,
-        new_master.astype(jnp.bfloat16),
-        new_first,
-        new_second,
+        flat(clipped),
+        norm.reshape(()),
+        flat(new_master),
+        flat(new_copy),
+        flat(new_first),
+        flat(new_second),
     )
 
 

time: 76.6 us -> 71.4 us (0.932)
  local copies, waits for them, and re-layouts: 4.28 us -> 0 us
  Pallas kernels: 67.9 us -> 70.5 us
  between operations: 2.56 us -> 0.64 us
  other arithmetic: 1.62 us -> 0 us
    unnamed x10 -> x0, local copies, waits for them, and re-layouts: 3 us -> none
    pallas_call x0 -> x1, Pallas kernels: none -> 2.81 us  [finish(): pl.pallas_call(finish_kernel, out_shape=(like(block_out.shape, BF16), lik...]
    convert_element_type x1 -> x0, other arithmetic: 1.62 us -> none  [on_device(): new_master.astype(jnp.bfloat16)]
    slice x1 -> x0, local copies, waits for them, and re-layouts: 1.28 us -> none  [on_device(): squares = squares[0, 0]]
where the time goes in v4:
time: 71.4 us; the launch traced here: 71.2 us
  Pallas kernels  70.5 us (99%)
    pallas_call x1, Pallas kernels, step(): pl.pallas_call(functools.partial(step_kernel, wide), out_shape=(jax.Shape...  67.7 us
    pallas_call x1, Pallas kernels, finish(): pl.pallas_call(finish_kernel, out_shape=(like(block_out.shape, BF16), lik...  2.81 us

profile of v4, /device:TPU:0, one launch (start us, length us, event | category | flops | bytes accessed | tf_op | source)
XLA Modules:
  0.0 71.2 jit_solution(14783431851906174285)
XLA Ops:
  0.6 67.7 %step.1 = (bf16[48,6528]{1,0:T(8,128)(2,1)}, f32[48,6528]{1,0:T(8,128)}, f32[145,128]{1,0:T(8,128)}, f32[8,128]{1,0:T(8,128)}) custom-call(bf16[48,6528]{1,0:T(8,128)(2,1)} %x_hbm.1, bf16[48,6528]{1,0:T(8,128)(2,1)} %dy_hbm.1, f32[145,128]{1,0:T(8,128)} %bitcast.9), custom_call_target="tpu_custom_call" | custom-call | tf_op jit(solution)/shard_map/step/pallas_call | solution.py:737
  68.4 2.8 %finish.1 = (bf16[48,6528]{1,0:T(8,128)(2,1)}, f32[48,6528]{1,0:T(8,128)}, f32[1,1]{1,0:T(1,128)}, f32[145,128]{1,0:T(8,128)}, f32[145,128]{1,0:T(8,128)}, /*ind...) custom-call(bf16[48,6528]{1,0:T(8,128)(2,1)} %get-tuple-element.20.refs_0_, ...), custom_call_target="tpu_custom_call" | custom-call | tf_op jit(solution)/shard_map/finish/pallas_call | solution.py:814

commit v5 on v4

--- a/solution.py
+++ b/solution.py
@@ -28,6 +28,7 @@
 PIECES = 1
 VEC_AT = 2304
 USED_ROWS = VEC_AT + 16
+QK_ROWS = 576
 QKV_ROWS = 864
 GELU_C = math.sqrt(2.0 / math.pi)
 
@@ -143,11 +144,11 @@
     x_hbm, dy_hbm, shard, out_hbm, ig_hbm, own, squares,
     x_ref, dy_ref, out_ref, ig_ref, flat, gflat,
     qs, ks, vs, os_, kbd, vbd, psc, xh1, r1, dx2s, h, h2, z, dul, o_t, dal, dyt, dqkv,
-    wq, wk, wv, wo, w1, w2, tmp, hm2, hm, acc, acc2, acc3,
+    wq, wk, wv, wo, w1, w2, tmp, hm2, acc, acc2, acc3,
     buf, parts, sib_in, plane_in, out_p, col_in, out_c, res, vec_own, vec_sib, vec_plane, vec_col,
-    vec_at, sq_plane, sq_col,
+    vec_at, sq_plane, sq_col, vec_in,
     io_sem, g_col, g_fw, g_sib, g_recv, g_recv_sib, s_send, s_recv, p_send, p_recv, c_send, c_recv,
-    f_sem, v_send, v_recv, n_send, n_recv,
+    f_sem, v_send, v_recv, n_send, n_recv, vg_send, vg_recv,
 ):
     n = x_ref.shape[0]
     toks = n * SEQ
@@ -165,7 +166,9 @@
     along = [lax.rem(zo + k, outer) for k in range(1, outer)]
     plane = [(zo * inner + q, core) for q in around]
     column = [(t * inner + pi, core) for t in along]
+    late = -(-QK_ROWS // (rows * inner))
     first = -(-QKV_ROWS // (rows * inner))
+    bounds = ((first, outer), (late, first), (0, late))
 
     copies_in = [
         pltpu.make_async_copy(x_hbm, x_ref, io_sem.at[0]),
@@ -184,11 +187,6 @@
         hm2[80 * p : 80 * (p + 1), :] = jnp.where(
             (lane >= lo) & (lane < lo + HEAD_DIM), 1.0, 0.0
         ).astype(BF16)
-    lane16 = lax.broadcasted_iota(jnp.int32, (16, 256), 1)
-    for k in range(HEADS):
-        hm[16 * k : 16 * (k + 1), :] = jnp.where(
-            (lane16 >= HEAD_DIM * k) & (lane16 < HEAD_DIM * (k + 1)), 1.0, 0.0
-        ).astype(BF16)
     ones_lane = (lax.broadcasted_iota(jnp.int32, (toks, 64), 1) == 0).astype(F32).astype(BF16)
     for ref in (h, h2, o_t):
         ref[:, D:256] = ones_lane
@@ -209,6 +207,27 @@
 
     def forwards(t, s):
         return [push(s, g_fw.at[t, k], g_recv, where) for k, where in enumerate(plane)]
+
+    vec_rows = [
+        (s, max(0, VEC_AT - rows * s) // 8 * 8, max(0, VEC_AT - rows * s), min(rows, USED_ROWS - rows * s))
+        for s in range(VEC_AT // rows, (USED_ROWS - 1) // rows + 1)
+    ]
+
+    def vec_push(j, where, base):
+        return [
+            remote(vec_in.at[j], vec_in.at[j], vg_send.at[j, base + k], vg_recv.at[j], dev)
+            for k, dev in enumerate(where)
+        ]
+
+    def vec_arrived(j):
+        remote(vec_in.at[j], vec_in.at[j], vg_send.at[j, 0], vg_recv.at[j], sibling).wait_recv()
+
+    for j, (s, a0, _, end) in enumerate(vec_rows):
+        @pl.when(me == s)
+        def _(j=j, a0=a0, end=end):
+            vec_in[j, 0 : end - a0, :] = shard[a0:end, :]
+            for copy in vec_push(j, column, 0) + vec_push(j, plane, outer - 1):
+                copy.start()
 
     own_pushes = [push(me, g_col.at[k], g_recv, where) for k, where in enumerate(column)]
     own_pushes += forwards(zo, me)
@@ -242,9 +261,12 @@
     def unpack(s):
         flat[rows * s : rows * (s + 1), :] = buf[s, 0:rows, :]
 
-    vec_shards = range(VEC_AT // rows, (USED_ROWS - 1) // rows + 1)
-    early_shards = [s for s in range(wide) if s < first * inner or s in vec_shards]
-    late_shards = [s for s in range(wide) if s not in early_shards]
+    for j, (s, _, _, _) in enumerate(vec_rows):
+        @pl.when((me != s) & (pi == s % inner))
+        def _(j=j):
+            vec_arrived(j)
+            for copy in vec_push(j, plane, outer - 1):
+                copy.start()
 
     for t in range(outer):
         forward_level(t)
@@ -306,12 +328,15 @@
 
     for t in range(first):
         pass_level(t)
-    for t in range(first, outer):
-        if any(s // inner == t for s in vec_shards):
-            pass_level(t)
-    for s in early_shards:
+    for s in range(first * inner):
         whole_shard(s)
         unpack(s)
+    for j, (s, a0, begin, end) in enumerate(vec_rows):
+        @pl.when(pi != s % inner)
+        def _(j=j):
+            vec_arrived(j)
+
+        flat[rows * s + begin : rows * s + end, :] = vec_in[j, begin - a0 : end - a0, :]
     for (base, count), ref in zip(MATS[0:3], (wq, wk, wv)):
         load_square(flat, base, count, tmp, ref)
 
@@ -351,8 +376,7 @@
         @pl.when(i == 1)
         def _():
             for t in range(first, outer):
-                if not any(s // inner == t for s in vec_shards):
-                    pass_level(t)
+                pass_level(t)
 
         r0 = pl.multiple_of(i * (LOCK1 * GROWS), 8)
         base0 = pl.multiple_of(i * (LOCK1 * 3 * HJ), 64)
@@ -388,7 +412,7 @@
 
     lax.fori_loop(0, groups // LOCK1, attn, 0)
 
-    for s in late_shards:
+    for s in range(first * inner, wide):
         whole_shard(s)
         unpack(s)
     for (base, count), ref in zip(MATS[3:5], (wo, w2)):
@@ -441,26 +465,24 @@
     def total(v):
         return jnp.sum(v, 0, keepdims=True)
 
-    def over_tokens(acc, a, b):
-        acc[...] = jnp.zeros(acc.shape, F32)
-        steps = DW_STEPS
-        size = toks // steps
-
-        @pl.loop(0, steps)
+    def over_tokens(*products):
+        for acc, _, _ in products:
+            acc[...] = jnp.zeros(acc.shape, F32)
+        size = toks // DW_STEPS
+
+        @pl.loop(0, DW_STEPS)
         def _(i):
             at = pl.ds(pl.multiple_of(i * size, 16), size)
-            acc[...] += tn(a[at, :], b[at, :])
-
-        return acc[...]
-
-    store_square(over_tokens(acc, z, dyt), gflat, 1920, FF, tmp)
-    dw1 = over_tokens(acc2, h2, dul)
+            for acc, a, b in products:
+                acc[...] += tn(a[at, :], b[at, :])
+
+    over_tokens((acc, z, dyt), (acc2, h2, dul), (acc3, o_t, dal))
+    store_square(acc[...], gflat, 1920, FF, tmp)
     for c in range(4):
-        gflat[pl.ds(W1_AT + c, D, stride=4), :] = dw1[0:D, 128 * c : 128 * (c + 1)]
-        vec_own[12 + c : 13 + c, :] = dw1[D : D + 1, 128 * c : 128 * (c + 1)]
-    dwo = over_tokens(acc, o_t, dal)
-    store_square(dwo, gflat, 864, D, tmp)
-    dbo = dwo[D : D + 1]
+        gflat[pl.ds(W1_AT + c, D, stride=4), :] = acc2[0:D, 128 * c : 128 * (c + 1)]
+        vec_own[12 + c : 13 + c, :] = acc2[D : D + 1, 128 * c : 128 * (c + 1)]
+    store_square(acc3[...], gflat, 864, D, tmp)
+    dbo = acc3[D : D + 1, :]
 
     def pack(lo, hi):
         for s in range(lo * inner, hi * inner):
@@ -493,7 +515,8 @@
             out_c.at[t], col_in.at[zo], c_send.at[t], c_recv.at[zo], (t * inner + pi, core)
         )
 
-    def sum_cores(part, lo, hi):
+    def sum_cores(part):
+        lo, hi = bounds[part]
         sends = plane_copies(part, lo, hi)
         for k, q in enumerate(places):
             remote(
@@ -507,7 +530,8 @@
             else:
                 plane_in[pi, lo:hi] = both
 
-    def sum_plane(part, lo, hi):
+    def sum_plane(part):
+        lo, hi = bounds[part]
         for k, q in enumerate(around):
             remote(
                 plane_in.at[q, lo:hi], plane_in.at[q, lo:hi],
@@ -523,36 +547,75 @@
             def _():
                 col_copy(t).start()
 
-    pack(first, outer)
-    for copy in sib_copies(0, first, outer):
-        copy.start()
-
-    def wide_rows(v):
-        blocks = []
-        for k in range(HEADS):
-            one = v[k]
-            parts = [
-                jnp.where((lane3 >= ROWS * b) & (lane3 < ROWS * (b + 1)), one, 0.0)
+    def send_cores(part):
+        pack(*bounds[part])
+        for copy in sib_copies(part, *bounds[part]):
+            copy.start()
+
+    send_cores(0)
+
+    def by_sample(v):
+        return jnp.concatenate(
+            [
+                jnp.where((lane3 >= ROWS * b) & (lane3 < ROWS * (b + 1)), v, 0.0).reshape(HJ, LANES)
                 for b in range(GROUP)
-            ]
-            parts.append(jnp.zeros((8, LANES), F32))
-            blocks.append(jnp.concatenate(parts, 0).astype(BF16))
-        return jnp.concatenate(blocks, 1)
-
-    def masked(v):
-        v3 = v.reshape(8, 16, 256)
-        return jnp.concatenate(
-            [(v3 * hm[16 * k : 16 * (k + 1), :][None]).reshape(128, 256) for k in range(HEADS)], 0
-        )
+            ],
+            0,
+        ).astype(BF16)
+
+    def own_lanes(v):
+        v = v.reshape(GROUP, HEADS, ROWS, 256)
+        out = []
+        for b in range(GROUP):
+            lo, hi = v[b, 0, :, 0:128], v[b, 5, :, 128:256]
+            for k in range(1, 6):
+                lo = jnp.where(lane3 >= HEAD_DIM * k, v[b, k, :, 0:128], lo)
+            for k in range(6, HEADS):
+                hi = jnp.where(lane3 >= HEAD_DIM * k - 128, v[b, k, :, 128:256], hi)
+            out.append(jnp.concatenate([lo, hi], 1))
+        return jnp.concatenate(out, 0)
+
+    def probs(at):
+        return psc[pl.ds(at, HJ), :].reshape(HEADS, ROWS, LANES)
+
+    def attn_back_v(i, carry):
+        @pl.when(i == 2)
+        def _():
+            sum_cores(0)
+
+        r0 = pl.multiple_of(i * (LOCK2 * GROWS), 8)
+        p0 = pl.multiple_of(i * (LOCK2 * HJ), 64)
+        for k in range(LOCK2):
+            dg = get_rows(os_, r0 + GROWS * k, LANES).astype(BF16)
+            dv = own_lanes(nn(by_sample(probs(p0 + HJ * k)), dg))
+            put_rows(vs, r0 + GROWS * k, dv.astype(BF16).astype(F32))
+        return carry
+
+    lax.fori_loop(0, groups // LOCK2, attn_back_v, 0)
+
+    def collect(refs):
+        def chunk(t0, count, carry):
+            at = rows_at(t0, count)
+            for k, ref in refs:
+                dqkv[at, 256 * k : 256 * (k + 1)] = get_tokens(ref, t0, count).astype(BF16)
+            return carry
+
+        over_token_chunks(chunk, WIDTH3, 0)
+
+    collect([(2, vs)])
+    over_tokens((acc, h, dqkv.at[:, 512:768]))
+    store_square(acc[...], gflat, 576, D, tmp)
+    dbv = acc[D : D + 1, :]
+    send_cores(1)
 
     def attn_back(i, carry):
         @pl.when(i == 1)
         def _():
-            sum_cores(0, first, outer)
+            sum_cores(1)
 
         @pl.when(i == 3)
         def _():
-            sum_plane(0, first, outer)
+            sum_plane(0)
 
         r0 = pl.multiple_of(i * (LOCK2 * GROWS), 8)
         base0 = pl.multiple_of(i * (LOCK2 * 3 * HJ), 64)
@@ -561,12 +624,11 @@
         qg = [get_rows(qs, r0 + GROWS * k, LANES).astype(BF16) for k in sets]
         dg = [get_rows(os_, r0 + GROWS * k, LANES).astype(BF16) for k in sets]
         dp = [squeeze(nt(vbd[pl.ds(base0 + 3 * HJ * k, 3 * HJ), :], dg[k])) for k in sets]
-        p = [psc[pl.ds(p0 + HJ * k, HJ), :].reshape(HEADS, ROWS, LANES) for k in sets]
+        p = [probs(p0 + HJ * k) for k in sets]
         t = [jnp.sum(p[k] * dp[k], 1, keepdims=True) for k in sets]
         ds = [p[k] * (dp[k] - t[k]) for k in sets]
         dst = [v.reshape(HJ, LANES).T for v in ds]
-        dv = [nn(wide_rows(p[k]), masked(dg[k])) for k in sets]
-        dk = [nn(wide_rows(ds[k]), masked(qg[k])) * scale for k in sets]
+        dk = [own_lanes(nn(by_sample(ds[k]), qg[k])) * scale for k in sets]
         for b in range(GROUP):
             for k in sets:
                 dq = nn(
@@ -575,26 +637,16 @@
                 )
                 put_rows(qs, r0 + GROWS * k + ROWS * b, (dq * scale).astype(BF16).astype(F32))
         for k in sets:
-            put_rows(vs, r0 + GROWS * k, dv[k].astype(BF16).astype(F32)[0:GROWS])
-            put_rows(ks, r0 + GROWS * k, dk[k].astype(BF16).astype(F32)[0:GROWS])
+            put_rows(ks, r0 + GROWS * k, dk[k].astype(BF16).astype(F32))
         return carry
 
     lax.fori_loop(0, groups // LOCK2, attn_back, 0)
 
-    def collect(t0, count, carry):
-        at = rows_at(t0, count)
-        dqkv[at, :] = jnp.concatenate(
-            [get_tokens(ref, t0, count).astype(BF16) for ref in (qs, ks, vs)], 1
-        )
-        return carry
-
-    over_token_chunks(collect, WIDTH3, 0)
-    dw = over_tokens(acc3, h, dqkv)
-    for k in range(3):
-        store_square(dw[:, 256 * k : 256 * (k + 1)], gflat, 288 * k, D, tmp)
-    pack(0, first)
-    for copy in sib_copies(1, 0, first):
-        copy.start()
+    collect([(0, qs), (1, ks)])
+    over_tokens((acc2, h, dqkv.at[:, 0:512]))
+    for k in range(2):
+        store_square(acc2[:, 256 * k : 256 * (k + 1)], gflat, 288 * k, D, tmp)
+    send_cores(2)
 
     def dense3(t0, count, carry):
         dg1, dn1 = carry
@@ -612,12 +664,13 @@
     def hook3(i):
         @pl.when(i == 1)
         def _():
-            sum_cores(1, 0, first)
+            sum_cores(2)
+            sum_plane(1)
 
     dg1, dn1 = over_token_chunks(dense3, WIDTH3, (zero, zero), hook3)
 
     vecs = [
-        total(dg1), total(dn1), dw[D : D + 1, 0:256], dw[D : D + 1, 512:768],
+        total(dg1), total(dn1), acc2[D : D + 1, 0:256], dbv,
         dbo, total(dg2), total(dn2), total(db2),
     ]
     for k in range(4):
@@ -649,7 +702,7 @@
     remote(vec_sib, vec_sib, v_send.at[0], v_recv.at[0], sibling).wait_recv()
     vec_plane[pi] = vec_own[...] + vec_sib[...]
     vec_sends += spread(vec_plane, pi, v_send, v_recv, 1, plane)
-    sum_plane(1, 0, first)
+    sum_plane(2)
     vec_col[zo] = collected(vec_plane, around, v_send, v_recv, 1)
     vec_sends += spread(vec_col, zo, v_send, v_recv, 1 + inner, column)
 
@@ -687,7 +740,18 @@
 
         for q in around:
             to_sibling(t * inner + q).wait_send()
-    for part, lo, hi in ((0, first, outer), (1, 0, first)):
+    for j, (s, _, _, _) in enumerate(vec_rows):
+        @pl.when(me == s)
+        def _(j=j):
+            for copy in vec_push(j, column, 0):
+                copy.wait_send()
+
+        @pl.when(pi == s % inner)
+        def _(j=j):
+            for copy in vec_push(j, plane, outer - 1):
+                copy.wait_send()
+
+    for part, (lo, hi) in enumerate(bounds):
         for copy in sib_copies(part, lo, hi) + plane_copies(part, lo, hi):
             copy.wait_send()
     copy_out.wait()
@@ -701,6 +765,7 @@
     groups = n // GROUP
     padded = (rows + 15) // 16 * 16
     half = padded // 2
+    vecs = (USED_ROWS - 1) // rows - VEC_AT // rows + 1
     vm, dma = pltpu.VMEM, pltpu.SemaphoreType.DMA
     sm = vm((2, n * ROWS + 8, LANES), F32)
     tok = vm((toks, 256), BF16)
@@ -716,8 +781,8 @@
         + [tok, tok, vm((toks, 3 * 256), BF16)]
         + [vm((256, 256), BF16)] * 4
         + [vm((256, 2 * FF), BF16), vm((FF, 256), BF16), vm((2, FF, 128), F32)]
-        + [vm((320, 256), BF16), vm((128, 256), BF16)]
-        + [vm((256, 256), F32), vm((256, 512), F32), vm((256, 768), F32)]
+        + [vm((320, 256), BF16)]
+        + [vm((256, 256), F32), vm((256, 512), F32), vm((256, 256), F32)]
         + [vm((wide, padded, LANES), F32), vm((outer, inner, padded, LANES), F32)]
         + [vm((outer, inner, half, LANES), F32), vm((inner, outer, half, LANES), F32)]
         + [vm((inner - 1, outer, half, LANES), F32)]
@@ -727,11 +792,13 @@
         + [vm((inner, 16, LANES), F32), vm((outer, 16, LANES), F32)]
         + [vm((wide * rows, LANES), F32)]
         + [vm((2 * inner, *tile), F32), vm((outer, *tile), F32)]
+        + [vm((vecs, min(24, padded), LANES), F32)]
         + [dma((4,)), dma((outer - 1,)), dma((outer, inner - 1)), dma((wide,)), dma((wide,)), dma((wide,))]
-        + [dma((2, inner)), dma((2, inner)), dma((2, inner)), dma((2, inner))]
+        + [dma((3, inner))] * 4
         + [dma((outer,)), dma((outer,)), dma((2,))]
         + [dma((1 + inner + outer,))] * 2
         + [dma((2 * inner + outer,))] * 2
+        + [dma((vecs, outer + inner - 2)), dma((vecs,))]
     )
     anywhere, vmem = pl.BlockSpec(memory_space=pl.ANY), pl.BlockSpec(memory_space=pltpu.VMEM)
     return pl.pallas_call(

time: 71.4 us -> 67 us (0.938)
  Pallas kernels: 70.5 us -> 66.1 us
    pallas_call x1, Pallas kernels: 67.7 us -> 63.3 us  [step(): pl.pallas_call(functools.partial(step_kernel, wide), out_shape=(jax.Shape...]
where the time goes in v5:
time: 67 us; the launch traced here: 66.8 us
  Pallas kernels  66.1 us (99%)
    pallas_call x1, Pallas kernels, step(): pl.pallas_call(functools.partial(step_kernel, wide), out_shape=(jax.Shape...  63.3 us
    pallas_call x1, Pallas kernels, finish(): pl.pallas_call(finish_kernel, out_shape=(like(block_out.shape, BF16), lik...  2.81 us

profile of v5, /device:TPU:0, one launch (start us, length us, event | category | flops | bytes accessed | tf_op | source)
XLA Modules:
  0.0 66.8 jit_solution(13142606691746082936)
XLA Ops:
  0.6 63.3 %step.1 = (bf16[48,6528]{1,0:T(8,128)(2,1)}, f32[48,6528]{1,0:T(8,128)}, f32[145,128]{1,0:T(8,128)}, f32[8,128]{1,0:T(8,128)}) custom-call(bf16[48,6528]{1,0:T(8,128)(2,1)} %x_hbm.1, bf16[48,6528]{1,0:T(8,128)(2,1)} %dy_hbm.1, f32[145,128]{1,0:T(8,128)} %bitcast.9), custom_call_target="tpu_custom_call" | custom-call | tf_op jit(solution)/shard_map/step/pallas_call | solution.py:804
  64.0 2.8 %finish.1 = (bf16[48,6528]{1,0:T(8,128)(2,1)}, f32[48,6528]{1,0:T(8,128)}, f32[1,1]{1,0:T(1,128)}, f32[145,128]{1,0:T(8,128)}, f32[145,128]{1,0:T(8,128)}, /*ind...) custom-call(bf16[48,6528]{1,0:T(8,128)(2,1)} %get-tuple-element.20.refs_0_, ...), custom_call_target="tpu_custom_call" | custom-call | tf_op jit(solution)/shard_map/finish/pallas_call | solution.py:881

commit v6 on v5

--- a/solution.py
+++ b/solution.py
@@ -17,7 +17,9 @@
 ROWS = 40
 GROUP = 3
 GROWS = GROUP * ROWS
-HJ = HEADS * ROWS
+PAIRS = HEADS // 2
+PAIR_DIM = 2 * HEAD_DIM
+HJ = PAIRS * ROWS
 LANES = 128
 F32 = jnp.float32
 BF16 = jnp.bfloat16
@@ -144,7 +146,7 @@
     x_hbm, dy_hbm, shard, out_hbm, ig_hbm, own, squares,
     x_ref, dy_ref, out_ref, ig_ref, flat, gflat,
     qs, ks, vs, os_, kbd, vbd, psc, xh1, r1, dx2s, h, h2, z, dul, o_t, dal, dyt, dqkv,
-    wq, wk, wv, wo, w1, w2, tmp, hm2, acc, acc2, acc3,
+    wq, wk, wv, wo, w1, w2, tmp, hm2, parity, acc, acc2, acc3,
     buf, parts, sib_in, plane_in, out_p, col_in, out_c, res, vec_own, vec_sib, vec_plane, vec_col,
     vec_at, sq_plane, sq_col, vec_in,
     io_sem, g_col, g_fw, g_sib, g_recv, g_recv_sib, s_send, s_recv, p_send, p_recv, c_send, c_recv,
@@ -182,10 +184,15 @@
     greet(known)
     lane = lax.broadcasted_iota(jnp.int32, (80, 256), 1)
     row = lax.broadcasted_iota(jnp.int32, (80, 256), 0)
-    for p in range(4):
-        lo = jnp.where(row < ROWS, HEAD_DIM * 2 * p, HEAD_DIM * (2 * p + 1))
+    for p in range(PAIRS // 2):
+        lo = jnp.where(row < ROWS, PAIR_DIM * 2 * p, PAIR_DIM * (2 * p + 1))
         hm2[80 * p : 80 * (p + 1), :] = jnp.where(
-            (lane >= lo) & (lane < lo + HEAD_DIM), 1.0, 0.0
+            (lane >= lo) & (lane < lo + PAIR_DIM), 1.0, 0.0
+        ).astype(BF16)
+    head = lax.broadcasted_iota(jnp.int32, (16, 256), 1) // HEAD_DIM
+    for k in range(2):
+        parity[16 * k : 16 * (k + 1), :] = jnp.where(
+            (lax.rem(head, 2) == k) & (head < HEADS), 1.0, 0.0
         ).astype(BF16)
     ones_lane = (lax.broadcasted_iota(jnp.int32, (toks, 64), 1) == 0).astype(F32).astype(BF16)
     for ref in (h, h2, o_t):
@@ -361,14 +368,26 @@
 
     over_token_chunks(dense1, WIDTH1, 0)
 
-    lane3 = lax.broadcasted_iota(jnp.int32, (1, LANES), 1)
+    lane3 = lax.rem(lax.broadcasted_iota(jnp.int32, (1, 256), 1), LANES)
+    odd_head = lax.rem(lax.broadcasted_iota(jnp.int32, (1, 256), 1) // HEAD_DIM, 2) == 1
 
     def squeeze(v):
         return jnp.where(
             lane3 < ROWS, v[0:HJ], jnp.where(lane3 < 2 * ROWS, v[HJ : 2 * HJ], v[2 * HJ : 3 * HJ])
-        ).reshape(HEADS, ROWS, LANES)
-
-    jrow = lax.broadcasted_iota(jnp.int32, (1, ROWS, LANES), 1)
+        ).reshape(PAIRS, ROWS, 256)
+
+    def by_parity(v):
+        v3 = v.reshape(8, 16, 256)
+        return jnp.concatenate(
+            [(v3 * parity[16 * k : 16 * (k + 1), :][None]).reshape(LANES, 256) for k in range(2)], 0
+        )
+
+    def per_query(left, right, b):
+        rows2 = jnp.concatenate([left[128 * k + ROWS * b : 128 * k + ROWS * (b + 1)] for k in range(2)], 0)
+        both = nn(rows2.astype(BF16), right)
+        return jnp.where(odd_head, both[ROWS : 2 * ROWS], both[0:ROWS])
+
+    jrow = lax.broadcasted_iota(jnp.int32, (1, ROWS, 256), 1)
     cexp = math.log2(math.e) / math.sqrt(HEAD_DIM)
     scale = 1.0 / math.sqrt(HEAD_DIM)
 
@@ -379,16 +398,16 @@
                 pass_level(t)
 
         r0 = pl.multiple_of(i * (LOCK1 * GROWS), 8)
-        base0 = pl.multiple_of(i * (LOCK1 * 3 * HJ), 64)
-        p0 = pl.multiple_of(i * (LOCK1 * HJ), 64)
+        base0 = pl.multiple_of(i * (LOCK1 * 3 * HJ), 32)
+        p0 = pl.multiple_of(i * (LOCK1 * HJ), 32)
         sets = range(LOCK1)
-        qg = [get_rows(qs, r0 + GROWS * k, LANES).astype(BF16) for k in sets]
+        qg = [by_parity(get_rows(qs, r0 + GROWS * k, LANES).astype(BF16)) for k in sets]
         for k in sets:
             for src, dst in ((ks, kbd), (vs, vbd)):
                 for b in range(GROUP):
                     one = get_rows(src, r0 + GROWS * k + ROWS * b, ROWS)
                     two = jnp.concatenate([one, one], 0).astype(BF16)
-                    for p in range(4):
+                    for p in range(PAIRS // 2):
                         dst[pl.ds(base0 + HJ * (3 * k + b) + 80 * p, 80), :] = (
                             two * hm2[80 * p : 80 * (p + 1), :]
                         )
@@ -397,16 +416,13 @@
         m = [jnp.max(v, 1, keepdims=True) for v in st]
         e = [jnp.exp2((st[k] - m[k]) * cexp) for k in sets]
         l = [1.0 / jnp.sum(v, 1, keepdims=True) for v in e]
-        p = [(e[k] * l[k]).reshape(HJ, LANES) for k in sets]
+        p = [(e[k] * l[k]).reshape(HJ, 256) for k in sets]
         for k in sets:
             psc[pl.ds(p0 + HJ * k, HJ), :] = p[k]
         pt = [v.T for v in p]
         for b in range(GROUP):
             for k in sets:
-                ob = nn(
-                    pt[k][ROWS * b : ROWS * (b + 1), :].astype(BF16),
-                    vbd[pl.ds(base0 + HJ * (3 * k + b), HJ), :],
-                )
+                ob = per_query(pt[k], vbd[pl.ds(base0 + HJ * (3 * k + b), HJ), :], b)
                 put_rows(os_, r0 + GROWS * k + ROWS * b, ob.astype(BF16).astype(F32)[0:SEQ])
         return carry
 
@@ -557,26 +573,28 @@
     def by_sample(v):
         return jnp.concatenate(
             [
-                jnp.where((lane3 >= ROWS * b) & (lane3 < ROWS * (b + 1)), v, 0.0).reshape(HJ, LANES)
+                jnp.where((lane3 >= ROWS * b) & (lane3 < ROWS * (b + 1)), v, 0.0).reshape(HJ, 256)
                 for b in range(GROUP)
             ],
             0,
         ).astype(BF16)
 
+    pair_lane = lax.broadcasted_iota(jnp.int32, (1, LANES), 1)
+
     def own_lanes(v):
-        v = v.reshape(GROUP, HEADS, ROWS, 256)
+        v = v.reshape(GROUP, PAIRS, ROWS, 256)
         out = []
         for b in range(GROUP):
-            lo, hi = v[b, 0, :, 0:128], v[b, 5, :, 128:256]
-            for k in range(1, 6):
-                lo = jnp.where(lane3 >= HEAD_DIM * k, v[b, k, :, 0:128], lo)
-            for k in range(6, HEADS):
-                hi = jnp.where(lane3 >= HEAD_DIM * k - 128, v[b, k, :, 128:256], hi)
+            lo = jnp.where(pair_lane < PAIR_DIM, v[b, 0, :, 0:128], v[b, 1, :, 0:128])
+            lo = jnp.where(pair_lane < 2 * PAIR_DIM, lo, v[b, 2, :, 0:128])
+            hi = jnp.where(
+                pair_lane < 3 * PAIR_DIM - 128, v[b, 2, :, 128:256], v[b, 3, :, 128:256]
+            )
             out.append(jnp.concatenate([lo, hi], 1))
         return jnp.concatenate(out, 0)
 
     def probs(at):
-        return psc[pl.ds(at, HJ), :].reshape(HEADS, ROWS, LANES)
+        return psc[pl.ds(at, HJ), :].reshape(PAIRS, ROWS, 256)
 
     def attn_back_v(i, carry):
         @pl.when(i == 2)
@@ -584,9 +602,9 @@
             sum_cores(0)
 
         r0 = pl.multiple_of(i * (LOCK2 * GROWS), 8)
-        p0 = pl.multiple_of(i * (LOCK2 * HJ), 64)
+        p0 = pl.multiple_of(i * (LOCK2 * HJ), 32)
         for k in range(LOCK2):
-            dg = get_rows(os_, r0 + GROWS * k, LANES).astype(BF16)
+            dg = by_parity(get_rows(os_, r0 + GROWS * k, LANES).astype(BF16))
             dv = own_lanes(nn(by_sample(probs(p0 + HJ * k)), dg))
             put_rows(vs, r0 + GROWS * k, dv.astype(BF16).astype(F32))
         return carry
@@ -618,23 +636,20 @@
             sum_plane(0)
 
         r0 = pl.multiple_of(i * (LOCK2 * GROWS), 8)
-        base0 = pl.multiple_of(i * (LOCK2 * 3 * HJ), 64)
-        p0 = pl.multiple_of(i * (LOCK2 * HJ), 64)
+        base0 = pl.multiple_of(i * (LOCK2 * 3 * HJ), 32)
+        p0 = pl.multiple_of(i * (LOCK2 * HJ), 32)
         sets = range(LOCK2)
-        qg = [get_rows(qs, r0 + GROWS * k, LANES).astype(BF16) for k in sets]
-        dg = [get_rows(os_, r0 + GROWS * k, LANES).astype(BF16) for k in sets]
+        qg = [by_parity(get_rows(qs, r0 + GROWS * k, LANES).astype(BF16)) for k in sets]
+        dg = [by_parity(get_rows(os_, r0 + GROWS * k, LANES).astype(BF16)) for k in sets]
         dp = [squeeze(nt(vbd[pl.ds(base0 + 3 * HJ * k, 3 * HJ), :], dg[k])) for k in sets]
         p = [probs(p0 + HJ * k) for k in sets]
         t = [jnp.sum(p[k] * dp[k], 1, keepdims=True) for k in sets]
         ds = [p[k] * (dp[k] - t[k]) for k in sets]
-        dst = [v.reshape(HJ, LANES).T for v in ds]
+        dst = [v.reshape(HJ, 256).T for v in ds]
         dk = [own_lanes(nn(by_sample(ds[k]), qg[k])) * scale for k in sets]
         for b in range(GROUP):
             for k in sets:
-                dq = nn(
-                    dst[k][ROWS * b : ROWS * (b + 1), :].astype(BF16),
-                    kbd[pl.ds(base0 + HJ * (3 * k + b), HJ), :],
-                )
+                dq = per_query(dst[k], kbd[pl.ds(base0 + HJ * (3 * k + b), HJ), :], b)
                 put_rows(qs, r0 + GROWS * k + ROWS * b, (dq * scale).astype(BF16).astype(F32))
         for k in sets:
             put_rows(ks, r0 + GROWS * k, dk[k].astype(BF16).astype(F32))
@@ -775,13 +790,13 @@
         + [vm((wide * rows, LANES), F32)] * 2
         + [sm] * 4
         + [vm((groups * 3 * HJ, 256), BF16)] * 2
-        + [vm((groups * HJ, LANES), F32)]
+        + [vm((groups * HJ, 256), F32)]
         + [vm((toks, 256), F32), vm((toks, 1), F32), vm((toks, 256), F32)]
         + [tok, tok, tok, vm((toks, 2 * FF), BF16), tok]
         + [tok, tok, vm((toks, 3 * 256), BF16)]
         + [vm((256, 256), BF16)] * 4
         + [vm((256, 2 * FF), BF16), vm((FF, 256), BF16), vm((2, FF, 128), F32)]
-        + [vm((320, 256), BF16)]
+        + [vm((HJ, 256), BF16), vm((32, 256), BF16)]
         + [vm((256, 256), F32), vm((256, 512), F32), vm((256, 256), F32)]
         + [vm((wide, padded, LANES), F32), vm((outer, inner, padded, LANES), F32)]
         + [vm((outer, inner, half, LANES), F32), vm((inner, outer, half, LANES), F32)]

time: 67 us -> 63.1 us (0.942)
  Pallas kernels: 66.1 us -> 62.2 us
    pallas_call x1, Pallas kernels: 63.3 us -> 59.4 us  [step(): pl.pallas_call(functools.partial(step_kernel, wide), out_shape=(jax.Shape...]
where the time goes in v6:
time: 63.1 us; the launch traced here: 62.9 us
  Pallas kernels  62.2 us (99%)
  between operations  0.64 us (1%)
    pallas_call x1, Pallas kernels, step(): pl.pallas_call(functools.partial(step_kernel, wide), out_shape=(jax.Shape...  59.4 us
    pallas_call x1, Pallas kernels, finish(): pl.pallas_call(finish_kernel, out_shape=(like(block_out.shape, BF16), lik...  2.81 us

profile of v6, /device:TPU:0, one launch (start us, length us, event | category | flops | bytes accessed | tf_op | source)
XLA Modules:
  0.0 62.9 jit_solution(7727029637205835922)
XLA Ops:
  0.6 59.4 %step.1 = (bf16[48,6528]{1,0:T(8,128)(2,1)}, f32[48,6528]{1,0:T(8,128)}, f32[145,128]{1,0:T(8,128)}, f32[8,128]{1,0:T(8,128)}) custom-call(bf16[48,6528]{1,0:T(8,128)(2,1)} %x_hbm.1, bf16[48,6528]{1,0:T(8,128)(2,1)} %dy_hbm.1, f32[145,128]{1,0:T(8,128)} %bitcast.9), custom_call_target="tpu_custom_call" | custom-call | tf_op jit(solution)/shard_map/step/pallas_call | solution.py:819
  60.1 2.8 %finish.1 = (bf16[48,6528]{1,0:T(8,128)(2,1)}, f32[48,6528]{1,0:T(8,128)}, f32[1,1]{1,0:T(1,128)}, f32[145,128]{1,0:T(8,128)}, f32[145,128]{1,0:T(8,128)}, /*ind...) custom-call(bf16[48,6528]{1,0:T(8,128)(2,1)} %get-tuple-element.20.refs_0_, ...), custom_call_target="tpu_custom_call" | custom-call | tf_op jit(solution)/shard_map/finish/pallas_call | solution.py:896

commit v7 on v6

--- a/solution.py
+++ b/solution.py
@@ -25,8 +25,8 @@
 BF16 = jnp.bfloat16
 MATS = ((0, D), (288, D), (576, D), (864, D), (1920, FF))
 W1_AT = 1152
-WIDTH1, WIDTH2, WIDTH3, DW_STEPS = 4, 4, 4, 2
-LOCK1, LOCK2 = 4, 4
+WIDTH1, WIDTH2, WIDTH3, DW_STEPS = 4, 6, 4, 2
+LOCK1, LOCK2 = 8, 4
 PIECES = 1
 VEC_AT = 2304
 USED_ROWS = VEC_AT + 16
@@ -147,7 +147,7 @@
     x_ref, dy_ref, out_ref, ig_ref, flat, gflat,
     qs, ks, vs, os_, kbd, vbd, psc, xh1, r1, dx2s, h, h2, z, dul, o_t, dal, dyt, dqkv,
     wq, wk, wv, wo, w1, w2, tmp, hm2, parity, acc, acc2, acc3,
-    buf, parts, sib_in, plane_in, out_p, col_in, out_c, res, vec_own, vec_sib, vec_plane, vec_col,
+    buf, parts, sib_in, plane_in, out_p, col_in, out_c, res, vec_own, vec_plane, vec_col,
     vec_at, sq_plane, sq_col, vec_in,
     io_sem, g_col, g_fw, g_sib, g_recv, g_recv_sib, s_send, s_recv, p_send, p_recv, c_send, c_recv,
     f_sem, v_send, v_recv, n_send, n_recv, vg_send, vg_recv,
@@ -323,29 +323,13 @@
     def rows_at(t, count):
         return pl.ds(pl.multiple_of(t * n, 32), count * n)
 
-    def norm1(t, count, carry):
-        at = rows_at(t, count)
-        xh, r = norm_fwd(tokens_of(x_ref, t, count))
-        xh1[at, :] = xh
-        r1[at, :] = r
-        return carry
-
     copies_in[0].wait()
-    over_token_chunks(norm1, WIDTH1, 0)
-
-    for t in range(first):
-        pass_level(t)
-    for s in range(first * inner):
-        whole_shard(s)
-        unpack(s)
     for j, (s, a0, begin, end) in enumerate(vec_rows):
         @pl.when(pi != s % inner)
         def _(j=j):
             vec_arrived(j)
 
         flat[rows * s + begin : rows * s + end, :] = vec_in[j, begin - a0 : end - a0, :]
-    for (base, count), ref in zip(MATS[0:3], (wq, wk, wv)):
-        load_square(flat, base, count, tmp, ref)
 
     def vec(k):
         a = VEC_AT + 3 * (k // 2)
@@ -357,16 +341,49 @@
     g1, n1, bq, bv, bo, g2, n2, b2 = [vec(k) for k in range(8)]
     b1 = jnp.concatenate([flat[VEC_AT + 12 + c : VEC_AT + 13 + c, :] for c in range(4)], 1)
 
-    def dense1(t, count, carry):
+    def norm1(t, count, carry):
         at = rows_at(t, count)
-        hb = (xh1[at, :] * g1 + n1).astype(BF16)
-        h[at, 0:D] = hb[:, 0:D]
+        xh, r = norm_fwd(tokens_of(x_ref, t, count))
+        xh1[at, :] = xh
+        r1[at, :] = r
+        h[at, 0:D] = (xh * g1 + n1).astype(BF16)[:, 0:D]
+        return carry
+
+    over_token_chunks(norm1, WIDTH1, 0)
+
+    def take_levels(lo, hi):
+        for s in range(lo * inner, hi * inner):
+            whole_shard(s)
+            unpack(s)
+
+    for t in range(late):
+        pass_level(t)
+    take_levels(0, late)
+    for (base, count), ref in zip(MATS[0:2], (wq, wk)):
+        load_square(flat, base, count, tmp, ref)
+
+    def pass_v(i):
+        @pl.when(i == 1)
+        def _():
+            for t in range(late, first):
+                pass_level(t)
+
+    def dense_qk(t, count, carry):
+        hb = h[rows_at(t, count), :]
         put_tokens(qs, t, (nn(hb, wq[...]) + bq).astype(BF16).astype(F32))
         put_tokens(ks, t, nn(hb, wk[...]).astype(BF16).astype(F32))
+        return carry
+
+    over_token_chunks(dense_qk, WIDTH1, 0, pass_v)
+    take_levels(late, first)
+    load_square(flat, MATS[2][0], MATS[2][1], tmp, wv)
+
+    def dense_v(t, count, carry):
+        hb = h[rows_at(t, count), :]
         put_tokens(vs, t, (nn(hb, wv[...]) + bv).astype(BF16).astype(F32))
         return carry
 
-    over_token_chunks(dense1, WIDTH1, 0)
+    over_token_chunks(dense_v, WIDTH1, 0)
 
     lane3 = lax.rem(lax.broadcasted_iota(jnp.int32, (1, 256), 1), LANES)
     odd_head = lax.rem(lax.broadcasted_iota(jnp.int32, (1, 256), 1) // HEAD_DIM, 2) == 1
@@ -428,9 +445,7 @@
 
     lax.fori_loop(0, groups // LOCK1, attn, 0)
 
-    for s in range(first * inner, wide):
-        whole_shard(s)
-        unpack(s)
+    take_levels(first, outer)
     for (base, count), ref in zip(MATS[3:5], (wo, w2)):
         load_square(flat, base, count, tmp, ref)
     for c in range(4):
@@ -693,8 +708,6 @@
         vec_own[3 * k : 3 * k + 1, :] = a[:, 0:128]
         vec_own[3 * k + 1 : 3 * k + 2, :] = jnp.concatenate([a[:, 128:192], b[:, 0:64]], 1)
         vec_own[3 * k + 2 : 3 * k + 3, :] = b[:, 64:192]
-    vec_sends = [remote(vec_own, vec_sib, v_send.at[0], v_recv.at[0], sibling)]
-    vec_sends[0].start()
     copy_ig = pltpu.make_async_copy(ig_ref, ig_hbm, io_sem.at[3])
     copy_ig.start()
 
@@ -714,12 +727,14 @@
             ).wait_recv()
         return jnp.sum(slots[...], 0)
 
-    remote(vec_sib, vec_sib, v_send.at[0], v_recv.at[0], sibling).wait_recv()
-    vec_plane[pi] = vec_own[...] + vec_sib[...]
-    vec_sends += spread(vec_plane, pi, v_send, v_recv, 1, plane)
+    slot = 2 * pi + core
+    near = [2 * q + core for q in around] + [2 * q + 1 - core for q in around] + [2 * pi + 1 - core]
+    disc = plane + cross + [sibling]
+    vec_plane[slot] = vec_own[...]
+    vec_sends = spread(vec_plane, slot, v_send, v_recv, 0, disc)
     sum_plane(2)
-    vec_col[zo] = collected(vec_plane, around, v_send, v_recv, 1)
-    vec_sends += spread(vec_col, zo, v_send, v_recv, 1 + inner, column)
+    vec_col[zo] = collected(vec_plane, near, v_send, v_recv, 0)
+    vec_sends += spread(vec_col, zo, v_send, v_recv, 2 * inner, column)
 
     col_in[zo] = out_c[zo]
     for t in along:
@@ -730,11 +745,9 @@
     res[mine, :] = line
     last = remote(res.at[mine], res.at[mine], f_sem.at[0], f_sem.at[1], sibling)
     last.start()
-    slot = 2 * pi + core
-    near = [2 * q + core for q in around] + [2 * q + 1 - core for q in around] + [2 * pi + 1 - core]
     sq_plane[slot] = rows8(line * line)
-    sq_sends = spread(sq_plane, slot, n_send, n_recv, 0, plane + cross + [sibling])
-    vec = collected(vec_col, along, v_send, v_recv, 1 + inner)
+    sq_sends = spread(sq_plane, slot, n_send, n_recv, 0, disc)
+    vec = collected(vec_col, along, v_send, v_recv, 2 * inner)
     vec_at[VEC_AT:USED_ROWS, :] = vec
     remote(res.at[theirs], res.at[theirs], f_sem.at[0], f_sem.at[1], sibling).wait_recv()
     own[...] = res[0:rows, :] + vec_at[pl.ds(me * rows, rows), :]
@@ -803,16 +816,14 @@
         + [vm((inner - 1, outer, half, LANES), F32)]
         + [vm((outer, half, LANES), F32)] * 2
         + [vm((padded, LANES), F32)]
-        + [vm((16, LANES), F32)] * 2
-        + [vm((inner, 16, LANES), F32), vm((outer, 16, LANES), F32)]
+        + [vm((16, LANES), F32), vm((2 * inner, 16, LANES), F32), vm((outer, 16, LANES), F32)]
         + [vm((wide * rows, LANES), F32)]
         + [vm((2 * inner, *tile), F32), vm((outer, *tile), F32)]
         + [vm((vecs, min(24, padded), LANES), F32)]
         + [dma((4,)), dma((outer - 1,)), dma((outer, inner - 1)), dma((wide,)), dma((wide,)), dma((wide,))]
         + [dma((3, inner))] * 4
         + [dma((outer,)), dma((outer,)), dma((2,))]
-        + [dma((1 + inner + outer,))] * 2
-        + [dma((2 * inner + outer,))] * 2
+        + [dma((2 * inner + outer,))] * 4
         + [dma((vecs, outer + inner - 2)), dma((vecs,))]
     )
     anywhere, vmem = pl.BlockSpec(memory_space=pl.ANY), pl.BlockSpec(memory_space=pltpu.VMEM)

time: 63.1 us -> 60.5 us (0.959)
  Pallas kernels: 62.2 us -> 59.7 us
    pallas_call x1, Pallas kernels: 59.4 us -> 56.9 us  [step(): pl.pallas_call(functools.partial(step_kernel, wide), out_shape=(jax.Shape...]
where the time goes in v7:
time: 60.5 us; the launch traced here: 60.3 us
  Pallas kernels  59.7 us (99%)
  between operations  0.64 us (1%)
    pallas_call x1, Pallas kernels, step(): pl.pallas_call(functools.partial(step_kernel, wide), out_shape=(jax.Shape...  56.9 us
    pallas_call x1, Pallas kernels, finish(): pl.pallas_call(finish_kernel, out_shape=(like(block_out.shape, BF16), lik...  2.81 us

profile of v7, /device:TPU:0, one launch (start us, length us, event | category | flops | bytes accessed | tf_op | source)
XLA Modules:
  0.0 60.3 jit_solution(9328209892837166771)
XLA Ops:
  0.6 56.9 %step.1 = (bf16[48,6528]{1,0:T(8,128)(2,1)}, f32[48,6528]{1,0:T(8,128)}, f32[145,128]{1,0:T(8,128)}, f32[8,128]{1,0:T(8,128)}) custom-call(bf16[48,6528]{1,0:T(8,128)(2,1)} %x_hbm.1, bf16[48,6528]{1,0:T(8,128)(2,1)} %dy_hbm.1, f32[145,128]{1,0:T(8,128)} %bitcast.9), custom_call_target="tpu_custom_call" | custom-call | tf_op jit(solution)/shard_map/step/pallas_call | solution.py:830
  57.5 2.8 %finish.1 = (bf16[48,6528]{1,0:T(8,128)(2,1)}, f32[48,6528]{1,0:T(8,128)}, f32[1,1]{1,0:T(1,128)}, f32[145,128]{1,0:T(8,128)}, f32[145,128]{1,0:T(8,128)}, /*ind...) custom-call(bf16[48,6528]{1,0:T(8,128)(2,1)} %get-tuple-element.20.refs_0_, ...), custom_call_target="tpu_custom_call" | custom-call | tf_op jit(solution)/shard_map/finish/pallas_call | solution.py:907

commit v8 on v7

--- a/solution.py
+++ b/solution.py
@@ -146,7 +146,7 @@
     x_hbm, dy_hbm, shard, out_hbm, ig_hbm, own, squares,
     x_ref, dy_ref, out_ref, ig_ref, flat, gflat,
     qs, ks, vs, os_, kbd, vbd, psc, xh1, r1, dx2s, h, h2, z, dul, o_t, dal, dyt, dqkv,
-    wq, wk, wv, wo, w1, w2, tmp, hm2, parity, acc, acc2, acc3,
+    wq, wk, wv, wo, w1, w2, tmp, hm2, parity, sample, hs, acc, acc2, acc3,
     buf, parts, sib_in, plane_in, out_p, col_in, out_c, res, vec_own, vec_plane, vec_col,
     vec_at, sq_plane, sq_col, vec_in,
     io_sem, g_col, g_fw, g_sib, g_recv, g_recv_sib, s_send, s_recv, p_send, p_recv, c_send, c_recv,
@@ -189,14 +189,19 @@
         hm2[80 * p : 80 * (p + 1), :] = jnp.where(
             (lane >= lo) & (lane < lo + PAIR_DIM), 1.0, 0.0
         ).astype(BF16)
-    head = lax.broadcasted_iota(jnp.int32, (16, 256), 1) // HEAD_DIM
+    lane16 = lax.broadcasted_iota(jnp.int32, (16, 256), 1)
+    for b in range(GROUP):
+        query = lax.rem(lane16, LANES)
+        sample[16 * b : 16 * (b + 1), :] = jnp.where(
+            (query >= ROWS * b) & (query < ROWS * (b + 1)), 1.0, 0.0
+        ).astype(BF16)
+    head = lane16 // HEAD_DIM
     for k in range(2):
         parity[16 * k : 16 * (k + 1), :] = jnp.where(
             (lax.rem(head, 2) == k) & (head < HEADS), 1.0, 0.0
         ).astype(BF16)
     ones_lane = (lax.broadcasted_iota(jnp.int32, (toks, 64), 1) == 0).astype(F32).astype(BF16)
-    for ref in (h, h2, o_t):
-        ref[:, D:256] = ones_lane
+    o_t[:, D:256] = ones_lane
     for ref in (qs, ks, vs, os_):
         ref[...] = jnp.zeros(ref.shape, F32)
 
@@ -331,9 +336,11 @@
 
         flat[rows * s + begin : rows * s + end, :] = vec_in[j, begin - a0 : end - a0, :]
 
+    ones3 = (lax.broadcasted_iota(jnp.int32, (1, 64), 1) < 3).astype(F32)
+
     def vec(k):
         a = VEC_AT + 3 * (k // 2)
-        zero = jnp.zeros((1, 64), F32)
+        zero = ones3 if k in (1, 6) else jnp.zeros((1, 64), F32)
         if k % 2 == 0:
             return jnp.concatenate([flat[a : a + 1, :], flat[a + 1 : a + 2, 0:64], zero], 1)
         return jnp.concatenate([flat[a + 1 : a + 2, 64:128], flat[a + 2 : a + 3, :], zero], 1)
@@ -346,10 +353,28 @@
         xh, r = norm_fwd(tokens_of(x_ref, t, count))
         xh1[at, :] = xh
         r1[at, :] = r
-        h[at, 0:D] = (xh * g1 + n1).astype(BF16)[:, 0:D]
+        hb = (xh * g1 + n1).astype(BF16)
+        h[at, :] = hb
+        put_tokens(os_, t, hb.astype(F32))
         return carry
 
     over_token_chunks(norm1, WIDTH1, 0)
+
+    def bias_rows(b):
+        row = lax.broadcasted_iota(jnp.int32, (16, b.shape[1]), 0)
+        out = jnp.zeros((16, b.shape[1]), F32)
+        for k in range(3):
+            part = b.astype(BF16).astype(F32)
+            out = jnp.where(row == k, part, out)
+            b = b - part
+        return out.astype(BF16)
+
+    half_groups = LOCK2 * GROWS
+
+    @pl.loop(0, groups // LOCK2)
+    def _(i):
+        at = pl.ds(pl.multiple_of(i * half_groups, 16), half_groups)
+        hs[at, :] = get_rows(os_, pl.multiple_of(i * half_groups, 8), half_groups).astype(BF16)
 
     def take_levels(lo, hi):
         for s in range(lo * inner, hi * inner):
@@ -361,6 +386,7 @@
     take_levels(0, late)
     for (base, count), ref in zip(MATS[0:2], (wq, wk)):
         load_square(flat, base, count, tmp, ref)
+    wq[D : D + 16, :] = bias_rows(bq)
 
     def pass_v(i):
         @pl.when(i == 1)
@@ -370,17 +396,18 @@
 
     def dense_qk(t, count, carry):
         hb = h[rows_at(t, count), :]
-        put_tokens(qs, t, (nn(hb, wq[...]) + bq).astype(BF16).astype(F32))
+        put_tokens(qs, t, nn(hb, wq[...]).astype(BF16).astype(F32))
         put_tokens(ks, t, nn(hb, wk[...]).astype(BF16).astype(F32))
         return carry
 
     over_token_chunks(dense_qk, WIDTH1, 0, pass_v)
     take_levels(late, first)
     load_square(flat, MATS[2][0], MATS[2][1], tmp, wv)
+    wv[D : D + 16, :] = bias_rows(bv)
 
     def dense_v(t, count, carry):
         hb = h[rows_at(t, count), :]
-        put_tokens(vs, t, (nn(hb, wv[...]) + bv).astype(BF16).astype(F32))
+        put_tokens(vs, t, nn(hb, wv[...]).astype(BF16).astype(F32))
         return carry
 
     over_token_chunks(dense_v, WIDTH1, 0)
@@ -404,7 +431,7 @@
         both = nn(rows2.astype(BF16), right)
         return jnp.where(odd_head, both[ROWS : 2 * ROWS], both[0:ROWS])
 
-    jrow = lax.broadcasted_iota(jnp.int32, (1, ROWS, 256), 1)
+    jrow = lax.broadcasted_iota(jnp.int32, (1, ROWS - 32, 256), 1)
     cexp = math.log2(math.e) / math.sqrt(HEAD_DIM)
     scale = 1.0 / math.sqrt(HEAD_DIM)
 
@@ -429,7 +456,10 @@
                             two * hm2[80 * p : 80 * (p + 1), :]
                         )
         st = [squeeze(nt(kbd[pl.ds(base0 + 3 * HJ * k, 3 * HJ), :], qg[k])) for k in sets]
-        st = [jnp.where(jrow < SEQ, v, -1e30) for v in st]
+        st = [
+            jnp.concatenate([v[:, 0:32], jnp.where(jrow < SEQ - 32, v[:, 32:ROWS], -1e30)], 1)
+            for v in st
+        ]
         m = [jnp.max(v, 1, keepdims=True) for v in st]
         e = [jnp.exp2((st[k] - m[k]) * cexp) for k in sets]
         l = [1.0 / jnp.sum(v, 1, keepdims=True) for v in e]
@@ -449,8 +479,10 @@
     for (base, count), ref in zip(MATS[3:5], (wo, w2)):
         load_square(flat, base, count, tmp, ref)
     for c in range(4):
-        w1[0:D, 128 * c : 128 * (c + 1)] = flat[pl.ds(W1_AT + c, D, stride=4), :].astype(BF16)
-    w1[D:256, :] = jnp.zeros((256 - D, 2 * FF), BF16)
+        part = flat[pl.ds(W1_AT + c, D, stride=4), :]
+        w1[0:D, 128 * c : 128 * (c + 1)] = (part if c < 2 else 0.5 * part).astype(BF16)
+    w1[D : D + 16, :] = bias_rows(jnp.concatenate([b1[:, 0:FF], 0.5 * b1[:, FF:]], 1))
+    w1[D + 16 : 256, :] = jnp.zeros((240 - D, 2 * FF), BF16)
     copies_in[1].wait()
 
     def dense2(t0, count, carry):
@@ -461,13 +493,13 @@
         x2 = tokens_of(x_ref, t0, count) + (nn(o, wo[...]) + bo)
         xh, r = norm_fwd(x2)
         hb = (xh * g2 + n2).astype(BF16)
-        h2[at, 0:D] = hb[:, 0:D]
-        u = nn(hb, w1[...]) + b1
+        h2[at, :] = hb
+        u = nn(hb, w1[...])
         gate, up = u[:, :FF], u[:, FF:]
         sq = gate * gate
         t = jnp.tanh(gate * (GELU_C + (GELU_C * 0.044715) * sq))
-        half = 0.5 + 0.5 * t
-        act = gate * half
+        t1 = 1.0 + t
+        act = gate * t1
         zb = (act * up).astype(BF16)
         z[at, :] = zb
         y = x2 + nn(zb, w2[...]) + b2
@@ -476,7 +508,7 @@
         dyb = dyf.astype(BF16)
         dyt[at, :] = dyb
         dz = nt(dyb, w2[...])
-        slope = half + gate * (0.5 - 0.5 * t * t) * (GELU_C + (3 * GELU_C * 0.044715) * sq)
+        slope = t1 + act * (1.0 - t) * (GELU_C + (3 * GELU_C * 0.044715) * sq)
         du = jnp.concatenate([(dz * up * slope).astype(BF16), (dz * act).astype(BF16)], 1)
         dul[at, :] = du
         dh = nt(du, w1[...])
@@ -499,7 +531,7 @@
     def over_tokens(*products):
         for acc, _, _ in products:
             acc[...] = jnp.zeros(acc.shape, F32)
-        size = toks // DW_STEPS
+        size = products[0][1].shape[0] // DW_STEPS
 
         @pl.loop(0, DW_STEPS)
         def _(i):
@@ -510,8 +542,10 @@
     over_tokens((acc, z, dyt), (acc2, h2, dul), (acc3, o_t, dal))
     store_square(acc[...], gflat, 1920, FF, tmp)
     for c in range(4):
-        gflat[pl.ds(W1_AT + c, D, stride=4), :] = acc2[0:D, 128 * c : 128 * (c + 1)]
-        vec_own[12 + c : 13 + c, :] = acc2[D : D + 1, 128 * c : 128 * (c + 1)]
+        part = acc2[0 : D + 8, 128 * c : 128 * (c + 1)]
+        part = part if c < 2 else 0.5 * part
+        gflat[pl.ds(W1_AT + c, D, stride=4), :] = part[0:D]
+        vec_own[12 + c : 13 + c, :] = part[D : D + 1]
     store_square(acc3[...], gflat, 864, D, tmp)
     dbo = acc3[D : D + 1, :]
 
@@ -586,13 +620,14 @@
     send_cores(0)
 
     def by_sample(v):
+        v = v.reshape(HJ, 256).astype(BF16).reshape(HJ // 16, 16, 256)
         return jnp.concatenate(
             [
-                jnp.where((lane3 >= ROWS * b) & (lane3 < ROWS * (b + 1)), v, 0.0).reshape(HJ, 256)
+                (v * sample[16 * b : 16 * (b + 1), :][None]).reshape(HJ, 256)
                 for b in range(GROUP)
             ],
             0,
-        ).astype(BF16)
+        )
 
     pair_lane = lax.broadcasted_iota(jnp.int32, (1, LANES), 1)
 
@@ -618,25 +653,18 @@
 
         r0 = pl.multiple_of(i * (LOCK2 * GROWS), 8)
         p0 = pl.multiple_of(i * (LOCK2 * HJ), 32)
+        out = []
         for k in range(LOCK2):
             dg = by_parity(get_rows(os_, r0 + GROWS * k, LANES).astype(BF16))
-            dv = own_lanes(nn(by_sample(probs(p0 + HJ * k)), dg))
-            put_rows(vs, r0 + GROWS * k, dv.astype(BF16).astype(F32))
+            out.append(own_lanes(nn(by_sample(probs(p0 + HJ * k)), dg)))
+        out = jnp.concatenate(out, 0).astype(BF16)
+        dqkv[pl.ds(pl.multiple_of(i * half_groups, 16), half_groups), 512:768] = out
+        put_rows(vs, r0, out.astype(F32))
         return carry
 
     lax.fori_loop(0, groups // LOCK2, attn_back_v, 0)
 
-    def collect(refs):
-        def chunk(t0, count, carry):
-            at = rows_at(t0, count)
-            for k, ref in refs:
-                dqkv[at, 256 * k : 256 * (k + 1)] = get_tokens(ref, t0, count).astype(BF16)
-            return carry
-
-        over_token_chunks(chunk, WIDTH3, 0)
-
-    collect([(2, vs)])
-    over_tokens((acc, h, dqkv.at[:, 512:768]))
+    over_tokens((acc, hs, dqkv.at[:, 512:768]))
     store_square(acc[...], gflat, 576, D, tmp)
     dbv = acc[D : D + 1, :]
     send_cores(1)
@@ -662,18 +690,21 @@
         ds = [p[k] * (dp[k] - t[k]) for k in sets]
         dst = [v.reshape(HJ, 256).T for v in ds]
         dk = [own_lanes(nn(by_sample(ds[k]), qg[k])) * scale for k in sets]
-        for b in range(GROUP):
-            for k in sets:
-                dq = per_query(dst[k], kbd[pl.ds(base0 + HJ * (3 * k + b), HJ), :], b)
-                put_rows(qs, r0 + GROWS * k + ROWS * b, (dq * scale).astype(BF16).astype(F32))
-        for k in sets:
-            put_rows(ks, r0 + GROWS * k, dk[k].astype(BF16).astype(F32))
+        dq = [
+            per_query(dst[k], kbd[pl.ds(base0 + HJ * (3 * k + b), HJ), :], b) * scale
+            for k in sets
+            for b in range(GROUP)
+        ]
+        at = pl.ds(pl.multiple_of(i * half_groups, 16), half_groups)
+        for col, ref, val in ((0, qs, dq), (256, ks, dk)):
+            val = jnp.concatenate(val, 0).astype(BF16)
+            dqkv[at, col : col + 256] = val
+            put_rows(ref, r0, val.astype(F32))
         return carry
 
     lax.fori_loop(0, groups // LOCK2, attn_back, 0)
 
-    collect([(0, qs), (1, ks)])
-    over_tokens((acc2, h, dqkv.at[:, 0:512]))
+    over_tokens((acc2, hs, dqkv.at[:, 0:512]))
     for k in range(2):
         store_square(acc2[:, 256 * k : 256 * (k + 1)], gflat, 288 * k, D, tmp)
     send_cores(2)
@@ -682,9 +713,9 @@
         dg1, dn1 = carry
         at = rows_at(t0, count)
         dh = (
-            nt(dqkv[at, 0:256], wq[...])
-            + nt(dqkv[at, 256:512], wk[...])
-            + nt(dqkv[at, 512:768], wv[...])
+            nt(get_tokens(qs, t0, count).astype(BF16), wq[...])
+            + nt(get_tokens(ks, t0, count).astype(BF16), wk[...])
+            + nt(get_tokens(vs, t0, count).astype(BF16), wv[...])
         )
         xh = xh1[at, :]
         ig = dx2s[at, :] + norm_back(dh, xh, r1[at, :], g1)
@@ -806,10 +837,10 @@
         + [vm((groups * HJ, 256), F32)]
         + [vm((toks, 256), F32), vm((toks, 1), F32), vm((toks, 256), F32)]
         + [tok, tok, tok, vm((toks, 2 * FF), BF16), tok]
-        + [tok, tok, vm((toks, 3 * 256), BF16)]
+        + [tok, tok, vm((n * ROWS, 3 * 256), BF16)]
         + [vm((256, 256), BF16)] * 4
         + [vm((256, 2 * FF), BF16), vm((FF, 256), BF16), vm((2, FF, 128), F32)]
-        + [vm((HJ, 256), BF16), vm((32, 256), BF16)]
+        + [vm((HJ, 256), BF16), vm((32, 256), BF16), vm((16 * GROUP, 256), BF16), vm((n * ROWS, 256), BF16)]
         + [vm((256, 256), F32), vm((256, 512), F32), vm((256, 256), F32)]
         + [vm((wide, padded, LANES), F32), vm((outer, inner, padded, LANES), F32)]
         + [vm((outer, inner, half, LANES), F32), vm((inner, outer, half, LANES), F32)]

time: 60.5 us -> 59.9 us (0.990)
    pallas_call x1, Pallas kernels: 56.9 us -> 56.3 us  [step(): pl.pallas_call(functools.partial(step_kernel, wide), out_shape=(jax.Shape...]
where the time goes in v8:
time: 59.9 us; the launch traced here: 59.7 us
  Pallas kernels  59.1 us (99%)
  between operations  0.64 us (1%)
    pallas_call x1, Pallas kernels, step(): pl.pallas_call(functools.partial(step_kernel, wide), out_shape=(jax.Shape...  56.3 us
    pallas_call x1, Pallas kernels, finish(): pl.pallas_call(finish_kernel, out_shape=(like(block_out.shape, BF16), lik...  2.81 us

profile of v8, /device:TPU:0, one launch (start us, length us, event | category | flops | bytes accessed | tf_op | source)
XLA Modules:
  0.0 59.7 jit_solution(15403399210319840642)
XLA Ops:
  0.6 56.3 %step.1 = (bf16[48,6528]{1,0:T(8,128)(2,1)}, f32[48,6528]{1,0:T(8,128)}, f32[145,128]{1,0:T(8,128)}, f32[8,128]{1,0:T(8,128)}) custom-call(bf16[48,6528]{1,0:T(8,128)(2,1)} %x_hbm.1, bf16[48,6528]{1,0:T(8,128)(2,1)} %dy_hbm.1, f32[145,128]{1,0:T(8,128)} %bitcast.9), custom_call_target="tpu_custom_call" | custom-call | tf_op jit(solution)/shard_map/step/pallas_call | solution.py:861
  56.9 2.8 %finish.1 = (bf16[48,6528]{1,0:T(8,128)(2,1)}, f32[48,6528]{1,0:T(8,128)}, f32[1,1]{1,0:T(1,128)}, f32[145,128]{1,0:T(8,128)}, f32[145,128]{1,0:T(8,128)}, /*ind...) custom-call(bf16[48,6528]{1,0:T(8,128)(2,1)} %get-tuple-element.20.refs_0_, ...), custom_call_target="tpu_custom_call" | custom-call | tf_op jit(solution)/shard_map/finish/pallas_call | solution.py:938

commit v9 on v8

--- a/solution.py
+++ b/solution.py
@@ -647,7 +647,7 @@
         return psc[pl.ds(at, HJ), :].reshape(PAIRS, ROWS, 256)
 
     def attn_back_v(i, carry):
-        @pl.when(i == 2)
+        @pl.when(i == 3)
         def _():
             sum_cores(0)
 
@@ -673,10 +673,6 @@
         @pl.when(i == 1)
         def _():
             sum_cores(1)
-
-        @pl.when(i == 3)
-        def _():
-            sum_plane(0)
 
         r0 = pl.multiple_of(i * (LOCK2 * GROWS), 8)
         base0 = pl.multiple_of(i * (LOCK2 * 3 * HJ), 32)
@@ -708,6 +704,7 @@
     for k in range(2):
         store_square(acc2[:, 256 * k : 256 * (k + 1)], gflat, 288 * k, D, tmp)
     send_cores(2)
+    sum_plane(0)
 
     def dense3(t0, count, carry):
         dg1, dn1 = carry

time: 59.9 us -> 58.3 us (0.973)
  Pallas kernels: 59.1 us -> 57.5 us
    pallas_call x1, Pallas kernels: 56.3 us -> 54.7 us  [step(): pl.pallas_call(functools.partial(step_kernel, wide), out_shape=(jax.Shape...]
where the time goes in v9:
time: 58.3 us; the launch traced here: 58.2 us
  Pallas kernels  57.5 us (99%)
  between operations  0.64 us (1%)
    pallas_call x1, Pallas kernels, step(): pl.pallas_call(functools.partial(step_kernel, wide), out_shape=(jax.Shape...  54.7 us
    pallas_call x1, Pallas kernels, finish(): pl.pallas_call(finish_kernel, out_shape=(like(block_out.shape, BF16), lik...  2.81 us

profile of v9, /device:TPU:0, one launch (start us, length us, event | category | flops | bytes accessed | tf_op | source)
XLA Modules:
  0.0 58.2 jit_solution(7324684604834539295)
XLA Ops:
  0.6 54.7 %step.1 = (bf16[48,6528]{1,0:T(8,128)(2,1)}, f32[48,6528]{1,0:T(8,128)}, f32[145,128]{1,0:T(8,128)}, f32[8,128]{1,0:T(8,128)}) custom-call(bf16[48,6528]{1,0:T(8,128)(2,1)} %x_hbm.1, bf16[48,6528]{1,0:T(8,128)(2,1)} %dy_hbm.1, f32[145,128]{1,0:T(8,128)} %bitcast.9), custom_call_target="tpu_custom_call" | custom-call | tf_op jit(solution)/shard_map/step/pallas_call | solution.py:858
  55.4 2.8 %finish.1 = (bf16[48,6528]{1,0:T(8,128)(2,1)}, f32[48,6528]{1,0:T(8,128)}, f32[1,1]{1,0:T(1,128)}, f32[145,128]{1,0:T(8,128)}, f32[145,128]{1,0:T(8,128)}, /*ind...) custom-call(bf16[48,6528]{1,0:T(8,128)(2,1)} %get-tuple-element.20.refs_0_, ...), custom_call_target="tpu_custom_call" | custom-call | tf_op jit(solution)/shard_map/finish/pallas_call | solution.py:935

commit v10 on v9

--- a/solution.py
+++ b/solution.py
@@ -145,7 +145,7 @@
     wide,
     x_hbm, dy_hbm, shard, out_hbm, ig_hbm, own, squares,
     x_ref, dy_ref, out_ref, ig_ref, flat, gflat,
-    qs, ks, vs, os_, kbd, vbd, psc, xh1, r1, dx2s, h, h2, z, dul, o_t, dal, dyt, dqkv,
+    qs, ks, vs, os_, kbd, vbd, psc, xb, xh1, r1, dx2s, h, h2, z, dul, o_t, dal, dyt, dqkv,
     wq, wk, wv, wo, w1, w2, tmp, hm2, parity, sample, hs, acc, acc2, acc3,
     buf, parts, sib_in, plane_in, out_p, col_in, out_c, res, vec_own, vec_plane, vec_col,
     vec_at, sq_plane, sq_col, vec_in,
@@ -350,15 +350,26 @@
 
     def norm1(t, count, carry):
         at = rows_at(t, count)
-        xh, r = norm_fwd(tokens_of(x_ref, t, count))
+        x = tokens_of(x_ref, t, count)
+        xh, r = norm_fwd(x)
         xh1[at, :] = xh
         r1[at, :] = r
         hb = (xh * g1 + n1).astype(BF16)
         h[at, :] = hb
         put_tokens(os_, t, hb.astype(F32))
+        xb[at, :] = x + bo
         return carry
 
     over_token_chunks(norm1, WIDTH1, 0)
+
+    def take_dy(t, count, db2):
+        dy = tokens_of(dy_ref, t, count)
+        dyt[rows_at(t, count), :] = dy.astype(BF16)
+        return db2 + rows8(dy)
+
+    zero = jnp.zeros((8, 256), F32)
+    copies_in[1].wait()
+    db2 = over_token_chunks(take_dy, WIDTH1, zero)
 
     def bias_rows(b):
         row = lax.broadcasted_iota(jnp.int32, (16, b.shape[1]), 0)
@@ -483,14 +494,12 @@
         w1[0:D, 128 * c : 128 * (c + 1)] = (part if c < 2 else 0.5 * part).astype(BF16)
     w1[D : D + 16, :] = bias_rows(jnp.concatenate([b1[:, 0:FF], 0.5 * b1[:, FF:]], 1))
     w1[D + 16 : 256, :] = jnp.zeros((240 - D, 2 * FF), BF16)
-    copies_in[1].wait()
-
     def dense2(t0, count, carry):
-        dg2, dn2, db2 = carry
+        dg2, dn2 = carry
         at = rows_at(t0, count)
         o = get_tokens(os_, t0, count).astype(BF16)
         o_t[at, 0:D] = o[:, 0:D]
-        x2 = tokens_of(x_ref, t0, count) + (nn(o, wo[...]) + bo)
+        x2 = xb[at, :] + nn(o, wo[...])
         xh, r = norm_fwd(x2)
         hb = (xh * g2 + n2).astype(BF16)
         h2[at, :] = hb
@@ -504,9 +513,8 @@
         z[at, :] = zb
         y = x2 + nn(zb, w2[...]) + b2
         out_ref[:, pl.ds(pl.multiple_of(t0 * D, 128), count * D)] = join_tokens(y, n).astype(BF16)
-        dyf = tokens_of(dy_ref, t0, count)
-        dyb = dyf.astype(BF16)
-        dyt[at, :] = dyb
+        dyb = dyt[at, :]
+        dyf = dyb.astype(F32)
         dz = nt(dyb, w2[...])
         slope = t1 + act * (1.0 - t) * (GELU_C + (3 * GELU_C * 0.044715) * sq)
         du = jnp.concatenate([(dz * up * slope).astype(BF16), (dz * act).astype(BF16)], 1)
@@ -517,10 +525,14 @@
         da = dx2.astype(BF16)
         dal[at, :] = da
         put_tokens(os_, t0, nt(da, wo[...]).astype(BF16).astype(F32))
-        return dg2 + rows8(dh * xh), dn2 + rows8(dh), db2 + rows8(dyf)
-
-    zero = jnp.zeros((8, 256), F32)
-    dg2, dn2, db2 = over_token_chunks(dense2, WIDTH2, (zero, zero, zero))
+        acc[...] += tn(zb, dyb)
+        acc2[...] += tn(hb, du)
+        acc3[...] += tn(o_t[at, :], da)
+        return dg2 + rows8(dh * xh), dn2 + rows8(dh)
+
+    for ref in (acc, acc2, acc3):
+        ref[...] = jnp.zeros(ref.shape, F32)
+    dg2, dn2 = over_token_chunks(dense2, WIDTH2, (zero, zero))
 
     copy_out = pltpu.make_async_copy(out_ref, out_hbm, io_sem.at[2])
     copy_out.start()
@@ -539,7 +551,6 @@
             for acc, a, b in products:
                 acc[...] += tn(a[at, :], b[at, :])
 
-    over_tokens((acc, z, dyt), (acc2, h2, dul), (acc3, o_t, dal))
     store_square(acc[...], gflat, 1920, FF, tmp)
     for c in range(4):
         part = acc2[0 : D + 8, 128 * c : 128 * (c + 1)]
@@ -832,7 +843,8 @@
         + [sm] * 4
         + [vm((groups * 3 * HJ, 256), BF16)] * 2
         + [vm((groups * HJ, 256), F32)]
-        + [vm((toks, 256), F32), vm((toks, 1), F32), vm((toks, 256), F32)]
+        + [vm((toks, 256), F32)] * 2
+        + [vm((toks, 1), F32), vm((toks, 256), F32)]
         + [tok, tok, tok, vm((toks, 2 * FF), BF16), tok]
         + [tok, tok, vm((n * ROWS, 3 * 256), BF16)]
         + [vm((256, 256), BF16)] * 4

time: 58.3 us -> 57.4 us (0.985)
  Pallas kernels: 57.5 us -> 56.6 us
    pallas_call x1, Pallas kernels: 54.7 us -> 53.8 us  [step(): pl.pallas_call(functools.partial(step_kernel, wide), out_shape=(jax.Shape...]
where the time goes in v10:
time: 57.4 us; the launch traced here: 57.2 us
  Pallas kernels  56.6 us (99%)
  between operations  0.64 us (1%)
    pallas_call x1, Pallas kernels, step(): pl.pallas_call(functools.partial(step_kernel, wide), out_shape=(jax.Shape...  53.8 us
    pallas_call x1, Pallas kernels, finish(): pl.pallas_call(finish_kernel, out_shape=(like(block_out.shape, BF16), lik...  2.81 us

profile of v10, /device:TPU:0, one launch (start us, length us, event | category | flops | bytes accessed | tf_op | source)
XLA Modules:
  0.0 57.2 jit_solution(15716166030257908870)
XLA Ops:
  0.6 53.8 %step.1 = (bf16[48,6528]{1,0:T(8,128)(2,1)}, f32[48,6528]{1,0:T(8,128)}, f32[145,128]{1,0:T(8,128)}, f32[8,128]{1,0:T(8,128)}) custom-call(bf16[48,6528]{1,0:T(8,128)(2,1)} %x_hbm.1, bf16[48,6528]{1,0:T(8,128)(2,1)} %dy_hbm.1, f32[145,128]{1,0:T(8,128)} %bitcast.9), custom_call_target="tpu_custom_call" | custom-call | tf_op jit(solution)/shard_map/step/pallas_call | solution.py:870
  54.4 2.8 %finish.1 = (bf16[48,6528]{1,0:T(8,128)(2,1)}, f32[48,6528]{1,0:T(8,128)}, f32[1,1]{1,0:T(1,128)}, f32[145,128]{1,0:T(8,128)}, f32[145,128]{1,0:T(8,128)}, /*ind...) custom-call(bf16[48,6528]{1,0:T(8,128)(2,1)} %get-tuple-element.20.refs_0_, ...), custom_call_target="tpu_custom_call" | custom-call | tf_op jit(solution)/shard_map/finish/pallas_call | solution.py:947

commit v11 on v10

--- a/solution.py
+++ b/solution.py
@@ -143,8 +143,8 @@
 
 def step_kernel(
     wide,
-    x_hbm, dy_hbm, shard, out_hbm, ig_hbm, own, squares,
-    x_ref, dy_ref, out_ref, ig_ref, flat, gflat,
+    x_hbm, dy_hbm, shard_hbm, out_hbm, ig_hbm, own_hbm, squares,
+    shard, own, x_ref, dy_ref, out_ref, ig_ref, flat, gflat,
     qs, ks, vs, os_, kbd, vbd, psc, xb, xh1, r1, dx2s, h, h2, z, dul, o_t, dal, dyt, dqkv,
     wq, wk, wv, wo, w1, w2, tmp, hm2, parity, sample, hs, acc, acc2, acc3,
     buf, parts, sib_in, plane_in, out_p, col_in, out_c, res, vec_own, vec_plane, vec_col,
@@ -175,13 +175,14 @@
     copies_in = [
         pltpu.make_async_copy(x_hbm, x_ref, io_sem.at[0]),
         pltpu.make_async_copy(dy_hbm, dy_ref, io_sem.at[1]),
+        pltpu.make_async_copy(shard_hbm, shard, io_sem.at[4]),
     ]
-    for copy in copies_in:
-        copy.start()
 
     cross = [(zo * inner + q, 1 - core) for q in around]
     known = plane + cross + column + [sibling]
     greet(known)
+    for copy in (copies_in[2], copies_in[0], copies_in[1]):
+        copy.start()
     lane = lax.broadcasted_iota(jnp.int32, (80, 256), 1)
     row = lax.broadcasted_iota(jnp.int32, (80, 256), 0)
     for p in range(PAIRS // 2):
@@ -207,6 +208,7 @@
 
     parts[...] = jnp.zeros(parts.shape, F32)
     vec_at[...] = jnp.zeros(vec_at.shape, F32)
+    copies_in[2].wait()
     pl.semaphore_wait(pltpu.get_barrier_semaphore(), len(known))
     buf[me, 0:rows, :] = shard[...]
     buf[me, rows:, :] = jnp.zeros((buf.shape[1] - rows, LANES), F32)
@@ -790,6 +792,8 @@
     vec_at[VEC_AT:USED_ROWS, :] = vec
     remote(res.at[theirs], res.at[theirs], f_sem.at[0], f_sem.at[1], sibling).wait_recv()
     own[...] = res[0:rows, :] + vec_at[pl.ds(me * rows, rows), :]
+    copy_own = pltpu.make_async_copy(own, own_hbm, io_sem.at[5])
+    copy_own.start()
     sq_col[zo] = collected(sq_plane, near, n_send, n_recv, 0)
     sq_sends += spread(sq_col, zo, n_send, n_recv, 2 * inner, column)
     both = collected(sq_col, along, n_send, n_recv, 2 * inner) + rows8(vec * vec)
@@ -823,6 +827,7 @@
             copy.wait_send()
     copy_out.wait()
     copy_ig.wait()
+    copy_own.wait()
 
 
 def step(x, dy, shard, wide):
@@ -838,7 +843,8 @@
     tok = vm((toks, 256), BF16)
     tile = (8, LANES)
     scratch = (
-        [vm(x.shape, BF16), vm(x.shape, BF16), vm(x.shape, BF16), vm(x.shape, F32)]
+        [vm((rows, LANES), F32)] * 2
+        + [vm(x.shape, BF16), vm(x.shape, BF16), vm(x.shape, BF16), vm(x.shape, F32)]
         + [vm((wide * rows, LANES), F32)] * 2
         + [sm] * 4
         + [vm((groups * 3 * HJ, 256), BF16)] * 2
@@ -860,7 +866,7 @@
         + [vm((wide * rows, LANES), F32)]
         + [vm((2 * inner, *tile), F32), vm((outer, *tile), F32)]
         + [vm((vecs, min(24, padded), LANES), F32)]
-        + [dma((4,)), dma((outer - 1,)), dma((outer, inner - 1)), dma((wide,)), dma((wide,)), dma((wide,))]
+        + [dma((6,)), dma((outer - 1,)), dma((outer, inner - 1)), dma((wide,)), dma((wide,)), dma((wide,))]
         + [dma((3, inner))] * 4
         + [dma((outer,)), dma((outer,)), dma((2,))]
         + [dma((2 * inner + outer,))] * 4
@@ -875,8 +881,8 @@
             jax.ShapeDtypeStruct((rows, LANES), F32),
             jax.ShapeDtypeStruct(tile, F32),
         ),
-        in_specs=[anywhere, anywhere, vmem],
-        out_specs=(anywhere, anywhere, vmem, vmem),
+        in_specs=[anywhere] * 3,
+        out_specs=(anywhere, anywhere, anywhere, vmem),
         scratch_shapes=scratch,
         compiler_params=pltpu.CompilerParams(
             collective_id=0, has_side_effects=True, vmem_limit_bytes=60 * 2**20

time: 57.4 us -> 56.7 us (0.988)
  Pallas kernels: 56.6 us -> 55.9 us
    pallas_call x1, Pallas kernels: 53.8 us -> 53.1 us  [step(): pl.pallas_call(functools.partial(step_kernel, wide), out_shape=(jax.Shape...]
where the time goes in v11:
time: 56.7 us; the launch traced here: 56.5 us
  Pallas kernels  55.9 us (99%)
  between operations  0.64 us (1%)
    pallas_call x1, Pallas kernels, step(): pl.pallas_call(functools.partial(step_kernel, wide), out_shape=(jax.Shape...  53.1 us
    pallas_call x1, Pallas kernels, finish(): pl.pallas_call(finish_kernel, out_shape=(like(block_out.shape, BF16), lik...  2.81 us

profile of v11, /device:TPU:0, one launch (start us, length us, event | category | flops | bytes accessed | tf_op | source)
XLA Modules:
  0.0 56.5 jit_solution(6903606014949001893)
XLA Ops:
  0.6 53.1 %step.1 = (bf16[48,6528]{1,0:T(8,128)(2,1)}, f32[48,6528]{1,0:T(8,128)}, f32[145,128]{1,0:T(8,128)}, f32[8,128]{1,0:T(8,128)}) custom-call(bf16[48,6528]{1,0:T(8,128)(2,1)} %x_hbm.1, bf16[48,6528]{1,0:T(8,128)(2,1)} %dy_hbm.1, f32[145,128]{1,0:T(8,128)} %bitcast.9), custom_call_target="tpu_custom_call" | custom-call | tf_op jit(solution)/shard_map/step/pallas_call | solution.py:876
  53.7 2.8 %finish.1 = (bf16[48,6528]{1,0:T(8,128)(2,1)}, f32[48,6528]{1,0:T(8,128)}, f32[1,1]{1,0:T(1,128)}, f32[145,128]{1,0:T(8,128)}, f32[145,128]{1,0:T(8,128)}, /*ind...) custom-call(bf16[48,6528]{1,0:T(8,128)(2,1)} %get-tuple-element.20.refs_0_, ...), custom_call_target="tpu_custom_call" | custom-call | tf_op jit(solution)/shard_map/finish/pallas_call | solution.py:953

commit v12 on v11

--- a/solution.py
+++ b/solution.py
@@ -25,7 +25,7 @@
 BF16 = jnp.bfloat16
 MATS = ((0, D), (288, D), (576, D), (864, D), (1920, FF))
 W1_AT = 1152
-WIDTH1, WIDTH2, WIDTH3, DW_STEPS = 4, 6, 4, 2
+WIDTH1, WIDTH2, WIDTH3, DW_STEPS = 8, 6, 3, 2
 LOCK1, LOCK2 = 8, 4
 PIECES = 1
 VEC_AT = 2304

time: 56.7 us -> 56.3 us (level)
  no operation moved by 1% of the time
where the time goes in v12:
time: 56.3 us; the launch traced here: 56.1 us
  Pallas kernels  55.5 us (99%)
  between operations  0.64 us (1%)
    pallas_call x1, Pallas kernels, step(): pl.pallas_call(functools.partial(step_kernel, wide), out_shape=(jax.Shape...  52.7 us
    pallas_call x1, Pallas kernels, finish(): pl.pallas_call(finish_kernel, out_shape=(like(block_out.shape, BF16), lik...  2.81 us

profile of v12, /device:TPU:0, one launch (start us, length us, event | category | flops | bytes accessed | tf_op | source)
XLA Modules:
  0.0 56.1 jit_solution(422529004641980855)
XLA Ops:
  0.6 52.7 %step.1 = (bf16[48,6528]{1,0:T(8,128)(2,1)}, f32[48,6528]{1,0:T(8,128)}, f32[145,128]{1,0:T(8,128)}, f32[8,128]{1,0:T(8,128)}) custom-call(bf16[48,6528]{1,0:T(8,128)(2,1)} %x_hbm.1, bf16[48,6528]{1,0:T(8,128)(2,1)} %dy_hbm.1, f32[145,128]{1,0:T(8,128)} %bitcast.9), custom_call_target="tpu_custom_call" | custom-call | tf_op jit(solution)/shard_map/step/pallas_call | solution.py:876
  53.3 2.8 %finish.1 = (bf16[48,6528]{1,0:T(8,128)(2,1)}, f32[48,6528]{1,0:T(8,128)}, f32[1,1]{1,0:T(1,128)}, f32[145,128]{1,0:T(8,128)}, f32[145,128]{1,0:T(8,128)}, /*ind...) custom-call(bf16[48,6528]{1,0:T(8,128)(2,1)} %get-tuple-element.20.refs_0_, ...), custom_call_target="tpu_custom_call" | custom-call | tf_op jit(solution)/shard_map/finish/pallas_call | solution.py:953

commit v13 on v12

--- a/solution.py
+++ b/solution.py
@@ -26,7 +26,7 @@
 MATS = ((0, D), (288, D), (576, D), (864, D), (1920, FF))
 W1_AT = 1152
 WIDTH1, WIDTH2, WIDTH3, DW_STEPS = 8, 6, 3, 2
-LOCK1, LOCK2 = 8, 4
+LOCK1, LOCK2, LOCK3 = 8, 8, 4
 PIECES = 1
 VEC_AT = 2304
 USED_ROWS = VEC_AT + 16
@@ -382,9 +382,9 @@
             b = b - part
         return out.astype(BF16)
 
-    half_groups = LOCK2 * GROWS
-
-    @pl.loop(0, groups // LOCK2)
+    half_groups = LOCK3 * GROWS
+
+    @pl.loop(0, groups // LOCK3)
     def _(i):
         at = pl.ds(pl.multiple_of(i * half_groups, 16), half_groups)
         hs[at, :] = get_rows(os_, pl.multiple_of(i * half_groups, 8), half_groups).astype(BF16)
@@ -664,10 +664,10 @@
         def _():
             sum_cores(0)
 
-        r0 = pl.multiple_of(i * (LOCK2 * GROWS), 8)
-        p0 = pl.multiple_of(i * (LOCK2 * HJ), 32)
+        r0 = pl.multiple_of(i * (LOCK3 * GROWS), 8)
+        p0 = pl.multiple_of(i * (LOCK3 * HJ), 32)
         out = []
-        for k in range(LOCK2):
+        for k in range(LOCK3):
             dg = by_parity(get_rows(os_, r0 + GROWS * k, LANES).astype(BF16))
             out.append(own_lanes(nn(by_sample(probs(p0 + HJ * k)), dg)))
         out = jnp.concatenate(out, 0).astype(BF16)
@@ -675,7 +675,7 @@
         put_rows(vs, r0, out.astype(F32))
         return carry
 
-    lax.fori_loop(0, groups // LOCK2, attn_back_v, 0)
+    lax.fori_loop(0, groups // LOCK3, attn_back_v, 0)
 
     over_tokens((acc, hs, dqkv.at[:, 512:768]))
     store_square(acc[...], gflat, 576, D, tmp)
@@ -704,7 +704,7 @@
             for k in sets
             for b in range(GROUP)
         ]
-        at = pl.ds(pl.multiple_of(i * half_groups, 16), half_groups)
+        at = pl.ds(pl.multiple_of(i * (LOCK2 * GROWS), 16), LOCK2 * GROWS)
         for col, ref, val in ((0, qs, dq), (256, ks, dk)):
             val = jnp.concatenate(val, 0).astype(BF16)
             dqkv[at, col : col + 256] = val
@@ -736,6 +736,9 @@
         @pl.when(i == 1)
         def _():
             sum_cores(2)
+
+        @pl.when(i == 2)
+        def _():
             sum_plane(1)
 
     dg1, dn1 = over_token_chunks(dense3, WIDTH3, (zero, zero), hook3)
@@ -839,7 +842,7 @@
     half = padded // 2
     vecs = (USED_ROWS - 1) // rows - VEC_AT // rows + 1
     vm, dma = pltpu.VMEM, pltpu.SemaphoreType.DMA
-    sm = vm((2, n * ROWS + 8, LANES), F32)
+    sm = vm((2, (n + 1) * ROWS, LANES), F32)
     tok = vm((toks, 256), BF16)
     tile = (8, LANES)
     scratch = (
@@ -854,7 +857,7 @@
         + [tok, tok, tok, vm((toks, 2 * FF), BF16), tok]
         + [tok, tok, vm((n * ROWS, 3 * 256), BF16)]
         + [vm((256, 256), BF16)] * 4
-        + [vm((256, 2 * FF), BF16), vm((FF, 256), BF16), vm((2, FF, 128), F32)]
+        + [vm((256, 2 * FF), BF16), vm((FF, 256), BF16), vm((2, FF + 8, 128), F32)]
         + [vm((HJ, 256), BF16), vm((32, 256), BF16), vm((16 * GROUP, 256), BF16), vm((n * ROWS, 256), BF16)]
         + [vm((256, 256), F32), vm((256, 512), F32), vm((256, 256), F32)]
         + [vm((wide, padded, LANES), F32), vm((outer, inner, padded, LANES), F32)]

time: 56.3 us -> 56 us (level)
  no operation moved by 1% of the time
where the time goes in v13:
time: 56 us; the launch traced here: 55.8 us
  Pallas kernels  55.2 us (99%)
  between operations  0.64 us (1%)
    pallas_call x1, Pallas kernels, step(): pl.pallas_call(functools.partial(step_kernel, wide), out_shape=(jax.Shape...  52.4 us
    pallas_call x1, Pallas kernels, finish(): pl.pallas_call(finish_kernel, out_shape=(like(block_out.shape, BF16), lik...  2.81 us

profile of v13, /device:TPU:0, one launch (start us, length us, event | category | flops | bytes accessed | tf_op | source)
XLA Modules:
  0.0 55.8 jit_solution(12964073743181139717)
XLA Ops:
  0.6 52.4 %step.1 = (bf16[48,6528]{1,0:T(8,128)(2,1)}, f32[48,6528]{1,0:T(8,128)}, f32[145,128]{1,0:T(8,128)}, f32[8,128]{1,0:T(8,128)}) custom-call(bf16[48,6528]{1,0:T(8,128)(2,1)} %x_hbm.1, bf16[48,6528]{1,0:T(8,128)(2,1)} %dy_hbm.1, f32[145,128]{1,0:T(8,128)} %bitcast.9), custom_call_target="tpu_custom_call" | custom-call | tf_op jit(solution)/shard_map/step/pallas_call | solution.py:879
  53.0 2.8 %finish.1 = (bf16[48,6528]{1,0:T(8,128)(2,1)}, f32[48,6528]{1,0:T(8,128)}, f32[1,1]{1,0:T(1,128)}, f32[145,128]{1,0:T(8,128)}, f32[145,128]{1,0:T(8,128)}, /*ind...) custom-call(bf16[48,6528]{1,0:T(8,128)(2,1)} %get-tuple-element.20.refs_0_, ...), custom_call_target="tpu_custom_call" | custom-call | tf_op jit(solution)/shard_map/finish/pallas_call | solution.py:956
